TPU v7x, 256 devices: a whole 4x4x8 slice. The times are simulated.
256 devices in a mesh: sub: 16 (over z, core), sep: 16 (over x, y).
Axes of the slice: x: 4, y: 4, z: 8, core: 2. Of those that a mesh axis runs over, the one named last changes fastest.
Arguments:
- modes: bfloat16 [16, 32768, 1024], P('sub', 'sep'), may hold values from -0.1875 to 0.1875
- coupling: bfloat16 [16, 32768, 512], P('sub', 'sep'), may hold values from -0.046875 to 0.046875
- eigvals: float32 [16, 1024], P('sub'), may hold values from 0.5 to 8
- mode_count: int32 [16], P('sub'), may hold values from 256 to 1024
- sep_map: int32 [16, 4], P('sub'), may hold values from 0 to 31, as said below
- sep_len: int32 [16, 4], P('sub'), may hold values from 64 to 128
- flex: float32 [4096, 4096], P('sep')
- init_vectors: float32 [4096, 256], P('sep'), may hold values from -6 to 6
Outputs:
- separator_modes: float32 [4096, 256], P('sep')
- quotient: float32 [256], replicated
- interior: bfloat16 [16, 32768, 256], P('sub', 'sep')
Inputs may be any that keep to these rules, and one draw needn't show every extreme that they name: `sep_map`: each row names 4 different separator blocks.
All inputs are finite; a program needn't handle non-finite values.
Results may differ from a plain program's by a relative error of at most 0.013.
Values may be sent and summed in bfloat16 or wider, within the bound.
No kernel may reach another device: no remote copies, remote signals or barrier semaphores. Data moves between devices by JAX's collectives and lax.ppermute only.
A program may use at most 128 MiB of HBM per device.

v0:
```python
import jax
import jax.numpy as jnp
from jax import lax
from jax.experimental import pallas as pl
from jax.experimental.pallas import tpu as pltpu
from jax.sharding import PartitionSpec as P

KB = 4
SB = 128
HIGHEST = lax.Precision.HIGHEST


def dot_f32(a, b, contract=((1,), (0,))):
    return lax.dot_general(
        a, b, (contract, ((), ())), precision=HIGHEST, preferred_element_type=jnp.float32
    )


def split_three(x):
    high = x.astype(jnp.bfloat16)
    rest = x - high.astype(jnp.float32)
    middle = rest.astype(jnp.bfloat16)
    return high, middle, (rest - middle.astype(jnp.float32)).astype(jnp.bfloat16)


def invert_factor(left_ref, right_ref):
    n = left_ref.shape[0]
    subs = lax.broadcasted_iota(jnp.int32, (8, n), 0)
    lanes = lax.broadcasted_iota(jnp.int32, (8, n), 1)

    def spread(x, row, lane):
        return jnp.broadcast_to(x[row : row + 1, lane : lane + 1], (8, n))

    def row_of(x, row):
        return jnp.broadcast_to(x[row : row + 1, :], (8, n))

    def stacked(pieces, base):
        out = base
        for row, piece in pieces:
            out = jnp.where(subs == row, piece, out)
        return out

    def panel(t, carry):
        start = pl.multiple_of(8 * t, 8)
        shift = (n - 8 * t) & (n - 1)
        pivots = left_ref[pl.ds(start, 8), :]
        pivots_right = right_ref[pl.ds(start, 8), :]
        corner = pltpu.roll(pivots, shift, 1)
        a = {(i, j): spread(corner, i, j) for i in range(8) for j in range(i + 1)}
        inverse, m = [], {}
        for j in range(8):
            inverse.append(1.0 / a[j, j])
            for i in range(j + 1, 8):
                m[i, j] = a[i, j] * inverse[j]
            for i in range(j + 1, 8):
                for k in range(j + 1, i + 1):
                    a[i, k] = a[i, k] - m[i, j] * a[k, j]
        unit = {}
        for i in range(8):
            for k in range(i):
                total = -m[i, k]
                for j in range(k + 1, i):
                    total = total - m[i, j] * unit[j, k]
                unit[i, k] = total
        zero = jnp.zeros((8, n), jnp.float32)
        down = [stacked([(i, unit[i, k]) for i in range(k + 1, 8)], zero) for k in range(7)]
        up = [stacked([(k, unit[i, k]) for k in range(i)], zero) for i in range(1, 8)]
        scale = stacked([(i, inverse[i]) for i in range(1, 8)], inverse[0])
        root = stacked([(i, a[i, i]) for i in range(1, 8)], a[0, 0])

        def reduce_rows(x):
            for_out = x
            for k in range(7):
                for_out = for_out + down[k] * row_of(x, k)
            scaled = for_out * scale
            back = scaled
            for i in range(1, 8):
                back = back + up[i - 1] * row_of(scaled, i)
            return for_out, back

        _, back_left = reduce_rows(pivots)
        done_right, back_right = reduce_rows(pivots_right)
        heads = jnp.where(lanes > 8 * t + 7, pivots, 0.0)
        upper = split_three(heads)
        lower = split_three(jnp.concatenate([back_left, back_right], axis=1))
        pairs = ((0, 0), (0, 1), (1, 0), (0, 2), (2, 0), (1, 1))
        change = lax.dot_general(
            jnp.concatenate([upper[p] for p, _ in pairs], axis=0),
            jnp.concatenate([lower[q] for _, q in pairs], axis=0),
            (((0,), (0,)), ((), ())),
            preferred_element_type=jnp.float32,
        )
        left_ref[...] = left_ref[...] - change[:, :n]
        right_ref[...] = right_ref[...] - change[:, n:]
        right_ref[pl.ds(start, 8), :] = done_right * lax.rsqrt(root)
        return carry

    lax.fori_loop(0, n // 8, panel, 0)


def factor_kernel(scale, gram_ref, out_ref, left_ref, right_ref):
    half = gram_ref.shape[0] // 2
    identity = jnp.where(
        lax.broadcasted_iota(jnp.int32, (half, half), 0)
        == lax.broadcasted_iota(jnp.int32, (half, half), 1),
        1.0,
        0.0,
    ).astype(jnp.float32)
    left_ref[...] = gram_ref[:half, :half]
    right_ref[...] = identity
    invert_factor(left_ref, right_ref)
    first = right_ref[...]
    below = dot_f32(gram_ref[half:, :half], first, ((1,), (1,)))
    left_ref[...] = gram_ref[half:, half:] - dot_f32(below, below, ((1,), (1,)))
    right_ref[...] = identity
    invert_factor(left_ref, right_ref)
    second = right_ref[...]
    corner = -dot_f32(second, dot_f32(below, first))
    out_ref[:half, :half] = first.T * scale
    out_ref[:half, half:] = corner.T * scale
    out_ref[half:, :half] = jnp.zeros((half, half), jnp.float32)
    out_ref[half:, half:] = second.T * scale


def inverse_transposed_factor(gram, scale, after):
    half = gram.shape[0] // 2
    return pl.pallas_call(
        lambda gram_ref, after_ref, *refs: factor_kernel(scale, gram_ref, *refs),
        out_shape=jax.ShapeDtypeStruct(gram.shape, jnp.float32),
        in_specs=[
            pl.BlockSpec(memory_space=pltpu.VMEM),
            pl.BlockSpec(memory_space=pl.ANY),
        ],
        out_specs=pl.BlockSpec(memory_space=pltpu.VMEM),
        scratch_shapes=[pltpu.VMEM((half, half), jnp.float32)] * 2,
        cost_estimate=pl.CostEstimate(
            flops=12_000_000_000, bytes_accessed=600_000, transcendentals=256
        ),
        name="factor",
    )(gram, after)


def gram_step(x, even_ref, odd_ref):
    high, middle, low = split_three(x)

    def product(a, b):
        return lax.dot_general(
            a, b, (((0,), (0,)), ((), ())), preferred_element_type=jnp.float32
        )

    even_ref[...] += product(high, high) + product(middle, middle)
    odd_ref[...] += product(high, middle) + product(high, low)


def gram_kernel(x_ref, after_ref, out_ref, even_ref, odd_ref):
    @pl.when(pl.program_id(0) == 0)
    def _():
        even_ref[...] = jnp.zeros_like(even_ref)
        odd_ref[...] = jnp.zeros_like(odd_ref)

    gram_step(x_ref[...], even_ref, odd_ref)

    @pl.when(pl.program_id(0) == pl.num_programs(0) - 1)
    def _():
        out_ref[...] = even_ref[...] + odd_ref[...] + odd_ref[...].T


def gram_of(x, after):
    rows, width = x.shape
    step = 256
    return pl.pallas_call(
        gram_kernel,
        grid=(rows // step,),
        out_shape=jax.ShapeDtypeStruct((width, width), jnp.float32),
        in_specs=[
            pl.BlockSpec((step, width), lambda i: (i, 0)),
            pl.BlockSpec(memory_space=pl.ANY),
        ],
        out_specs=pl.BlockSpec((width, width), lambda i: (0, 0)),
        scratch_shapes=[pltpu.VMEM((width, width), jnp.float32)] * 2,
        cost_estimate=pl.CostEstimate(
            flops=3_000_000_000, bytes_accessed=2_400_000, transcendentals=0
        ),
        name="gram",
    )(x, after)


def sums_kernel(raw_ref, iterate_ref, factor_ref, image_ref, out_ref, even_ref, odd_ref, rows_ref):
    @pl.when(pl.program_id(0) == 0)
    def _():
        even_ref[...] = jnp.zeros_like(even_ref)
        odd_ref[...] = jnp.zeros_like(odd_ref)
        rows_ref[...] = jnp.zeros_like(rows_ref)

    image = dot_f32(raw_ref[...], factor_ref[...])
    image_ref[...] = image
    gram_step(image, even_ref, odd_ref)
    iterate = iterate_ref[...]
    rows_ref[0:1, :] += jnp.sum(iterate * image, axis=0, keepdims=True)
    rows_ref[1:2, :] += jnp.sum(iterate * iterate, axis=0, keepdims=True)

    @pl.when(pl.program_id(0) == pl.num_programs(0) - 1)
    def _():
        width = even_ref.shape[0]
        out_ref[:width, :] = even_ref[...] + odd_ref[...] + odd_ref[...].T
        out_ref[width:, :] = rows_ref[...]


def image_and_sums(raw, iterate, factor):
    rows, width = raw.shape
    step = 256
    block = pl.BlockSpec((step, width), lambda i: (i, 0))
    return pl.pallas_call(
        sums_kernel,
        grid=(rows // step,),
        out_shape=(
            jax.ShapeDtypeStruct((rows, width), jnp.float32),
            jax.ShapeDtypeStruct((width + 8, width), jnp.float32),
        ),
        in_specs=[block, block, pl.BlockSpec((width, width), lambda i: (0, 0))],
        out_specs=(block, pl.BlockSpec((width + 8, width), lambda i: (0, 0))),
        scratch_shapes=[
            pltpu.VMEM((width, width), jnp.float32),
            pltpu.VMEM((width, width), jnp.float32),
            pltpu.VMEM((8, width), jnp.float32),
        ],
        cost_estimate=pl.CostEstimate(
            flops=4_000_000_000, bytes_accessed=7_000_000, transcendentals=0
        ),
        name="sums",
    )(raw, iterate, factor)


def final_kernel(place_ref, here_ref, mine_ref, twin_ref, factor_ref, own_ref, touched_ref):
    i = pl.program_id(0)
    image = jnp.where(here_ref[i] == 1, mine_ref[0], twin_ref[0])
    vectors = dot_f32(image, factor_ref[...])

    @pl.when(i < 2)
    def _():
        own_ref[...] = vectors

    @pl.when(i >= 2)
    def _():
        touched_ref[...] = vectors.astype(jnp.bfloat16)


def final_vectors(place, here, mine, twin, factor):
    width = factor.shape[0]
    block = pl.BlockSpec((1, SB, width), lambda i, place, here: (place[i], 0, 0))
    return pl.pallas_call(
        final_kernel,
        grid_spec=pltpu.PrefetchScalarGridSpec(
            num_scalar_prefetch=2,
            grid=(2 + KB,),
            in_specs=[block, block, pl.BlockSpec((width, width), lambda i, place, here: (0, 0))],
            out_specs=(
                pl.BlockSpec((SB, width), lambda i, place, here: (jnp.minimum(i, 1), 0)),
                pl.BlockSpec((SB, width), lambda i, place, here: (jnp.maximum(i - 2, 0), 0)),
            ),
        ),
        out_shape=(
            jax.ShapeDtypeStruct((2 * SB, width), jnp.float32),
            jax.ShapeDtypeStruct((KB * SB, width), jnp.bfloat16),
        ),
        cost_estimate=pl.CostEstimate(
            flops=600_000_000, bytes_accessed=3_000_000, transcendentals=0
        ),
        name="final",
    )(place, here, mine, twin, factor)


def gather_blocks(x, axis):
    count = lax.axis_size(axis)
    spread = jnp.broadcast_to(x[None], (count,) + x.shape)
    return lax.all_to_all(spread, axis, 0, 0, tiled=True)


def per_device(modes, coupling, eigvals, mode_count, sep_map, sep_len, flex, init_vectors):
    shapes = modes[0]
    sep_count = lax.axis_size("sep")
    sub_count = lax.axis_size("sub")
    sep_index = lax.axis_index("sep")
    sub_index = lax.axis_index("sub")
    layers = sub_count // 2
    layer, core = sub_index // 2, sub_index % 2
    mode_total = shapes.shape[1]
    mode_rows = mode_total // sep_count
    vec_width = init_vectors.shape[1]
    owned_rows = init_vectors.shape[0]
    total_rows = owned_rows * sep_count
    local_dofs = KB * SB
    slim = SB // layers
    scaling = float(total_rows) ** 0.5

    def from_twin(x):
        return lax.ppermute(x, "sub", [(i, i ^ 1) for i in range(sub_count)])

    start_rows = lax.dynamic_slice_in_dim(init_vectors, core * SB, SB, 0)
    start_half = lax.all_gather(start_rows.astype(jnp.bfloat16), "sep", axis=0, tiled=True)
    start_twin = from_twin(start_half)

    dof_ids = jnp.arange(SB, dtype=jnp.int32)
    live_dofs = (dof_ids[None, :] < sep_len[0][:, None]).reshape(1, local_dofs)
    masked = jnp.where(live_dofs, coupling[0], jnp.zeros_like(coupling[0]))
    partial = lax.dot_general(
        shapes, masked, (((0,), (0,)), ((), ())), preferred_element_type=jnp.float32
    )
    shares = lax.all_to_all(
        partial.astype(jnp.bfloat16).reshape(sep_count, mode_rows, local_dofs),
        "sep",
        0,
        0,
        tiled=True,
    )
    own_projected = jnp.sum(shares.astype(jnp.float32), axis=0).astype(jnp.bfloat16)
    projected = gather_blocks(own_projected, "sep").reshape(mode_total, local_dofs)
    mode_ids = jnp.arange(mode_total, dtype=jnp.int32)
    mode_weight = jnp.where(mode_ids < mode_count[0], 1.0 / eigvals[0], 0.0)

    blocks = sep_map[0]
    own_blocks = 2 * sep_index + jnp.arange(2, dtype=jnp.int32)
    picks = own_blocks[:, None] == blocks[None, :]
    by_block = projected.reshape(mode_total, KB, SB)
    picked_columns = jnp.sum(
        jnp.where(picks[None, :, :, None], by_block[:, None], jnp.zeros_like(by_block[:, None])), axis=2
    ).reshape(mode_total, 2 * SB)
    wide = projected.astype(jnp.float32)
    operator_rows = dot_f32(
        picked_columns.astype(jnp.float32), mode_weight[:, None] * wide, ((0,), (0,))
    )
    outgoing = operator_rows.reshape(2, layers, slim, local_dofs).transpose(1, 0, 2, 3)
    outgoing = outgoing.reshape(sub_count, slim, local_dofs)
    map_lanes = jnp.pad(blocks.astype(jnp.float32), (0, SB - KB))
    outgoing = jnp.concatenate(
        [outgoing, jnp.broadcast_to(map_lanes, (sub_count, slim, SB))], axis=2
    )
    incoming = lax.all_to_all(outgoing, "sub", 0, 0, tiled=True)
    map_all = incoming[:, 0, local_dofs : local_dofs + KB].astype(jnp.int32)
    incoming = incoming[:, :, :local_dofs]

    block_total = total_rows // SB
    row_start = core * SB + layer * slim
    flex_rows = lax.dynamic_slice_in_dim(flex, row_start, slim, 0)
    matches = (
        map_all.reshape(-1)[:, None] == jnp.arange(block_total, dtype=jnp.int32)[None, :]
    ).astype(jnp.float32)
    by_source = incoming.reshape(sub_count, slim, KB, SB).transpose(0, 2, 1, 3)
    placed = dot_f32(matches, by_source.reshape(sub_count * KB, slim * SB), ((0,), (0,)))
    operator = flex_rows + placed.reshape(block_total, slim, SB).transpose(1, 0, 2).reshape(
        slim, total_rows
    )
    halves = operator.reshape(slim, sep_count, 2, SB).transpose(2, 0, 1, 3).reshape(
        2, slim, total_rows // 2
    )
    own_half = lax.dynamic_index_in_dim(halves, core, 0, keepdims=False)
    twin_half = lax.dynamic_index_in_dim(halves, 1 - core, 0, keepdims=False)

    operator_half = jnp.concatenate([own_half, from_twin(twin_half)], axis=0)

    def spread_layers(rows):
        part = rows.reshape(1, 1, 1, slim, vec_width)
        for axis, distance in enumerate((4, 2, 1)):
            perm = [
                (z * 2 + c, (z ^ distance) * 2 + c) for z in range(layers) for c in range(2)
            ]
            other = lax.ppermute(part, "sub", perm)
            upper = (layer & distance) > 0
            part = jnp.where(
                upper,
                jnp.concatenate([other, part], axis=axis),
                jnp.concatenate([part, other], axis=axis),
            )
        return part.reshape(SB, vec_width)

    def gather_half(part):
        return gather_blocks(part, "sep").reshape(total_rows // 2, vec_width)

    first_rows = dot_f32(
        jnp.concatenate([own_half, twin_half], axis=1),
        jnp.concatenate([start_half, start_twin], axis=0).astype(jnp.float32),
    )
    first_half = gather_half(spread_layers(first_rows))
    both_rows = dot_f32(operator_half, first_half)
    second_rows = both_rows[:slim] + from_twin(both_rows[slim:])
    second_part = spread_layers(second_rows)
    raw_half = gather_half(second_part)

    first_gram = gram_of(first_half, second_part)
    first_gram = first_gram + from_twin(first_gram)
    first_factor = inverse_transposed_factor(first_gram, scaling, second_part)
    iterate_half = dot_f32(first_half, first_factor)

    image_half, second_sums = image_and_sums(raw_half, iterate_half, first_factor)
    second_sums = second_sums + from_twin(second_sums)
    second_factor = inverse_transposed_factor(second_sums[:vec_width], scaling, second_part)
    quotient = second_sums[vec_width] / second_sums[vec_width + 1]
    image_twin = from_twin(image_half)
    wanted = jnp.concatenate([own_blocks, blocks])
    separator_modes, touched = final_vectors(
        wanted // 2,
        (wanted % 2 == core).astype(jnp.int32),
        image_half.reshape(sep_count, SB, vec_width),
        image_twin.reshape(sep_count, SB, vec_width),
        second_factor,
    )
    amplitude = jnp.dot(
        projected, touched, preferred_element_type=jnp.float32
    )
    terms = (mode_weight[:, None] * amplitude).astype(jnp.bfloat16)
    interior = jnp.dot(shapes, terms, preferred_element_type=jnp.float32)
    return (separator_modes, quotient, interior.astype(jnp.bfloat16)[None])


def solution(mesh):
    placed = (
        P("sub", "sep", None),
        P("sub", "sep", None),
        P("sub", None),
        P("sub"),
        P("sub", None),
        P("sub", None),
        P("sep", None),
        P("sep", None),
    )
    return jax.shard_map(
        per_device,
        mesh=mesh,
        in_specs=placed,
        out_specs=(P("sep", None), P(), P("sub", "sep", None)),
        check_vma=False,
    )
```

profile of v0, /device:TPU:1, one launch (start us, length us, event | category | flops | bytes accessed | tf_op | source)
XLA Modules:
  0.0 257.4 jit_solution(18149318240361223872)
XLA Ops:
  7.2 0.8 fusion.52
  7.9 5.2 %fusion.22 = bf16[1024,512]{0,1:T(8,128)(2,1)S(1)} fusion(bf16[1,2048,1024]{2,1,0:T(8,128)(2,1)} %param.8, bf16[1,2048,512]{2,1,0:T(8,128)(2,1)} %param.9, pred[512]{0:T(512)(128)(4,1)S(1)} %fusion.52), kind=kOutput, calls=%fused_computation.16 | convolution fusion | flops 2149056512 | bytes 7340544 | tf_op jit(solution)/shard_map/dot_general | solution.py:306
  13.1 1.3 copy.44
  14.5 7.6 %all-to-all-start = ((bf16[16,64,512]{2,1,0:T(8,128)(2,1)}), bf16[16,64,512]{2,1,0:T(8,128)(2,1)S(1)}, u32[]{:S(2)}, u32[]{:S(2)}) async-start(bf16[16,64,512]{2,1,0:T(8,128)(2,1)} %bitcast.6), calls=%async_computation | async-start | bytes 2097152 | tf_op jit(solution)/shard_map/all_to_all | solution.py:309
  22.8 14.7 %all-to-all-done = bf16[16,64,512]{2,1,0:T(8,128)(2,1)S(1)} async-done(((bf16[16,64,512]{2,1,0:T(8,128)(2,1)}), bf16[16,64,512]{2,1,0:T(8,128)(2,1)S(1)}, u32[]{:S(2)}, u32[]{:S(2)}) %all-to-all-start) | async-done | bytes 1048608 | tf_op jit(solution)/shard_map/all_to_all | solution.py:309
  37.7 1.1 broadcast_in_dim.75
  38.8 4.0 %all-to-all-start.1 = ((bf16[16,64,512]{2,1,0:T(8,128)(2,1)}), bf16[16,64,512]{2,1,0:T(8,128)(2,1)S(1)}, u32[]{:S(2)}, u32[]{:S(2)}) async-start(bf16[16,64,512]{2,1,0:T(8,128)(2,1)} %broadcast_in_dim.75), calls=%async_computation.1 | async-start | bytes 2097152 | tf_op jit(solution)/shard_map/all_to_all | solution.py:276
  44.8 13.2 %all-to-all-done.1 = bf16[16,64,512]{2,1,0:T(8,128)(2,1)S(1)} async-done(((bf16[16,64,512]{2,1,0:T(8,128)(2,1)}), bf16[16,64,512]{2,1,0:T(8,128)(2,1)S(1)}, u32[]{:S(2)}, u32[]{:S(2)}) %all-to-all-start.1) | async-done | bytes 1048608 | tf_op jit(solution)/shard_map/all_to_all | solution.py:276
  59.3 1.2 convolution_bitcast_fusion
  60.5 0.9 pad_maximum_fusion
  61.4 12.0 %all-to-all-start.2 = ((f32[16,16,640]{2,1,0:T(8,128)}), f32[16,16,640]{2,1,0:T(8,128)S(1)}, u32[]{:S(2)}, u32[]{:S(2)}) async-start(f32[16,16,640]{2,1,0:T(8,128)} %pad_maximum_fusion), calls=%async_computation.2 | async-start | bytes 1310720 | tf_op jit(solution)/shard_map/all_to_all | solution.py:338
  73.4 8.7 %all-gather.2.cloned.1.call-done = bf16[2048,256]{1,0:T(8,128)(2,1)} async-done(((bf16[128,256]{1,0:T(8,128)(2,1)}), bf16[2048,256]{1,0:T(8,128)(2,1)}) %all-gather.2.cloned.1.call-update) | async-done | bytes 1048592 | tf_op jit(solution)/shard_map/all_gather | solution.py:300
  82.1 1.9 collective-permute-start.1
  84.0 9.4 %all-to-all-done.2 = f32[16,16,640]{2,1,0:T(8,128)S(1)} async-done(((f32[16,16,640]{2,1,0:T(8,128)}), f32[16,16,640]{2,1,0:T(8,128)S(1)}, u32[]{:S(2)}, u32[]{:S(2)}) %all-to-all-start.2) | async-done | bytes 655392 | tf_op jit(solution)/shard_map/all_to_all | solution.py:338
  94.1 1.1 bitcast_add_fusion
  95.6 2.2 fusion.10
  97.8 1.1 collective-permute-start.2
  98.9 5.6 %collective-permute-done.2 = f32[1,1,1,16,256]{4,3,2,1,0:T(8,128)S(1)} collective-permute-done((f32[1,1,1,16,256]{4,3,2,1,0:T(8,128)S(1)}, f32[1,1,1,16,256]{4,3,2,1,0:T(8,128)S(1)}, u32[]{:S(2)}, u32[]{:S(2)}) %collective-permute-start.2) | collective-permute-done | bytes 16416 | tf_op jit(solution)/shard_map/ppermute | solution.py:367
  104.6 4.3 %collective-permute-done.3 = f32[2,1,1,16,256]{4,3,2,1,0:T(8,128)S(1)} collective-permute-done((f32[2,1,1,16,256]{4,3,2,1,0:T(8,128)S(1)}, f32[2,1,1,16,256]{4,3,2,1,0:T(8,128)S(1)}, u32[]{:S(2)}, u32[]{:S(2)}) %collective-permute-start.3) | collective-permute-done | bytes 32800 | tf_op jit(solution)/shard_map/ppermute | solution.py:367
  109.0 3.1 %collective-permute-done.4 = f32[2,2,1,16,256]{4,3,0,2,1:T(8,128)S(1)} collective-permute-done((f32[2,2,1,16,256]{4,3,0,2,1:T(8,128)S(1)}, f32[2,2,1,16,256]{4,3,0,2,1:T(8,128)S(1)}, u32[]{:S(2)}, u32[]{:S(2)}) %collective-permute-start.4) | collective-permute-done | bytes 65568 | tf_op jit(solution)/shard_map/ppermute | solution.py:367
  112.2 1.5 broadcast_in_dim.81
  113.7 3.7 %all-to-all-start.3 = ((f32[16,128,256]{2,1,0:T(8,128)}), f32[16,128,256]{2,1,0:T(8,128)S(1)}, u32[]{:S(2)}, u32[]{:S(2)}) async-start(f32[16,128,256]{2,1,0:T(8,128)} %broadcast_in_dim.81), calls=%async_computation.3 | async-start | bytes 4194304 | tf_op jit(solution)/shard_map/all_to_all | solution.py:276
  117.4 1.6 collective-permute-start
  119.1 1.3 collective-permute-done
  120.4 22.7 %all-to-all-done.3 = f32[16,128,256]{2,1,0:T(8,128)S(1)} async-done(((f32[16,128,256]{2,1,0:T(8,128)}), f32[16,128,256]{2,1,0:T(8,128)S(1)}, u32[]{:S(2)}, u32[]{:S(2)}) %all-to-all-start.3) | async-done | bytes 2097184 | tf_op jit(solution)/shard_map/all_to_all | solution.py:276
  143.1 2.1 fusion.33
  145.2 5.3 %collective-permute-start.5 = (f32[16,256]{1,0:T(8,128)S(1)}, f32[16,256]{1,0:T(8,128)S(1)}, u32[]{:S(2)}, u32[]{:S(2)}) collective-permute-start(f32[16,256]{1,0:T(8,128)S(1)} %slice.31), channel_id=1, source_target_pairs={{0,16},{16,0},{32,48},{48,32},{64,80},{80,64},{96,112},{112,96},{1... | collective-permute-start | bytes 49160 | tf_op jit(solution)/shard_map/ppermute | solution.py:297
  150.5 0.8 collective-permute-done.5
  151.8 6.1 %collective-permute-done.6 = f32[1,1,1,16,256]{4,3,2,1,0:T(8,128)S(1)} collective-permute-done((f32[1,1,1,16,256]{4,3,2,1,0:T(8,128)S(1)}, f32[1,1,1,16,256]{4,3,2,1,0:T(8,128)S(1)}, u32[]{:S(2)}, u32[]{:S(2)}) %collective-permute-start.6) | collective-permute-done | bytes 16416 | tf_op jit(solution)/shard_map/ppermute | solution.py:367
  157.9 3.7 %collective-permute-done.7 = f32[2,1,1,16,256]{4,3,0,2,1:T(8,128)S(1)} collective-permute-done((f32[2,1,1,16,256]{4,3,0,2,1:T(8,128)S(1)}, f32[2,1,1,16,256]{4,3,0,2,1:T(8,128)S(1)}, u32[]{:S(2)}, u32[]{:S(2)}) %collective-permute-start.7) | collective-permute-done | bytes 32800 | tf_op jit(solution)/shard_map/ppermute | solution.py:367
  161.7 3.1 %collective-permute-done.8 = f32[2,2,1,16,256]{4,3,0,2,1:T(8,128)S(1)} collective-permute-done((f32[2,2,1,16,256]{4,3,0,2,1:T(8,128)S(1)}, f32[2,2,1,16,256]{4,3,0,2,1:T(8,128)S(1)}, u32[]{:S(2)}, u32[]{:S(2)}) %collective-permute-start.8) | collective-permute-done | bytes 65568 | tf_op jit(solution)/shard_map/ppermute | solution.py:367
  164.8 1.6 broadcast_in_dim.82
  166.4 4.4 %all-to-all-start.4 = ((f32[16,128,256]{2,1,0:T(8,128)}), f32[16,128,256]{2,1,0:T(8,128)}, u32[]{:S(2)}, u32[]{:S(2)}) async-start(f32[16,128,256]{2,1,0:T(8,128)} %broadcast_in_dim.82), calls=%async_computation.4 | async-start | bytes 4194304 | tf_op jit(solution)/shard_map/all_to_all | solution.py:276
  170.9 6.5 %gram.1 = f32[256,256]{1,0:T(8,128)} custom-call(f32[2048,256]{1,0:T(8,128)} %bitcast.125, f32[128,256]{1,0:T(8,128)} %bitcast.137), custom_call_target="tpu_custom_call" | custom-call | flops 3000000000 | bytes 2400000 | tf_op jit(solution)/shard_map/gram/pallas_call | solution.py:171
  177.4 4.0 %collective-permute-start.9 = (f32[256,256]{1,0:T(8,128)}, f32[256,256]{1,0:T(8,128)S(1)}, u32[]{:S(2)}, u32[]{:S(2)}) collective-permute-start(f32[256,256]{1,0:T(8,128)} %gram.1), channel_id=1, source_target_pairs={{0,16},{16,0},{32,48},{48,32},{64,80},{80,64},{96,112},{112,96},{1... | collective-permute-start | bytes 786440 | tf_op jit(solution)/shard_map/ppermute | solution.py:297
  181.3 1.4 collective-permute-done.9
  182.7 1.7 add.65.gram_ref
  184.4 16.0 %factor.2.factor_ref = f32[256,256]{1,0:T(8,128)} custom-call(f32[256,256]{1,0:T(8,128)} %add.65.gram_ref, f32[128,256]{1,0:T(8,128)} %bitcast.138), custom_call_target="tpu_custom_call" | custom-call | flops 12000000000 | bytes 600000 | tf_op jit(solution)/shard_map/factor/pallas_call | solution.py:127
  200.4 4.2 %fusion.58.iterate_ref = f32[2048,256]{1,0:T(8,128)} fusion(f32[2048,256]{1,0:T(8,128)S(1)} %bitcast.126, f32[256,256]{1,0:T(8,128)} %factor.2.factor_ref), kind=kOutput, calls=%fused_computation.87 | convolution fusion | flops 1610612736 | bytes 4456448 | tf_op jit(solution)/shard_map/dot_general | solution.py:14
  204.5 10.3 %sums.1 = (f32[2048,256]{1,0:T(8,128)}, f32[264,256]{1,0:T(8,128)}) custom-call(f32[2048,256]{1,0:T(8,128)} %bitcast.38.raw_ref, f32[2048,256]{1,0:T(8,128)} %fusion.58.iterate_ref, f32[256,256]{1,0:T(8,128)} %factor.2.factor_ref), custom_call_target="tpu_custom_call" | custom-call | flops 4000000000 | bytes 7000000 | tf_op jit(solution)/shard_map/sums/pallas_call | solution.py:213
  216.6 3.0 %collective-permute-done.11 = f32[264,256]{1,0:T(8,128)S(1)} collective-permute-done((f32[264,256]{1,0:T(8,128)}, f32[264,256]{1,0:T(8,128)S(1)}, u32[]{:S(2)}, u32[]{:S(2)}) %collective-permute-start.11) | collective-permute-done | bytes 270368 | tf_op jit(solution)/shard_map/ppermute | solution.py:297
  219.6 1.0 add.66
  220.6 0.7 slice.32.gram_ref
  221.9 15.8 %factor.3.factor_ref = f32[256,256]{1,0:T(8,128)} custom-call(f32[256,256]{1,0:T(8,128)} %slice.32.gram_ref, f32[128,256]{1,0:T(8,128)} %bitcast.139), custom_call_target="tpu_custom_call" | custom-call | flops 12000000000 | bytes 600000 | tf_op jit(solution)/shard_map/factor/pallas_call | solution.py:127
  237.7 1.3 copy-done.3
  239.0 6.0 %final.1 = (f32[256,256]{1,0:T(8,128)}, bf16[512,256]{1,0:T(8,128)(2,1)}) custom-call(s32[6]{0:T(128)} %and_select_fusion.1.place_ref, s32[6]{0:T(128)} %get-tuple-element.25.here_ref, f32[16,128,256]{2,1,0:T(8,128)} %bitcast.129, f32[16,128,256]{2,1,0:T(8,128)} %bitcast.130, f32[256,256]{1,0:T(8,128)} %factor.3.factor_ref), custom_call_target="tpu_custom_call" | custom-call | flops 600000000 | bytes 3000000 | tf_op jit(solution)/shard_map/final/pallas_call | solution.py:251
  245.0 4.3 %fusion.7 = bf16[1,2048,256]{1,2,0:T(8,128)(2,1)S(1)} fusion(bf16[1,2048,1024]{2,1,0:T(8,128)(2,1)} %param.8, bf16[1024,512]{1,0:T(8,128)(2,1)S(1)} %bitcast.127, bf16[512,256]{1,0:T(8,128)(2,1)} %get-tuple-element.10, f32[1024]{0:T(1024)S(1)} %fusion.51), kind=kOutput, calls=%fused_computation.5 | convolution fusion | flops 1343225856 | bytes 6557696 | tf_op jit(solution)/shard_map/dot_general | solution.py:411
  249.3 1.3 copy.58
  (69 shorter events, 7.6 us)
Async XLA Ops:
  7.2 15.0 %copy-start = (f32[256,256]{1,0:T(8,128)S(1)}, f32[256,256]{1,0:T(8,128)}, u32[]{:S(2)}) copy-start(f32[256,256]{1,0:T(8,128)} %param.15) | copy-start | bytes 786436
  14.5 23.1 %all-to-all-start = ((bf16[16,64,512]{2,1,0:T(8,128)(2,1)}), bf16[16,64,512]{2,1,0:T(8,128)(2,1)S(1)}, u32[]{:S(2)}, u32[]{:S(2)}) async-start(bf16[16,64,512]{2,1,0:T(8,128)(2,1)} %bitcast.6), calls=%async_computation | async-start | bytes 2097152 | tf_op jit(solution)/shard_map/all_to_all | solution.py:309
  22.0 60.0 %all-gather.2.cloned.1.call-start = ((), (), s32[]{:S(2)}) async-start(), calls=%async_computation.5 | async-start | bytes 1114112 | tf_op jit(solution)/shard_map/all_gather | solution.py:300
  22.8 20.5 %copy-start.6 = (f32[1,1024]{1,0:T(1,128)S(1)}, f32[1,1024]{1,0:T(1,128)}, u32[]{:S(2)}) copy-start(f32[1,1024]{1,0:T(1,128)} %param.10) | copy-start | bytes 12292
  22.8 21.9 %copy-start.7 = (s32[1,4]{1,0:T(1,128)S(1)}, s32[1,4]{1,0:T(1,128)}, u32[]{:S(2)}) copy-start(s32[1,4]{1,0:T(1,128)} %param.12) | copy-start | bytes 52
  38.8 19.2 %all-to-all-start.1 = ((bf16[16,64,512]{2,1,0:T(8,128)(2,1)}), bf16[16,64,512]{2,1,0:T(8,128)(2,1)S(1)}, u32[]{:S(2)}, u32[]{:S(2)}) async-start(bf16[16,64,512]{2,1,0:T(8,128)(2,1)} %broadcast_in_dim.75), calls=%async_computation.1 | async-start | bytes 2097152 | tf_op jit(solution)/shard_map/all_to_all | solution.py:276
  61.4 32.0 %all-to-all-start.2 = ((f32[16,16,640]{2,1,0:T(8,128)}), f32[16,16,640]{2,1,0:T(8,128)S(1)}, u32[]{:S(2)}, u32[]{:S(2)}) async-start(f32[16,16,640]{2,1,0:T(8,128)} %pad_maximum_fusion), calls=%async_computation.2 | async-start | bytes 1310720 | tf_op jit(solution)/shard_map/all_to_all | solution.py:338
  82.1 13.5 %collective-permute-start.1 = (bf16[2048,256]{1,0:T(8,128)(2,1)}, bf16[2048,256]{1,0:T(8,128)(2,1)}, u32[]{:S(2)}, u32[]{:S(2)}) collective-permute-start(bf16[2048,256]{1,0:T(8,128)(2,1)} %all-gather.2.cloned.1.call-done), channel_id=1, source_target_pairs={{0,16},{16,0},{32,48},{48,32},{64,80},{80,64},{96,112},{112,96},{1... | collective-permute-start | bytes 3145736 | tf_op jit(solution)/shard_map/ppermute | solution.py:297
  93.6 2.0 copy-start.8
  95.6 13.3 %copy-start.5 = (f32[16,2048]{1,0:T(8,128)}, f32[16,2048]{1,0:T(8,128)S(1)}, u32[]{:S(2)}) copy-start(f32[16,2048]{1,0:T(8,128)S(1)} %get-tuple-element.28) | copy-start | bytes 393220
  97.8 6.7 %collective-permute-start.2 = (f32[1,1,1,16,256]{4,3,2,1,0:T(8,128)S(1)}, f32[1,1,1,16,256]{4,3,2,1,0:T(8,128)S(1)}, u32[]{:S(2)}, u32[]{:S(2)}) collective-permute-start(f32[1,1,1,16,256]{4,3,2,1,0:T(8,128)S(1)} %bitcast.142), channel_id=1, source_target_pairs={{0,128},{16,144},{32,160},{48,176},{64,192},{80,208},{96,224},{112... | collective-permute-start | bytes 49160 | tf_op jit(solution)/shard_map/ppermute | solution.py:367
  104.6 4.3 %collective-permute-start.3 = (f32[2,1,1,16,256]{4,3,2,1,0:T(8,128)S(1)}, f32[2,1,1,16,256]{4,3,2,1,0:T(8,128)S(1)}, u32[]{:S(2)}, u32[]{:S(2)}) collective-permute-start(f32[2,1,1,16,256]{4,3,2,1,0:T(8,128)S(1)} %maximum_select_fusion.4), channel_id=1, source_target_pairs={{0,64},{16,80},{32,96},{48,112},{64,0},{80,16},{96,32},{112,48},{1... | collective-permute-start | bytes 98312 | tf_op jit(solution)/shard_map/ppermute | solution.py:367
  108.9 3.2 %collective-permute-start.4 = (f32[2,2,1,16,256]{4,3,0,2,1:T(8,128)S(1)}, f32[2,2,1,16,256]{4,3,0,2,1:T(8,128)S(1)}, u32[]{:S(2)}, u32[]{:S(2)}) collective-permute-start(f32[2,2,1,16,256]{4,3,0,2,1:T(8,128)S(1)} %maximum_select_fusion.2), channel_id=1, source_target_pairs={{0,32},{16,48},{32,0},{48,16},{64,96},{80,112},{96,64},{112,80},{1... | collective-permute-start | bytes 196616 | tf_op jit(solution)/shard_map/ppermute | solution.py:367
  113.7 29.4 %all-to-all-start.3 = ((f32[16,128,256]{2,1,0:T(8,128)}), f32[16,128,256]{2,1,0:T(8,128)S(1)}, u32[]{:S(2)}, u32[]{:S(2)}) async-start(f32[16,128,256]{2,1,0:T(8,128)} %broadcast_in_dim.81), calls=%async_computation.3 | async-start | bytes 4194304 | tf_op jit(solution)/shard_map/all_to_all | solution.py:276
  117.4 3.0 %collective-permute-start = (f32[16,2048]{1,0:T(8,128)}, f32[16,2048]{1,0:T(8,128)}, u32[]{:S(2)}, u32[]{:S(2)}) collective-permute-start(f32[16,2048]{1,0:T(8,128)} %copy-done.5), channel_id=1, source_target_pairs={{0,16},{16,0},{32,48},{48,32},{64,80},{80,64},{96,112},{112,96},{1... | collective-permute-start | bytes 393224 | tf_op jit(solution)/shard_map/ppermute | solution.py:297
  143.1 23.4 %copy-start.1 = (f32[16,128,256]{2,1,0:T(8,128)}, f32[16,128,256]{2,1,0:T(8,128)S(1)}, u32[]{:S(2)}) copy-start(f32[16,128,256]{2,1,0:T(8,128)S(1)} %all-to-all-done.3) | copy-start | bytes 6291460
  145.2 6.2 %collective-permute-start.5 = (f32[16,256]{1,0:T(8,128)S(1)}, f32[16,256]{1,0:T(8,128)S(1)}, u32[]{:S(2)}, u32[]{:S(2)}) collective-permute-start(f32[16,256]{1,0:T(8,128)S(1)} %slice.31), channel_id=1, source_target_pairs={{0,16},{16,0},{32,48},{48,32},{64,80},{80,64},{96,112},{112,96},{1... | collective-permute-start | bytes 49160 | tf_op jit(solution)/shard_map/ppermute | solution.py:297
  151.4 6.5 %collective-permute-start.6 = (f32[1,1,1,16,256]{4,3,2,1,0:T(8,128)S(1)}, f32[1,1,1,16,256]{4,3,2,1,0:T(8,128)S(1)}, u32[]{:S(2)}, u32[]{:S(2)}) collective-permute-start(f32[1,1,1,16,256]{4,3,2,1,0:T(8,128)S(1)} %get-tuple-element.29), channel_id=1, source_target_pairs={{0,128},{16,144},{32,160},{48,176},{64,192},{80,208},{96,224},{112... | collective-permute-start | bytes 49160 | tf_op jit(solution)/shard_map/ppermute | solution.py:367
  157.9 3.7 %collective-permute-start.7 = (f32[2,1,1,16,256]{4,3,0,2,1:T(8,128)S(1)}, f32[2,1,1,16,256]{4,3,0,2,1:T(8,128)S(1)}, u32[]{:S(2)}, u32[]{:S(2)}) collective-permute-start(f32[2,1,1,16,256]{4,3,0,2,1:T(8,128)S(1)} %fusion.40), channel_id=1, source_target_pairs={{0,64},{16,80},{32,96},{48,112},{64,0},{80,16},{96,32},{112,48},{1... | collective-permute-start | bytes 98312 | tf_op jit(solution)/shard_map/ppermute | solution.py:367
  161.6 3.2 %collective-permute-start.8 = (f32[2,2,1,16,256]{4,3,0,2,1:T(8,128)S(1)}, f32[2,2,1,16,256]{4,3,0,2,1:T(8,128)S(1)}, u32[]{:S(2)}, u32[]{:S(2)}) collective-permute-start(f32[2,2,1,16,256]{4,3,0,2,1:T(8,128)S(1)} %maximum_select_fusion.3), channel_id=1, source_target_pairs={{0,32},{16,48},{32,0},{48,16},{64,96},{80,112},{96,64},{112,80},{1... | collective-permute-start | bytes 196616 | tf_op jit(solution)/shard_map/ppermute | solution.py:367
  164.8 1.6 copy-start.4
  166.4 38.1 %all-to-all-start.4 = ((f32[16,128,256]{2,1,0:T(8,128)}), f32[16,128,256]{2,1,0:T(8,128)}, u32[]{:S(2)}, u32[]{:S(2)}) async-start(f32[16,128,256]{2,1,0:T(8,128)} %broadcast_in_dim.82), calls=%async_computation.4 | async-start | bytes 4194304 | tf_op jit(solution)/shard_map/all_to_all | solution.py:276
  177.4 5.3 %collective-permute-start.9 = (f32[256,256]{1,0:T(8,128)}, f32[256,256]{1,0:T(8,128)S(1)}, u32[]{:S(2)}, u32[]{:S(2)}) collective-permute-start(f32[256,256]{1,0:T(8,128)} %gram.1), channel_id=1, source_target_pairs={{0,16},{16,0},{32,48},{48,32},{64,80},{80,64},{96,112},{112,96},{1... | collective-permute-start | bytes 786440 | tf_op jit(solution)/shard_map/ppermute | solution.py:297
  184.4 16.0 %copy-start.2 = (f32[16,128,256]{2,1,0:T(8,128)S(1)}, f32[16,128,256]{2,1,0:T(8,128)}, u32[]{:S(2)}) copy-start(f32[16,128,256]{2,1,0:T(8,128)} %copy-done.1) | copy-start | bytes 6291460
  214.8 22.9 %collective-permute-start.10 = (f32[2048,256]{1,0:T(8,128)}, f32[2048,256]{1,0:T(8,128)S(1)}, u32[]{:S(2)}, u32[]{:S(2)}) collective-permute-start(f32[2048,256]{1,0:T(8,128)} %get-tuple-element.7), channel_id=1, source_target_pairs={{0,16},{16,0},{32,48},{48,32},{64,80},{80,64},{96,112},{112,96},{1... | collective-permute-start | bytes 6291464 | tf_op jit(solution)/shard_map/ppermute | solution.py:297
  215.8 3.8 %collective-permute-start.11 = (f32[264,256]{1,0:T(8,128)}, f32[264,256]{1,0:T(8,128)S(1)}, u32[]{:S(2)}, u32[]{:S(2)}) collective-permute-start(f32[264,256]{1,0:T(8,128)} %get-tuple-element.8), channel_id=1, source_target_pairs={{0,16},{16,0},{32,48},{48,32},{64,80},{80,64},{96,112},{112,96},{1... | collective-permute-start | bytes 811016 | tf_op jit(solution)/shard_map/ppermute | solution.py:297
  237.7 1.3 copy-start.3
Sparse Core Ops, SparseCore 0:
  25.9 56.1 all-gather.1
where the time goes:
time: 259 us; the launch traced here: 257 us
  waiting for transfers between devices  101 us (39%)
  Pallas kernels  54.6 us (21%)
  starting transfers between devices  46.8 us (18%)
  matrix products  19.6 us (8%)
  between operations  15.1 us (6%)
  local copies, waits for them, and re-layouts  11.3 us (4%)
  other arithmetic  9.03 us (3%)
    all_to_all x3, waiting for transfers between devices, gather_blocks(): return lax.all_to_all(spread, axis, 0, 0, tiled=True)  35.9 us
    pallas_call x2, Pallas kernels, inverse_transposed_factor(): pl.pallas_call(lambda gram_ref, after_ref, *refs: factor_kernel(scale, gr...  31.8 us
    ppermute x6, waiting for transfers between devices, spread_layers(): other = lax.ppermute(part, 'sub', perm)  25.9 us
    all_to_all x1, waiting for transfers between devices, per_device(): lax.all_to_all(partial.astype(jnp.bfloat16).reshape(sep_count, mode_rows,...  14.7 us
    ppermute x6, starting transfers between devices, from_twin(): return lax.ppermute(x, 'sub', [(i, i ^ 1) for i in range(sub_count)])  13.3 us
    all_to_all x3, starting transfers between devices, gather_blocks(): return lax.all_to_all(spread, axis, 0, 0, tiled=True)  12.1 us
    all_to_all x1, starting transfers between devices, per_device(): incoming = lax.all_to_all(outgoing, 'sub', 0, 0, tiled=True)  12 us
    pallas_call x1, Pallas kernels, image_and_sums(): pl.pallas_call(sums_kernel, grid=(rows // step,), out_shape=(jax.ShapeDty...  10.3 us
  transfers between devices with their start and end apart: 18, of which 15 were waited for; matrix products, arithmetic and copies ran while one was open for 7% of the time, Pallas kernels for 15%

commit v1 on v0

v1 whole, which is shorter than its diff:
```python
import jax
import jax.numpy as jnp
from jax import lax
from jax.experimental import pallas as pl
from jax.experimental.pallas import tpu as pltpu
from jax.sharding import PartitionSpec as P

KB = 4
SB = 128
CHUNK = 2048
VMEM_BYTES = 32 * 1024 * 1024
HIGHEST = lax.Precision.HIGHEST
WHOLE = pl.BlockSpec(memory_space=pltpu.VMEM)


def dot_f32(a, b, contract=((1,), (0,))):
    return lax.dot_general(
        a, b, (contract, ((), ())), precision=HIGHEST, preferred_element_type=jnp.float32
    )


def split_three(x):
    high = x.astype(jnp.bfloat16)
    rest = x - high.astype(jnp.float32)
    middle = rest.astype(jnp.bfloat16)
    return high, middle, (rest - middle.astype(jnp.float32)).astype(jnp.bfloat16)


def invert_factor(left_ref, right_ref):
    n = left_ref.shape[0]
    subs = lax.broadcasted_iota(jnp.int32, (8, n), 0)
    lanes = lax.broadcasted_iota(jnp.int32, (8, n), 1)

    def spread(x, row, lane):
        return jnp.broadcast_to(x[row : row + 1, lane : lane + 1], (8, n))

    def row_of(x, row):
        return jnp.broadcast_to(x[row : row + 1, :], (8, n))

    def stacked(pieces, base):
        out = base
        for row, piece in pieces:
            out = jnp.where(subs == row, piece, out)
        return out

    def panel(t, carry):
        start = pl.multiple_of(8 * t, 8)
        shift = (n - 8 * t) & (n - 1)
        pivots = left_ref[pl.ds(start, 8), :]
        pivots_right = right_ref[pl.ds(start, 8), :]
        corner = pltpu.roll(pivots, shift, 1)
        a = {(i, j): spread(corner, i, j) for i in range(8) for j in range(i + 1)}
        inverse, m = [], {}
        for j in range(8):
            inverse.append(1.0 / a[j, j])
            for i in range(j + 1, 8):
                m[i, j] = a[i, j] * inverse[j]
            for i in range(j + 1, 8):
                for k in range(j + 1, i + 1):
                    a[i, k] = a[i, k] - m[i, j] * a[k, j]
        unit = {}
        for i in range(8):
            for k in range(i):
                total = -m[i, k]
                for j in range(k + 1, i):
                    total = total - m[i, j] * unit[j, k]
                unit[i, k] = total
        zero = jnp.zeros((8, n), jnp.float32)
        down = [stacked([(i, unit[i, k]) for i in range(k + 1, 8)], zero) for k in range(7)]
        up = [stacked([(k, unit[i, k]) for k in range(i)], zero) for i in range(1, 8)]
        scale = stacked([(i, inverse[i]) for i in range(1, 8)], inverse[0])
        root = stacked([(i, a[i, i]) for i in range(1, 8)], a[0, 0])

        def reduce_rows(x):
            for_out = x
            for k in range(7):
                for_out = for_out + down[k] * row_of(x, k)
            scaled = for_out * scale
            back = scaled
            for i in range(1, 8):
                back = back + up[i - 1] * row_of(scaled, i)
            return for_out, back

        _, back_left = reduce_rows(pivots)
        done_right, back_right = reduce_rows(pivots_right)
        heads = jnp.where(lanes > 8 * t + 7, pivots, 0.0)
        upper = split_three(heads)
        lower = split_three(jnp.concatenate([back_left, back_right], axis=1))
        pairs = ((0, 0), (0, 1), (1, 0), (0, 2), (2, 0), (1, 1))
        change = lax.dot_general(
            jnp.concatenate([upper[p] for p, _ in pairs], axis=0),
            jnp.concatenate([lower[q] for _, q in pairs], axis=0),
            (((0,), (0,)), ((), ())),
            preferred_element_type=jnp.float32,
        )
        left_ref[...] = left_ref[...] - change[:, :n]
        right_ref[...] = right_ref[...] - change[:, n:]
        right_ref[pl.ds(start, 8), :] = done_right * lax.rsqrt(root)
        return carry

    lax.fori_loop(0, n // 8, panel, 0)


def factor_kernel(scale, gram_ref, twin_ref, out_ref, left_ref, right_ref):
    half = gram_ref.shape[0] // 2
    identity = jnp.where(
        lax.broadcasted_iota(jnp.int32, (half, half), 0)
        == lax.broadcasted_iota(jnp.int32, (half, half), 1),
        1.0,
        0.0,
    ).astype(jnp.float32)
    left_ref[...] = gram_ref[:half, :half] + twin_ref[:half, :half]
    right_ref[...] = identity
    invert_factor(left_ref, right_ref)
    first = right_ref[...]
    below = dot_f32(gram_ref[half:, :half] + twin_ref[half:, :half], first, ((1,), (1,)))
    left_ref[...] = (gram_ref[half:, half:] + twin_ref[half:, half:]) - dot_f32(
        below, below, ((1,), (1,))
    )
    right_ref[...] = identity
    invert_factor(left_ref, right_ref)
    second = right_ref[...]
    corner = -dot_f32(second, dot_f32(below, first))
    out_ref[:half, :half] = first.T * scale
    out_ref[:half, half:] = corner.T * scale
    out_ref[half:, :half] = jnp.zeros((half, half), jnp.float32)
    out_ref[half:, half:] = second.T * scale


def inverse_transposed_factor(gram, twin, scale):
    half = gram.shape[0] // 2
    return pl.pallas_call(
        lambda *refs: factor_kernel(scale, *refs),
        out_shape=jax.ShapeDtypeStruct(gram.shape, jnp.float32),
        in_specs=[pl.BlockSpec(memory_space=pltpu.VMEM)] * 2,
        out_specs=pl.BlockSpec(memory_space=pltpu.VMEM),
        scratch_shapes=[pltpu.VMEM((half, half), jnp.float32)] * 2,
        cost_estimate=pl.CostEstimate(
            flops=12_000_000_000, bytes_accessed=800_000, transcendentals=256
        ),
        name="factor",
    )(gram, twin)


def gram_step(x, even_ref, odd_ref):
    high, middle, low = split_three(x)

    def product(a, b):
        return lax.dot_general(
            a, b, (((0,), (0,)), ((), ())), preferred_element_type=jnp.float32
        )

    even_ref[...] += product(high, high) + product(middle, middle)
    odd_ref[...] += product(high, middle) + product(high, low)


def gram_kernel(x_ref, after_ref, out_ref, even_ref, odd_ref):
    even_ref[...] = jnp.zeros_like(even_ref)
    odd_ref[...] = jnp.zeros_like(odd_ref)

    def chunk(c, carry):
        gram_step(x_ref[pl.ds(pl.multiple_of(c * CHUNK, CHUNK), CHUNK), :], even_ref, odd_ref)
        return carry

    lax.fori_loop(0, x_ref.shape[0] // CHUNK, chunk, 0)
    out_ref[...] = even_ref[...] + odd_ref[...] + odd_ref[...].T


def gram_of(x, after):
    width = x.shape[1]
    return pl.pallas_call(
        gram_kernel,
        out_shape=jax.ShapeDtypeStruct((width, width), jnp.float32),
        in_specs=[WHOLE, pl.BlockSpec(memory_space=pl.ANY)],
        out_specs=WHOLE,
        scratch_shapes=[pltpu.VMEM((width, width), jnp.float32)] * 2,
        compiler_params=pltpu.CompilerParams(vmem_limit_bytes=VMEM_BYTES),
        cost_estimate=pl.CostEstimate(
            flops=2_000_000_000, bytes_accessed=2_400_000, transcendentals=0
        ),
        name="gram",
    )(x, after)


def image_kernel(raw_ref, factor_ref, image_ref, out_ref, even_ref, odd_ref):
    even_ref[...] = jnp.zeros_like(even_ref)
    odd_ref[...] = jnp.zeros_like(odd_ref)

    def chunk(c, carry):
        place = pl.ds(pl.multiple_of(c * CHUNK, CHUNK), CHUNK)
        image = dot_f32(raw_ref[place, :], factor_ref[...])
        image_ref[place, :] = image
        gram_step(image, even_ref, odd_ref)
        return carry

    lax.fori_loop(0, raw_ref.shape[0] // CHUNK, chunk, 0)
    out_ref[...] = even_ref[...] + odd_ref[...] + odd_ref[...].T


def image_and_gram(raw, factor):
    rows, width = raw.shape
    return pl.pallas_call(
        image_kernel,
        out_shape=(
            jax.ShapeDtypeStruct((rows, width), jnp.float32),
            jax.ShapeDtypeStruct((width, width), jnp.float32),
        ),
        in_specs=[WHOLE, WHOLE],
        out_specs=(WHOLE, WHOLE),
        scratch_shapes=[pltpu.VMEM((width, width), jnp.float32)] * 2,
        compiler_params=pltpu.CompilerParams(vmem_limit_bytes=VMEM_BYTES),
        cost_estimate=pl.CostEstimate(
            flops=3_000_000_000, bytes_accessed=5_000_000, transcendentals=0
        ),
        name="image",
    )(raw, factor)


def quotient_kernel(first_ref, factor_ref, image_ref, after_ref, out_ref):
    def chunk(c, carry):
        cross, square = carry
        place = pl.ds(pl.multiple_of(c * CHUNK, CHUNK), CHUNK)
        iterate = dot_f32(first_ref[place, :], factor_ref[...])
        return (
            cross + jnp.sum(iterate * image_ref[place, :], axis=0, keepdims=True),
            square + jnp.sum(iterate * iterate, axis=0, keepdims=True),
        )

    zero = jnp.zeros((1, first_ref.shape[1]), jnp.float32)
    cross, square = lax.fori_loop(0, first_ref.shape[0] // CHUNK, chunk, (zero, zero))
    out_ref[...] = jnp.zeros_like(out_ref)
    out_ref[0:1, :] = cross
    out_ref[1:2, :] = square


def quotient_sums(first, factor, image, after):
    width = first.shape[1]
    return pl.pallas_call(
        quotient_kernel,
        out_shape=jax.ShapeDtypeStruct((8, width), jnp.float32),
        in_specs=[WHOLE, WHOLE, WHOLE, pl.BlockSpec(memory_space=pl.ANY)],
        out_specs=WHOLE,
        compiler_params=pltpu.CompilerParams(vmem_limit_bytes=VMEM_BYTES),
        cost_estimate=pl.CostEstimate(
            flops=2_000_000_000, bytes_accessed=5_000_000, transcendentals=0
        ),
        name="quotient",
    )(first, factor, image, after)


def rows_kernel(blocks_ref, first_ref, weight_ref, gathered_ref, out_ref, start_ref):
    slim = out_ref.shape[1]
    sources, height, modes = gathered_ref.shape
    height = height // 2
    dofs = sources * height
    width = start_ref.shape[2]
    for q in range(modes // width):
        start_ref[:, height * q : height * (q + 1), :] = gathered_ref[
            :, height:, width * q : width * (q + 1)
        ]
    everything = gathered_ref[:, :height, :].reshape(dofs, modes)
    lane = lax.broadcasted_iota(jnp.int32, (slim, SB), 1)
    numbers = jnp.zeros((slim, SB), jnp.int32)
    for k in range(KB):
        numbers = jnp.where(lane == k, blocks_ref[k], numbers)
    numbers = numbers.astype(jnp.float32).astype(jnp.bfloat16)
    for h in range(2):
        wanted = first_ref[0] + h
        place = jnp.int32(0)
        found = jnp.int32(0)
        for k in range(KB):
            hit = (blocks_ref[k] == wanted).astype(jnp.int32)
            place += k * hit
            found += hit
        span = sources // KB
        picked = gathered_ref[pl.ds(place * span, span), :height, :].reshape(SB, modes)
        weighted = picked.astype(jnp.float32) * (weight_ref[...] * found.astype(jnp.float32))
        high, middle, low = split_three(weighted)

        def product(part):
            return lax.dot_general(
                part, everything, (((1,), (1,)), ((), ())), preferred_element_type=jnp.float32
            )

        rows = (product(high) + (product(middle) + product(low))).astype(jnp.bfloat16)
        for z in range(SB // slim):
            out_ref[2 * z + h, :, :dofs] = rows[z * slim : (z + 1) * slim, :]
            out_ref[2 * z + h, :, dofs:] = numbers


def operator_rows(blocks, first, weight, gathered, slim):
    sources, height, modes = gathered.shape
    dofs = sources * height // 2
    width = height * modes // 2 // SB
    scalars = pl.BlockSpec(memory_space=pltpu.SMEM)
    return pl.pallas_call(
        rows_kernel,
        out_shape=(
            jax.ShapeDtypeStruct((2 * SB // slim, slim, dofs + SB), jnp.bfloat16),
            jax.ShapeDtypeStruct((sources, SB, width), jnp.bfloat16),
        ),
        in_specs=[scalars, scalars, WHOLE, WHOLE],
        out_specs=(WHOLE, WHOLE),
        compiler_params=pltpu.CompilerParams(vmem_limit_bytes=VMEM_BYTES),
        cost_estimate=pl.CostEstimate(
            flops=800_000_000, bytes_accessed=2_700_000, transcendentals=0
        ),
        name="rows",
    )(blocks, first, weight, gathered)


def build_kernel(
    map_ref, core_ref, incoming_ref, flex_ref, start_ref, twin_ref,
    rows_ref, own_ref, other_ref, halves_ref,
):
    slim, total = flex_ref.shape
    for b in range(total // SB):
        halves_ref[b % 2, :, (b // 2) * SB : (b // 2 + 1) * SB] = flex_ref[
            :, b * SB : (b + 1) * SB
        ]
    for s in range(incoming_ref.shape[0]):
        for k in range(KB):
            b = map_ref[s * KB + k]
            place = pl.ds(pl.multiple_of((b >> 1) * SB, SB), SB)
            halves_ref[b & 1, :, place] += incoming_ref[s, :, k * SB : (k + 1) * SB].astype(
                jnp.float32
            )
    own = halves_ref[core_ref[0]]
    other = halves_ref[1 - core_ref[0]]
    own_ref[...] = own
    other_ref[...] = other
    first = jnp.dot(
        jnp.concatenate(split_three(own), axis=0), start_ref[...], preferred_element_type=jnp.float32
    )
    second = jnp.dot(
        jnp.concatenate(split_three(other), axis=0), twin_ref[...], preferred_element_type=jnp.float32
    )
    both = first + second
    rows_ref[...] = both[:slim] + (both[slim : 2 * slim] + both[2 * slim :])


def build_rows(map_all, core, incoming, flex, start, twin):
    slim = incoming.shape[1]
    total = flex.shape[1]
    width = start.shape[1]
    scalars = pl.BlockSpec(memory_space=pltpu.SMEM)
    half = jax.ShapeDtypeStruct((slim, total // 2), jnp.float32)
    return pl.pallas_call(
        build_kernel,
        out_shape=(jax.ShapeDtypeStruct((slim, width), jnp.float32), half, half),
        in_specs=[scalars] * 2 + [WHOLE] * 4,
        out_specs=(WHOLE, WHOLE, WHOLE),
        scratch_shapes=[
            pltpu.VMEM((2, slim, total // 2), jnp.float32),
        ],
        compiler_params=pltpu.CompilerParams(vmem_limit_bytes=VMEM_BYTES),
        cost_estimate=pl.CostEstimate(
            flops=300_000_000, bytes_accessed=4_000_000, transcendentals=0
        ),
        name="build",
    )(map_all, core, incoming, flex, start, twin)


def last_kernel(
    scale,
    place_ref, here_ref, gram_ref, gram_twin_ref, mine_ref, twin_ref, weight_ref, gathered_ref,
    modes_ref, own_ref, interior_ref, factor_ref, left_ref, right_ref, image_ref, dofs_ref,
    local_ref, result_ref, image_sems, mode_sem, dofs_sem, result_sems,
):
    count = 2 + KB
    rows = local_ref.shape[0]
    step = rows // 4
    load_modes = pltpu.make_async_copy(modes_ref, local_ref, mode_sem)
    load_dofs = pltpu.make_async_copy(
        gathered_ref.at[:, pl.ds(0, dofs_ref.shape[1]), :], dofs_ref, dofs_sem
    )
    for k in range(count):
        source = pl.ds(pl.multiple_of(place_ref[k] * SB, SB), SB)
        target = image_ref.at[pl.ds(k * SB, SB), :]

        @pl.when(here_ref[k] == 1)
        def _():
            pltpu.make_async_copy(mine_ref.at[source, :], target, image_sems.at[k]).start()

        @pl.when(here_ref[k] != 1)
        def _():
            pltpu.make_async_copy(twin_ref.at[source, :], target, image_sems.at[k]).start()

    load_modes.start()
    load_dofs.start()
    factor_kernel(scale, gram_ref, gram_twin_ref, factor_ref, left_ref, right_ref)
    for k in range(count):
        target = image_ref.at[pl.ds(k * SB, SB), :]
        pltpu.make_async_copy(mine_ref.at[pl.ds(0, SB), :], target, image_sems.at[k]).wait()
    load_dofs.wait()
    load_modes.wait()
    vectors = dot_f32(image_ref[...], factor_ref[...])
    own_ref[...] = vectors[: 2 * SB, :]
    touched = vectors[2 * SB :, :].astype(jnp.bfloat16)
    amplitude = lax.dot_general(
        touched,
        dofs_ref[...].reshape(KB * SB, dofs_ref.shape[2]),
        (((0,), (0,)), ((), ())),
        preferred_element_type=jnp.float32,
    )
    terms = (weight_ref[...] * amplitude).astype(jnp.bfloat16)
    stores = []
    for c in range(4):
        part = pl.ds(c * step, step)
        result_ref[part, :] = lax.dot_general(
            local_ref[part, :], terms, (((1,), (1,)), ((), ())), preferred_element_type=jnp.float32
        ).astype(jnp.bfloat16)
        stores.append(
            pltpu.make_async_copy(result_ref.at[part, :], interior_ref.at[part, :], result_sems.at[c])
        )
        stores[-1].start()
    for store in stores:
        store.wait()


def last_products(place, here, gram, gram_twin, mine, twin, weight, gathered, modes, scale):
    width = gram.shape[0]
    rows, count = modes.shape
    scalars = pl.BlockSpec(memory_space=pltpu.SMEM)
    anywhere = pl.BlockSpec(memory_space=pl.ANY)
    return pl.pallas_call(
        lambda *refs: last_kernel(scale, *refs),
        in_specs=[scalars, scalars, WHOLE, WHOLE, anywhere, anywhere, WHOLE, anywhere, anywhere],
        out_specs=(WHOLE, anywhere),
        out_shape=(
            jax.ShapeDtypeStruct((2 * SB, width), jnp.float32),
            jax.ShapeDtypeStruct((rows, width), jnp.bfloat16),
        ),
        scratch_shapes=[
            pltpu.VMEM((width, width), jnp.float32),
            pltpu.VMEM((width // 2, width // 2), jnp.float32),
            pltpu.VMEM((width // 2, width // 2), jnp.float32),
            pltpu.VMEM(((2 + KB) * SB, width), jnp.float32),
            pltpu.VMEM((gathered.shape[0], gathered.shape[1] // 2, count), jnp.bfloat16),
            pltpu.VMEM((rows, count), jnp.bfloat16),
            pltpu.VMEM((rows, width), jnp.bfloat16),
            pltpu.SemaphoreType.DMA((2 + KB,)),
            pltpu.SemaphoreType.DMA,
            pltpu.SemaphoreType.DMA,
            pltpu.SemaphoreType.DMA((4,)),
        ],
        compiler_params=pltpu.CompilerParams(vmem_limit_bytes=VMEM_BYTES),
        cost_estimate=pl.CostEstimate(
            flops=16_000_000_000, bytes_accessed=8_000_000, transcendentals=256
        ),
        name="last",
    )(place, here, gram, gram_twin, mine, twin, weight, gathered, modes)


def gather_blocks(x, axis):
    count = lax.axis_size(axis)
    spread = jnp.broadcast_to(x[None], (count,) + x.shape)
    return lax.all_to_all(spread, axis, 0, 0, tiled=True)


def per_device(modes, coupling, eigvals, mode_count, sep_map, sep_len, flex, init_vectors):
    shapes = modes[0]
    sep_count = lax.axis_size("sep")
    sub_count = lax.axis_size("sub")
    sep_index = lax.axis_index("sep")
    sub_index = lax.axis_index("sub")
    layers = sub_count // 2
    layer, core = sub_index >> 1, sub_index & 1
    mode_total = shapes.shape[1]
    vec_width = init_vectors.shape[1]
    owned_rows = init_vectors.shape[0]
    total_rows = owned_rows * sep_count
    local_dofs = KB * SB
    slim = SB // layers
    scaling = float(total_rows) ** 0.5

    def from_twin(x):
        return lax.ppermute(x, "sub", [(i, i ^ 1) for i in range(sub_count)])

    dof_ids = jnp.arange(SB, dtype=jnp.int32)
    live_dofs = (dof_ids[None, :] < sep_len[0][:, None]).reshape(local_dofs, 1)
    partial = lax.dot_general(
        coupling[0], shapes, (((0,), (0,)), ((), ())), preferred_element_type=jnp.float32
    )
    partial = jnp.where(live_dofs, partial, 0.0).astype(jnp.bfloat16)
    shares = lax.all_to_all(
        partial.reshape(sep_count, local_dofs // sep_count, mode_total), "sep", 0, 0, tiled=True
    )
    own_projected = jnp.sum(shares.astype(jnp.float32), axis=0).astype(jnp.bfloat16)
    share = local_dofs // sep_count
    fold = mode_total // vec_width
    start_rows = lax.dynamic_slice_in_dim(init_vectors, core * SB, SB, 0).astype(jnp.bfloat16)
    start_rows = jnp.concatenate([start_rows[share * q : share * (q + 1)] for q in range(fold)], axis=1)
    gathered = gather_blocks(jnp.concatenate([own_projected, start_rows], axis=0), "sep")
    mode_ids = jnp.arange(mode_total, dtype=jnp.int32)[None]
    mode_weight = jnp.where(mode_ids < mode_count[0], 1.0 / eigvals, 0.0)

    blocks = sep_map[0]
    outgoing, start_half = operator_rows(
        blocks, (2 * sep_index)[None], mode_weight, gathered, slim
    )
    start_half = start_half.reshape(total_rows // 2, vec_width)
    start_twin = from_twin(start_half)
    incoming = lax.all_to_all(outgoing, "sub", 0, 0, tiled=True)
    map_all = incoming[:, 0, local_dofs : local_dofs + KB].astype(jnp.int32).reshape(-1)

    row_start = core * SB + layer * slim
    flex_rows = lax.dynamic_slice_in_dim(flex, row_start, slim, 0)
    first_rows, own_half, twin_half = build_rows(
        map_all, core[None], incoming, flex_rows, start_half, start_twin
    )
    operator_half = jnp.concatenate([own_half, from_twin(twin_half)], axis=0)

    def from_layer(x, distance):
        perm = [(z * 2 + c, (z ^ distance) * 2 + c) for z in range(layers) for c in range(2)]
        return lax.ppermute(x, "sub", perm)

    def spread_layers(rows):
        other = from_layer(rows, 4)
        upper = (layer & 4) > 0
        pair = jnp.stack([jnp.where(upper, other, rows), jnp.where(upper, rows, other)])
        pieces = [pair] + [from_layer(pair, distance) for distance in (1, 2, 3)]
        odd, high = (layer & 1) > 0, (layer & 2) > 0
        pieces = [jnp.where(odd, pieces[q ^ 1], pieces[q]) for q in range(4)]
        pieces = [jnp.where(high, pieces[q ^ 2], pieces[q]) for q in range(4)]
        return jnp.stack(pieces, axis=1).reshape(SB, vec_width)

    def gather_half(part):
        return gather_blocks(part, "sep").reshape(total_rows // 2, vec_width)

    first_half = gather_half(spread_layers(first_rows))
    both_rows = dot_f32(operator_half, first_half)
    second_rows = both_rows[:slim] + from_twin(both_rows[slim:])
    second_part = spread_layers(second_rows)
    raw_half = gather_half(second_part)

    first_gram = gram_of(first_half, second_part)
    first_factor = inverse_transposed_factor(first_gram, from_twin(first_gram), scaling)

    image_half, second_gram = image_and_gram(raw_half, first_factor)
    sums = quotient_sums(first_half, first_factor, image_half, second_gram)
    sums = sums + from_twin(sums)
    quotient = sums[0] / sums[1]
    wanted = jnp.concatenate([2 * sep_index + jnp.arange(2, dtype=jnp.int32), blocks])
    separator_modes, interior = last_products(
        wanted >> 1,
        ((wanted & 1) == core).astype(jnp.int32),
        second_gram,
        from_twin(second_gram),
        image_half,
        from_twin(image_half),
        mode_weight,
        gathered,
        shapes,
        scaling,
    )
    return (separator_modes, quotient, interior[None])


def solution(mesh):
    placed = (
        P("sub", "sep", None),
        P("sub", "sep", None),
        P("sub", None),
        P("sub"),
        P("sub", None),
        P("sub", None),
        P("sep", None),
        P("sep", None),
    )
    return jax.shard_map(
        per_device,
        mesh=mesh,
        in_specs=placed,
        out_specs=(P("sep", None), P(), P("sub", "sep", None)),
        check_vma=False,
    )
```

time: 259 us -> 239 us (0.923)
  starting transfers between devices: 46.8 us -> 63.6 us
  between operations: 15.1 us -> 1.73 us
  matrix products: 19.6 us -> 8.19 us
  waiting for transfers between devices: 101 us -> 93.6 us
  other arithmetic: 9.03 us -> 1.94 us
    all_to_all x3, waiting for transfers between devices: 35.9 us -> 47.1 us  [gather_blocks(): return lax.all_to_all(spread, axis, 0, 0, tiled=True)]
    ppermute x6 -> x7, starting transfers between devices: 13.3 us -> 24.3 us  [from_twin(): return lax.ppermute(x, 'sub', [(i, i ^ 1) for i in range(sub_count)])]
    ppermute x6 -> x8, waiting for transfers between devices: 25.9 us -> 16.8 us  [from_layer(): return lax.ppermute(x, 'sub', perm)]
    all_gather x1 -> x0, waiting for transfers between devices: 8.66 us -> none  [per_device(): lax.all_gather(start_rows.astype(jnp.bfloat16), 'sep', axis=0, tiled=True)]
    ppermute x6 -> x8, starting transfers between devices: 1.68 us -> 9.5 us  [from_layer(): return lax.ppermute(x, 'sub', perm)]
    dot_general x5 -> x1, matrix products: 10.1 us -> 2.69 us  [dot_f32(): lax.dot_general(a, b, (contract, ((), ())), precision=HIGHEST, preferred_...]
    dot_general x2 -> x1, matrix products: 9.46 us -> 5.5 us  [per_device(): lax.dot_general(coupling[0], shapes, (((0,), (0,)), ((), ())), preferred_...]
    add x4 -> x3, other arithmetic: 3.81 us -> 0.01 us  [the longest x1 0.01 us: per_device(): second_rows = both_rows[:slim] + from_twin(both_rows[slim:])]
  transfers between devices with their start and end apart: 18 -> 20, of which waited for: 15 -> 15; matrix products, arithmetic and copies ran while one was open for 7% -> 1% of each run, Pallas kernels for 15% -> 9%
where the time goes in v1:
time: 239 us; the launch traced here: 238 us
  waiting for transfers between devices  93.6 us (39%)
  starting transfers between devices  63.6 us (27%)
  Pallas kernels  56.1 us (23%)
  local copies, waits for them, and re-layouts  12.9 us (5%)
  matrix products  8.19 us (3%)
    all_to_all x3, waiting for transfers between devices, gather_blocks(): return lax.all_to_all(spread, axis, 0, 0, tiled=True)  47.1 us
    ppermute x7, starting transfers between devices, from_twin(): return lax.ppermute(x, 'sub', [(i, i ^ 1) for i in range(sub_count)])  24.3 us
    pallas_call x1, Pallas kernels, last_products(): pl.pallas_call(lambda *refs: last_kernel(scale, *refs), in_specs=[scalars...  21.3 us
    ppermute x8, waiting for transfers between devices, from_layer(): return lax.ppermute(x, 'sub', perm)  16.8 us
    pallas_call x1, Pallas kernels, inverse_transposed_factor(): pl.pallas_call(lambda *refs: factor_kernel(scale, *refs), out_shape=jax.S...  15.9 us
    all_to_all x1, waiting for transfers between devices, per_device(): lax.all_to_all(partial.reshape(sep_count, local_dofs // sep_count, mode_t...  14.6 us
    all_to_all x3, starting transfers between devices, gather_blocks(): return lax.all_to_all(spread, axis, 0, 0, tiled=True)  13.6 us
    all_to_all x1, waiting for transfers between devices, per_device(): incoming = lax.all_to_all(outgoing, 'sub', 0, 0, tiled=True)  11.4 us
  transfers between devices with their start and end apart: 20, of which 15 were waited for; matrix products, arithmetic and copies ran while one was open for 1% of the time, Pallas kernels for 9%

profile of v1, /device:TPU:1, one launch (start us, length us, event | category | flops | bytes accessed | tf_op | source)
XLA Modules:
  0.0 238.0 jit_solution(7789876044683828453)
XLA Ops:
  0.6 0.9 fusion.9
  1.5 0.7 copy-done
  2.2 5.5 %select_convert_fusion = bf16[512,1024]{1,0:T(8,128)(2,1)} fusion(bf16[1,2048,512]{2,1,0:T(8,128)(2,1)S(1)} %copy-done, pred[512]{0:T(512)(128)(4,1)S(1)} %fusion.9, bf16[1,2048,1024]{2,1,0:T(8,128)(2,1)} %param.8), kind=kOutput, calls=%fused_computation.2 | convolution fusion | flops 2148532224 | bytes 7340544 | tf_op jit(solution)/shard_map/dot_general | solution.py:482
  7.7 7.6 %all-to-all-start = ((bf16[16,32,1024]{2,1,0:T(8,128)(2,1)}), bf16[16,32,1024]{2,1,0:T(8,128)(2,1)S(1)}, u32[]{:S(2)}, u32[]{:S(2)}) async-start(bf16[16,32,1024]{2,1,0:T(8,128)(2,1)} %bitcast.57), calls=%async_computation | async-start | bytes 2097152 | tf_op jit(solution)/shard_map/all_to_all | solution.py:486
  15.3 0.9 dynamic-slice_convert_fusion
  16.3 14.6 %all-to-all-done = bf16[16,32,1024]{2,1,0:T(8,128)(2,1)S(1)} async-done(((bf16[16,32,1024]{2,1,0:T(8,128)(2,1)}), bf16[16,32,1024]{2,1,0:T(8,128)(2,1)S(1)}, u32[]{:S(2)}, u32[]{:S(2)}) %all-to-all-start) | async-done | bytes 1048608 | tf_op jit(solution)/shard_map/all_to_all | solution.py:486
  31.1 1.6 broadcast_in_dim.51
  32.7 4.6 %all-to-all-start.1 = ((bf16[16,64,1024]{2,1,0:T(8,128)(2,1)}), bf16[16,64,1024]{2,1,0:T(8,128)(2,1)}, u32[]{:S(2)}, u32[]{:S(2)}) async-start(bf16[16,64,1024]{2,1,0:T(8,128)(2,1)} %broadcast_in_dim.51), calls=%async_computation.1 | async-start | bytes 4194304 | tf_op jit(solution)/shard_map/all_to_all | solution.py:458
  37.9 24.6 %all-to-all-done.1.gathered_ref.refs_7_ = bf16[16,64,1024]{2,1,0:T(8,128)(2,1)} async-done(((bf16[16,64,1024]{2,1,0:T(8,128)(2,1)}), bf16[16,64,1024]{2,1,0:T(8,128)(2,1)}, u32[]{:S(2)}, u32[]{:S(2)}) %all-to-all-start.1) | async-done | bytes 2097184 | tf_op jit(solution)/shard_map/all_to_all | solution.py:458
  62.5 3.8 %rows.1 = (bf16[16,16,640]{2,1,0:T(8,128)(2,1)S(1)}, bf16[16,128,256]{2,1,0:T(8,128)(2,1)S(1)}) custom-call(s32[4]{0:T(128)S(1)} %bitcast.53, s32[1]{0:T(128)} %bitcast.1.first_ref, f32[1,1024]{1,0:T(1,128)S(1)} %compare_select_fusion.weight_ref.refs_6_, bf16[16,64,1024]{2,1,0:T(8,128)(2,1)} %all-to-all-done.1.gathered_ref.refs_7_), custom_call_target="tpu_custom_call" | custom-call | flops 800000000 | bytes 2700000 | tf_op jit(solution)/shard_map/rows/pallas_call | solution.py:296
  66.3 0.7 copy-done.2
  67.1 5.7 %collective-permute-start = (bf16[2048,256]{1,0:T(8,128)(2,1)S(1)}, bf16[2048,256]{1,0:T(8,128)(2,1)}, u32[]{:S(2)}, u32[]{:S(2)}) collective-permute-start(bf16[2048,256]{1,0:T(8,128)(2,1)S(1)} %bitcast.49), channel_id=1, source_target_pairs={{0,16},{16,0},{32,48},{48,32},{64,80},{80,64},{96,112},{112,96},{1... | collective-permute-start | bytes 3145736 | tf_op jit(solution)/shard_map/ppermute | solution.py:478
  72.8 8.6 %all-to-all-start.2 = ((bf16[16,16,640]{2,1,0:T(8,128)(2,1)}), bf16[16,16,640]{2,1,0:T(8,128)(2,1)S(1)}, u32[]{:S(2)}, u32[]{:S(2)}) async-start(bf16[16,16,640]{2,1,0:T(8,128)(2,1)} %copy-done.2), calls=%async_computation.2 | async-start | bytes 655360 | tf_op jit(solution)/shard_map/all_to_all | solution.py:504
  81.3 1.7 constant_dynamic-slice_fusion.flex_ref
  83.0 11.4 %all-to-all-done.2.incoming_ref = bf16[16,16,640]{2,1,0:T(8,128)(2,1)S(1)} async-done(((bf16[16,16,640]{2,1,0:T(8,128)(2,1)}), bf16[16,16,640]{2,1,0:T(8,128)(2,1)S(1)}, u32[]{:S(2)}, u32[]{:S(2)}) %all-to-all-start.2) | async-done | bytes 327712 | tf_op jit(solution)/shard_map/all_to_all | solution.py:504
  94.6 0.9 copy-done.1
  95.5 2.0 build.1
  98.8 1.0 collective-permute-start.2
  99.8 5.8 %collective-permute-done.2 = f32[16,256]{1,0:T(8,128)S(1)} collective-permute-done((f32[16,256]{1,0:T(8,128)S(1)}, f32[16,256]{1,0:T(8,128)S(1)}, u32[]{:S(2)}, u32[]{:S(2)}) %collective-permute-start.2) | collective-permute-done | bytes 16416 | tf_op jit(solution)/shard_map/ppermute | solution.py:516
  105.7 0.9 collective-permute-start.4
  106.6 2.6 %collective-permute-start.3 = (f32[2,16,256]{2,1,0:T(8,128)S(1)}, f32[2,16,256]{2,1,0:T(8,128)S(1)}, u32[]{:S(2)}, u32[]{:S(2)}) collective-permute-start(f32[2,16,256]{2,1,0:T(8,128)S(1)} %pad_maximum_fusion.2), channel_id=1, source_target_pairs={{0,96},{16,112},{32,64},{48,80},{64,32},{80,48},{96,0},{112,16},{1... | collective-permute-start | bytes 98312 | tf_op jit(solution)/shard_map/ppermute | solution.py:516
  109.5 1.6 collective-permute-done.3
  111.2 1.6 broadcast_in_dim.54
  112.8 4.6 %all-to-all-start.3 = ((f32[16,128,256]{2,1,0:T(8,128)}), f32[16,128,256]{2,1,0:T(8,128)}, u32[]{:S(2)}, u32[]{:S(2)}) async-start(f32[16,128,256]{2,1,0:T(8,128)} %broadcast_in_dim.54), calls=%async_computation.3 | async-start | bytes 4194304 | tf_op jit(solution)/shard_map/all_to_all | solution.py:458
  117.4 3.3 %collective-permute-start.1 = (f32[16,2048]{1,0:T(8,128)S(1)}, f32[16,2048]{1,0:T(8,128)S(1)}, u32[]{:S(2)}, u32[]{:S(2)}) collective-permute-start(f32[16,2048]{1,0:T(8,128)S(1)} %copy-done.9), channel_id=1, source_target_pairs={{0,16},{16,0},{32,48},{48,32},{64,80},{80,64},{96,112},{112,96},{1... | collective-permute-start | bytes 393224 | tf_op jit(solution)/shard_map/ppermute | solution.py:478
  120.7 1.0 collective-permute-done.1
  121.7 20.9 %all-to-all-done.3 = f32[16,128,256]{2,1,0:T(8,128)} async-done(((f32[16,128,256]{2,1,0:T(8,128)}), f32[16,128,256]{2,1,0:T(8,128)}, u32[]{:S(2)}, u32[]{:S(2)}) %all-to-all-start.3) | async-done | bytes 2097184 | tf_op jit(solution)/shard_map/all_to_all | solution.py:458
  142.6 2.7 %fusion.4 = f32[32,256]{1,0:T(8,128)S(1)} fusion(f32[2048,256]{1,0:T(8,128)} %bitcast.17.x_ref.first_ref, f32[16,2048]{1,0:T(8,128)S(1)} %collective-permute-done.1, f32[16,2048]{1,0:T(8,128)S(1)} %copy-done.4), kind=kOutput, calls=%fused_computation.3 | convolution fusion | flops 201392128 | bytes 2392064 | tf_op jit(solution)/shard_map/dot_general | solution.py:17
  145.3 5.9 %collective-permute-start.6 = (f32[16,256]{1,0:T(8,128)S(1)}, f32[16,256]{1,0:T(8,128)S(1)}, u32[]{:S(2)}, u32[]{:S(2)}) collective-permute-start(f32[16,256]{1,0:T(8,128)S(1)} %slice.42), channel_id=1, source_target_pairs={{0,16},{16,0},{32,48},{48,32},{64,80},{80,64},{96,112},{112,96},{1... | collective-permute-start | bytes 49160 | tf_op jit(solution)/shard_map/ppermute | solution.py:478
  151.2 0.8 collective-permute-done.6
  152.0 1.3 collective-permute-start.7
  153.3 5.4 %collective-permute-done.7 = f32[16,256]{1,0:T(8,128)S(1)} collective-permute-done((f32[16,256]{1,0:T(8,128)S(1)}, f32[16,256]{1,0:T(8,128)S(1)}, u32[]{:S(2)}, u32[]{:S(2)}) %collective-permute-start.7) | collective-permute-done | bytes 16416 | tf_op jit(solution)/shard_map/ppermute | solution.py:516
  158.8 2.5 %collective-permute-start.9 = (f32[2,16,256]{2,1,0:T(8,128)S(1)}, f32[2,16,256]{2,1,0:T(8,128)S(1)}, u32[]{:S(2)}, u32[]{:S(2)}) collective-permute-start(f32[2,16,256]{2,1,0:T(8,128)S(1)} %pad_maximum_fusion.3), channel_id=1, source_target_pairs={{0,64},{16,80},{32,96},{48,112},{64,0},{80,16},{96,32},{112,48},{1... | collective-permute-start | bytes 98312 | tf_op jit(solution)/shard_map/ppermute | solution.py:516
  161.3 1.1 collective-permute-start.8
  162.6 3.5 %collective-permute-done.8 = f32[2,16,256]{2,1,0:T(8,128)S(1)} collective-permute-done((f32[2,16,256]{2,1,0:T(8,128)S(1)}, f32[2,16,256]{2,1,0:T(8,128)S(1)}, u32[]{:S(2)}, u32[]{:S(2)}) %collective-permute-start.8) | collective-permute-done | bytes 32800 | tf_op jit(solution)/shard_map/ppermute | solution.py:516
  166.1 1.6 broadcast_in_dim.56
  167.8 4.4 %all-to-all-start.4 = ((f32[16,128,256]{2,1,0:T(8,128)}), f32[16,128,256]{2,1,0:T(8,128)}, u32[]{:S(2)}, u32[]{:S(2)}) async-start(f32[16,128,256]{2,1,0:T(8,128)} %broadcast_in_dim.56), calls=%async_computation.4 | async-start | bytes 4194304 | tf_op jit(solution)/shard_map/all_to_all | solution.py:458
  172.2 2.9 %gram.1.refs_0_ = f32[256,256]{1,0:T(8,128)S(1)} custom-call(f32[2048,256]{1,0:T(8,128)} %bitcast.17.x_ref.first_ref, f32[128,256]{1,0:T(8,128)S(1)} %bitcast.52), custom_call_target="tpu_custom_call" | custom-call | flops 2000000000 | bytes 2400000 | tf_op jit(solution)/shard_map/gram/pallas_call | solution.py:171
  175.1 3.1 %collective-permute-start.11 = (f32[256,256]{1,0:T(8,128)S(1)}, f32[256,256]{1,0:T(8,128)S(1)}, u32[]{:S(2)}, u32[]{:S(2)}) collective-permute-start(f32[256,256]{1,0:T(8,128)S(1)} %gram.1.refs_0_), channel_id=1, source_target_pairs={{0,16},{16,0},{32,48},{48,32},{64,80},{80,64},{96,112},{112,96},{1... | collective-permute-start | bytes 786440 | tf_op jit(solution)/shard_map/ppermute | solution.py:478
  178.2 1.2 collective-permute-done.11.refs_1_
  180.1 15.9 %factor.1.factor_ref = f32[256,256]{1,0:T(8,128)} custom-call(f32[256,256]{1,0:T(8,128)} %copy-done.7, f32[256,256]{1,0:T(8,128)} %copy-done.13), custom_call_target="tpu_custom_call" | custom-call | flops 12000000000 | bytes 800000 | tf_op jit(solution)/shard_map/factor/pallas_call | solution.py:132
  196.0 1.6 all-to-all-done.4
  197.6 0.9 copy-done.10
  198.5 6.4 %image.1 = (f32[2048,256]{1,0:T(8,128)S(1)}, f32[256,256]{1,0:T(8,128)S(1)}) custom-call(f32[2048,256]{1,0:T(8,128)} %bitcast.25.raw_ref, f32[256,256]{1,0:T(8,128)S(1)} %copy-done.10), custom_call_target="tpu_custom_call" | custom-call | flops 3000000000 | bytes 5000000 | tf_op jit(solution)/shard_map/image/pallas_call | solution.py:202
  205.0 5.6 %collective-permute-start.13 = (f32[2048,256]{1,0:T(8,128)S(1)}, f32[2048,256]{1,0:T(8,128)S(1)}, u32[]{:S(2)}, u32[]{:S(2)}) collective-permute-start(f32[2048,256]{1,0:T(8,128)S(1)} %get-tuple-element.18.refs_4_.image_ref), channel_id=1, source_target_pairs={{0,16},{16,0},{32,48},{48,32},{64,80},{80,64},{96,112},{112,96},{1... | collective-permute-start | bytes 6291464 | tf_op jit(solution)/shard_map/ppermute | solution.py:478
  210.7 3.7 %quotient.1 = f32[8,256]{1,0:T(8,128)S(1)} custom-call(f32[2048,256]{1,0:T(8,128)} %bitcast.17.x_ref.first_ref, f32[256,256]{1,0:T(8,128)S(1)} %copy-done.11, f32[2048,256]{1,0:T(8,128)S(1)} %get-tuple-element.18.refs_4_.image_ref, f32[256,256]{1,0:T(8,128)S(1)} %get-tuple-element.17.refs_2_.after_ref), custom_call_target="tpu_custom_call" | custom-call | flops 2000000000 | bytes 5000000 | tf_op jit(solution)/shard_map/quotient/pallas_call | solution.py:238
  215.2 0.8 collective-permute-done.14
  216.5 21.3 %last.1 = (f32[256,256]{1,0:T(8,128)}, bf16[2048,256]{1,0:T(8,128)(2,1)}) custom-call(s32[6]{0:T(128)S(1)} %broadcast_shift-right-arithmetic_fusion.refs_0_, s32[6]{0:T(128)S(1)} %compare_convert_fusion.refs_1_, f32[256,256]{1,0:T(8,128)S(1)} %get-tuple-element.17.refs_2_.after_ref, f32[256,256]{1,0:T(8,128)S(1)} %collective-permute-done.12.refs_3_, ...), custom_call_target="tpu_custom_call" | custom-call | flops 16000000000 | bytes 8000000 | tf_op jit(solution)/shard_map/last/pallas_call | solution.py:426
  (58 shorter events, 4.8 us)
Async XLA Ops:
  0.6 1.6 copy-start
  7.7 23.1 %all-to-all-start = ((bf16[16,32,1024]{2,1,0:T(8,128)(2,1)}), bf16[16,32,1024]{2,1,0:T(8,128)(2,1)S(1)}, u32[]{:S(2)}, u32[]{:S(2)}) async-start(bf16[16,32,1024]{2,1,0:T(8,128)(2,1)} %bitcast.57), calls=%async_computation | async-start | bytes 2097152 | tf_op jit(solution)/shard_map/all_to_all | solution.py:486
  32.7 5.2 %copy-start.12 = (f32[1,1024]{1,0:T(1,128)S(1)}, f32[1,1024]{1,0:T(1,128)}, u32[]{:S(2)}) copy-start(f32[1,1024]{1,0:T(1,128)} %param.10) | copy-start | bytes 12292
  32.7 29.8 %copy-start.5 = (s32[1,4]{1,0:T(1,128)S(1)}, s32[1,4]{1,0:T(1,128)}, u32[]{:S(2)}) copy-start(s32[1,4]{1,0:T(1,128)} %param.12) | copy-start | bytes 52
  32.7 29.8 %all-to-all-start.1 = ((bf16[16,64,1024]{2,1,0:T(8,128)(2,1)}), bf16[16,64,1024]{2,1,0:T(8,128)(2,1)}, u32[]{:S(2)}, u32[]{:S(2)}) async-start(bf16[16,64,1024]{2,1,0:T(8,128)(2,1)} %broadcast_in_dim.51), calls=%async_computation.1 | async-start | bytes 4194304 | tf_op jit(solution)/shard_map/all_to_all | solution.py:458
  66.3 0.7 copy-start.2
  67.1 27.5 %collective-permute-start = (bf16[2048,256]{1,0:T(8,128)(2,1)S(1)}, bf16[2048,256]{1,0:T(8,128)(2,1)}, u32[]{:S(2)}, u32[]{:S(2)}) collective-permute-start(bf16[2048,256]{1,0:T(8,128)(2,1)S(1)} %bitcast.49), channel_id=1, source_target_pairs={{0,16},{16,0},{32,48},{48,32},{64,80},{80,64},{96,112},{112,96},{1... | collective-permute-start | bytes 3145736 | tf_op jit(solution)/shard_map/ppermute | solution.py:478
  72.8 21.7 %all-to-all-start.2 = ((bf16[16,16,640]{2,1,0:T(8,128)(2,1)}), bf16[16,16,640]{2,1,0:T(8,128)(2,1)S(1)}, u32[]{:S(2)}, u32[]{:S(2)}) async-start(bf16[16,16,640]{2,1,0:T(8,128)(2,1)} %copy-done.2), calls=%async_computation.2 | async-start | bytes 655360 | tf_op jit(solution)/shard_map/all_to_all | solution.py:504
  94.5 1.0 copy-start.1
  97.5 0.7 copy-start.3
  98.2 0.7 copy-start.8
  98.8 6.7 %collective-permute-start.2 = (f32[16,256]{1,0:T(8,128)S(1)}, f32[16,256]{1,0:T(8,128)S(1)}, u32[]{:S(2)}, u32[]{:S(2)}) collective-permute-start(f32[16,256]{1,0:T(8,128)S(1)} %get-tuple-element.16), channel_id=1, source_target_pairs={{0,128},{16,144},{32,160},{48,176},{64,192},{80,208},{96,224},{112... | collective-permute-start | bytes 49160 | tf_op jit(solution)/shard_map/ppermute | solution.py:516
  105.6 3.6 %collective-permute-start.5 = (f32[2,16,256]{2,1,0:T(8,128)S(1)}, f32[2,16,256]{2,1,0:T(8,128)S(1)}, u32[]{:S(2)}, u32[]{:S(2)}) collective-permute-start(f32[2,16,256]{2,1,0:T(8,128)S(1)} %pad_maximum_fusion.2), channel_id=1, source_target_pairs={{0,32},{16,48},{32,0},{48,16},{64,96},{80,112},{96,64},{112,80},{1... | collective-permute-start | bytes 98312 | tf_op jit(solution)/shard_map/ppermute | solution.py:516
  105.7 3.9 %collective-permute-start.4 = (f32[2,16,256]{2,1,0:T(8,128)S(1)}, f32[2,16,256]{2,1,0:T(8,128)S(1)}, u32[]{:S(2)}, u32[]{:S(2)}) collective-permute-start(f32[2,16,256]{2,1,0:T(8,128)S(1)} %pad_maximum_fusion.2), channel_id=1, source_target_pairs={{0,64},{16,80},{32,96},{48,112},{64,0},{80,16},{96,32},{112,48},{1... | collective-permute-start | bytes 98312 | tf_op jit(solution)/shard_map/ppermute | solution.py:516
  106.6 4.6 %collective-permute-start.3 = (f32[2,16,256]{2,1,0:T(8,128)S(1)}, f32[2,16,256]{2,1,0:T(8,128)S(1)}, u32[]{:S(2)}, u32[]{:S(2)}) collective-permute-start(f32[2,16,256]{2,1,0:T(8,128)S(1)} %pad_maximum_fusion.2), channel_id=1, source_target_pairs={{0,96},{16,112},{32,64},{48,80},{64,32},{80,48},{96,0},{112,16},{1... | collective-permute-start | bytes 98312 | tf_op jit(solution)/shard_map/ppermute | solution.py:516
  112.8 4.6 %copy-start.9 = (f32[16,2048]{1,0:T(8,128)S(1)}, f32[16,2048]{1,0:T(8,128)}, u32[]{:S(2)}) copy-start(f32[16,2048]{1,0:T(8,128)} %copy-done.8) | copy-start | bytes 393220
  112.8 29.8 %copy-start.4 = (f32[16,2048]{1,0:T(8,128)S(1)}, f32[16,2048]{1,0:T(8,128)}, u32[]{:S(2)}) copy-start(f32[16,2048]{1,0:T(8,128)} %copy-done.3) | copy-start | bytes 393220
  112.8 29.8 %all-to-all-start.3 = ((f32[16,128,256]{2,1,0:T(8,128)}), f32[16,128,256]{2,1,0:T(8,128)}, u32[]{:S(2)}, u32[]{:S(2)}) async-start(f32[16,128,256]{2,1,0:T(8,128)} %broadcast_in_dim.54), calls=%async_computation.3 | async-start | bytes 4194304 | tf_op jit(solution)/shard_map/all_to_all | solution.py:458
  117.4 4.3 %collective-permute-start.1 = (f32[16,2048]{1,0:T(8,128)S(1)}, f32[16,2048]{1,0:T(8,128)S(1)}, u32[]{:S(2)}, u32[]{:S(2)}) collective-permute-start(f32[16,2048]{1,0:T(8,128)S(1)} %copy-done.9), channel_id=1, source_target_pairs={{0,16},{16,0},{32,48},{48,32},{64,80},{80,64},{96,112},{112,96},{1... | collective-permute-start | bytes 393224 | tf_op jit(solution)/shard_map/ppermute | solution.py:478
  145.3 6.7 %collective-permute-start.6 = (f32[16,256]{1,0:T(8,128)S(1)}, f32[16,256]{1,0:T(8,128)S(1)}, u32[]{:S(2)}, u32[]{:S(2)}) collective-permute-start(f32[16,256]{1,0:T(8,128)S(1)} %slice.42), channel_id=1, source_target_pairs={{0,16},{16,0},{32,48},{48,32},{64,80},{80,64},{96,112},{112,96},{1... | collective-permute-start | bytes 49160 | tf_op jit(solution)/shard_map/ppermute | solution.py:478
  152.0 6.7 %collective-permute-start.7 = (f32[16,256]{1,0:T(8,128)S(1)}, f32[16,256]{1,0:T(8,128)S(1)}, u32[]{:S(2)}, u32[]{:S(2)}) collective-permute-start(f32[16,256]{1,0:T(8,128)S(1)} %slice_add_fusion), channel_id=1, source_target_pairs={{0,128},{16,144},{32,160},{48,176},{64,192},{80,208},{96,224},{112... | collective-permute-start | bytes 49160 | tf_op jit(solution)/shard_map/ppermute | solution.py:516
  158.7 3.6 %collective-permute-start.10 = (f32[2,16,256]{2,1,0:T(8,128)S(1)}, f32[2,16,256]{2,1,0:T(8,128)S(1)}, u32[]{:S(2)}, u32[]{:S(2)}) collective-permute-start(f32[2,16,256]{2,1,0:T(8,128)S(1)} %pad_maximum_fusion.3), channel_id=1, source_target_pairs={{0,32},{16,48},{32,0},{48,16},{64,96},{80,112},{96,64},{112,80},{1... | collective-permute-start | bytes 98312 | tf_op jit(solution)/shard_map/ppermute | solution.py:516
  158.8 3.8 %collective-permute-start.9 = (f32[2,16,256]{2,1,0:T(8,128)S(1)}, f32[2,16,256]{2,1,0:T(8,128)S(1)}, u32[]{:S(2)}, u32[]{:S(2)}) collective-permute-start(f32[2,16,256]{2,1,0:T(8,128)S(1)} %pad_maximum_fusion.3), channel_id=1, source_target_pairs={{0,64},{16,80},{32,96},{48,112},{64,0},{80,16},{96,32},{112,48},{1... | collective-permute-start | bytes 98312 | tf_op jit(solution)/shard_map/ppermute | solution.py:516
  161.3 4.8 %collective-permute-start.8 = (f32[2,16,256]{2,1,0:T(8,128)S(1)}, f32[2,16,256]{2,1,0:T(8,128)S(1)}, u32[]{:S(2)}, u32[]{:S(2)}) collective-permute-start(f32[2,16,256]{2,1,0:T(8,128)S(1)} %pad_maximum_fusion.3), channel_id=1, source_target_pairs={{0,96},{16,112},{32,64},{48,80},{64,32},{80,48},{96,0},{112,16},{1... | collective-permute-start | bytes 98312 | tf_op jit(solution)/shard_map/ppermute | solution.py:516
  167.8 29.8 %all-to-all-start.4 = ((f32[16,128,256]{2,1,0:T(8,128)}), f32[16,128,256]{2,1,0:T(8,128)}, u32[]{:S(2)}, u32[]{:S(2)}) async-start(f32[16,128,256]{2,1,0:T(8,128)} %broadcast_in_dim.56), calls=%async_computation.4 | async-start | bytes 4194304 | tf_op jit(solution)/shard_map/all_to_all | solution.py:458
  175.1 4.2 %copy-start.7 = (f32[256,256]{1,0:T(8,128)}, f32[256,256]{1,0:T(8,128)S(1)}, u32[]{:S(2)}) copy-start(f32[256,256]{1,0:T(8,128)S(1)} %gram.1.refs_0_) | copy-start | bytes 786436
  175.1 4.2 %collective-permute-start.11 = (f32[256,256]{1,0:T(8,128)S(1)}, f32[256,256]{1,0:T(8,128)S(1)}, u32[]{:S(2)}, u32[]{:S(2)}) collective-permute-start(f32[256,256]{1,0:T(8,128)S(1)} %gram.1.refs_0_), channel_id=1, source_target_pairs={{0,16},{16,0},{32,48},{48,32},{64,80},{80,64},{96,112},{112,96},{1... | collective-permute-start | bytes 786440 | tf_op jit(solution)/shard_map/ppermute | solution.py:478
  179.4 0.7 copy-start.13
  197.6 1.0 copy-start.10
  198.5 12.2 %copy-start.11 = (f32[256,256]{1,0:T(8,128)S(1)}, f32[256,256]{1,0:T(8,128)}, u32[]{:S(2)}) copy-start(f32[256,256]{1,0:T(8,128)} %factor.1.factor_ref) | copy-start | bytes 786436
  205.0 11.5 %collective-permute-start.13 = (f32[2048,256]{1,0:T(8,128)S(1)}, f32[2048,256]{1,0:T(8,128)S(1)}, u32[]{:S(2)}, u32[]{:S(2)}) collective-permute-start(f32[2048,256]{1,0:T(8,128)S(1)} %get-tuple-element.18.refs_4_.image_ref), channel_id=1, source_target_pairs={{0,16},{16,0},{32,48},{48,32},{64,80},{80,64},{96,112},{112,96},{1... | collective-permute-start | bytes 6291464 | tf_op jit(solution)/shard_map/ppermute | solution.py:478
  210.7 5.8 %copy-start.6 = (bf16[1,2048,1024]{2,1,0:T(8,128)(2,1)S(1)}, bf16[1,2048,1024]{2,1,0:T(8,128)(2,1)}, u32[]{:S(2)}) copy-start(bf16[1,2048,1024]{2,1,0:T(8,128)(2,1)} %param.8) | copy-start | bytes 12582916
  210.7 5.8 %collective-permute-start.12 = (f32[256,256]{1,0:T(8,128)S(1)}, f32[256,256]{1,0:T(8,128)S(1)}, u32[]{:S(2)}, u32[]{:S(2)}) collective-permute-start(f32[256,256]{1,0:T(8,128)S(1)} %get-tuple-element.17.refs_2_.after_ref), channel_id=1, source_target_pairs={{0,16},{16,0},{32,48},{48,32},{64,80},{80,64},{96,112},{112,96},{1... | collective-permute-start | bytes 786440 | tf_op jit(solution)/shard_map/ppermute | solution.py:478
  214.4 1.5 collective-permute-start.14

commit v2 on v1

--- a/solution.py
+++ b/solution.py
@@ -8,7 +8,7 @@
 KB = 4
 SB = 128
 CHUNK = 2048
-VMEM_BYTES = 32 * 1024 * 1024
+VMEM_BYTES = 20 * 1024 * 1024
 HIGHEST = lax.Precision.HIGHEST
 WHOLE = pl.BlockSpec(memory_space=pltpu.VMEM)
 
@@ -102,7 +102,7 @@
 
 
 def factor_kernel(scale, gram_ref, twin_ref, out_ref, left_ref, right_ref):
-    half = gram_ref.shape[0] // 2
+    half = gram_ref.shape[1] // 2
     identity = jnp.where(
         lax.broadcasted_iota(jnp.int32, (half, half), 0)
         == lax.broadcasted_iota(jnp.int32, (half, half), 1),
@@ -113,10 +113,10 @@
     right_ref[...] = identity
     invert_factor(left_ref, right_ref)
     first = right_ref[...]
-    below = dot_f32(gram_ref[half:, :half] + twin_ref[half:, :half], first, ((1,), (1,)))
-    left_ref[...] = (gram_ref[half:, half:] + twin_ref[half:, half:]) - dot_f32(
-        below, below, ((1,), (1,))
-    )
+    below = dot_f32(gram_ref[half : 2 * half, :half] + twin_ref[half : 2 * half, :half], first, ((1,), (1,)))
+    left_ref[...] = (
+        gram_ref[half : 2 * half, half:] + twin_ref[half : 2 * half, half:]
+    ) - dot_f32(below, below, ((1,), (1,)))
     right_ref[...] = identity
     invert_factor(left_ref, right_ref)
     second = right_ref[...]
@@ -135,6 +135,7 @@
         in_specs=[pl.BlockSpec(memory_space=pltpu.VMEM)] * 2,
         out_specs=pl.BlockSpec(memory_space=pltpu.VMEM),
         scratch_shapes=[pltpu.VMEM((half, half), jnp.float32)] * 2,
+        compiler_params=pltpu.CompilerParams(vmem_limit_bytes=VMEM_BYTES),
         cost_estimate=pl.CostEstimate(
             flops=12_000_000_000, bytes_accessed=800_000, transcendentals=256
         ),
@@ -182,70 +183,87 @@
     )(x, after)
 
 
-def image_kernel(raw_ref, factor_ref, image_ref, out_ref, even_ref, odd_ref):
+def iterate_kernel(first_ref, factor_ref, iterate_ref):
+    iterate_ref[...] = dot_f32(first_ref[...], factor_ref[...])
+
+
+def iterate_of(first, factor):
+    return pl.pallas_call(
+        iterate_kernel,
+        out_shape=jax.ShapeDtypeStruct(first.shape, jnp.float32),
+        in_specs=[WHOLE, WHOLE],
+        out_specs=WHOLE,
+        compiler_params=pltpu.CompilerParams(vmem_limit_bytes=VMEM_BYTES),
+        cost_estimate=pl.CostEstimate(
+            flops=2_000_000_000, bytes_accessed=4_000_000, transcendentals=0
+        ),
+        name="iterate",
+    )(first, factor)
+
+
+def image_kernel(raw_ref, iterate_ref, factor_ref, image_ref, out_ref, even_ref, odd_ref):
+    width = even_ref.shape[0]
     even_ref[...] = jnp.zeros_like(even_ref)
     odd_ref[...] = jnp.zeros_like(odd_ref)
-
-    def chunk(c, carry):
-        place = pl.ds(pl.multiple_of(c * CHUNK, CHUNK), CHUNK)
-        image = dot_f32(raw_ref[place, :], factor_ref[...])
-        image_ref[place, :] = image
-        gram_step(image, even_ref, odd_ref)
-        return carry
-
-    lax.fori_loop(0, raw_ref.shape[0] // CHUNK, chunk, 0)
-    out_ref[...] = even_ref[...] + odd_ref[...] + odd_ref[...].T
-
-
-def image_and_gram(raw, factor):
+    image = dot_f32(raw_ref[...], factor_ref[...])
+    image_ref[...] = image
+    gram_step(image, even_ref, odd_ref)
+    iterate = iterate_ref[...]
+    out_ref[width:, :] = jnp.zeros((out_ref.shape[0] - width, width), jnp.float32)
+    out_ref[width : width + 1, :] = jnp.sum(iterate * image, axis=0, keepdims=True)
+    out_ref[width + 1 : width + 2, :] = jnp.sum(iterate * iterate, axis=0, keepdims=True)
+    out_ref[:width, :] = even_ref[...] + odd_ref[...] + odd_ref[...].T
+
+
+def image_and_sums(raw, iterate, factor):
     rows, width = raw.shape
     return pl.pallas_call(
         image_kernel,
         out_shape=(
             jax.ShapeDtypeStruct((rows, width), jnp.float32),
-            jax.ShapeDtypeStruct((width, width), jnp.float32),
-        ),
-        in_specs=[WHOLE, WHOLE],
+            jax.ShapeDtypeStruct((width + 8, width), jnp.float32),
+        ),
+        in_specs=[WHOLE, WHOLE, WHOLE],
         out_specs=(WHOLE, WHOLE),
         scratch_shapes=[pltpu.VMEM((width, width), jnp.float32)] * 2,
         compiler_params=pltpu.CompilerParams(vmem_limit_bytes=VMEM_BYTES),
         cost_estimate=pl.CostEstimate(
-            flops=3_000_000_000, bytes_accessed=5_000_000, transcendentals=0
+            flops=3_000_000_000, bytes_accessed=7_000_000, transcendentals=0
         ),
         name="image",
-    )(raw, factor)
-
-
-def quotient_kernel(first_ref, factor_ref, image_ref, after_ref, out_ref):
-    def chunk(c, carry):
-        cross, square = carry
-        place = pl.ds(pl.multiple_of(c * CHUNK, CHUNK), CHUNK)
-        iterate = dot_f32(first_ref[place, :], factor_ref[...])
-        return (
-            cross + jnp.sum(iterate * image_ref[place, :], axis=0, keepdims=True),
-            square + jnp.sum(iterate * iterate, axis=0, keepdims=True),
-        )
-
-    zero = jnp.zeros((1, first_ref.shape[1]), jnp.float32)
-    cross, square = lax.fori_loop(0, first_ref.shape[0] // CHUNK, chunk, (zero, zero))
-    out_ref[...] = jnp.zeros_like(out_ref)
-    out_ref[0:1, :] = cross
-    out_ref[1:2, :] = square
-
-
-def quotient_sums(first, factor, image, after):
-    width = first.shape[1]
-    return pl.pallas_call(
-        quotient_kernel,
-        out_shape=jax.ShapeDtypeStruct((8, width), jnp.float32),
-        in_specs=[WHOLE, WHOLE, WHOLE, pl.BlockSpec(memory_space=pl.ANY)],
-        out_specs=WHOLE,
-        compiler_params=pltpu.CompilerParams(vmem_limit_bytes=VMEM_BYTES),
-        cost_estimate=pl.CostEstimate(
-            flops=2_000_000_000, bytes_accessed=5_000_000, transcendentals=0
-        ),
-        name="quotient",
-    )(first, factor, image, after)
+    )(raw, iterate, factor)
+
+
+def spread_kernel(low_ref, own_ref, one_ref, two_ref, three_ref, after_ref, out_ref, part_ref, sems):
+    slim = own_ref.shape[1]
+    for e, piece_ref in enumerate((own_ref, one_ref, two_ref, three_ref)):
+        for b in range(2):
+            place = (4 * b + (low_ref[0] ^ e)) * slim
+            part_ref[pl.ds(pl.multiple_of(place, slim), slim), :] = piece_ref[b]
+    copies = [
+        pltpu.make_async_copy(part_ref, out_ref.at[k], sems.at[k]) for k in range(out_ref.shape[0])
+    ]
+    for copy in copies:
+        copy.start()
+    for copy in copies:
+        copy.wait()
+
+
+def spread_rows(low, pieces, after, count):
+    slim, width = pieces[0].shape[1:]
+    anywhere = pl.BlockSpec(memory_space=pl.ANY)
+    return pl.pallas_call(
+        spread_kernel,
+        out_shape=jax.ShapeDtypeStruct((count, 8 * slim, width), jnp.float32),
+        in_specs=[pl.BlockSpec(memory_space=pltpu.SMEM)] + [WHOLE] * 4 + [anywhere],
+        out_specs=anywhere,
+        scratch_shapes=[
+            pltpu.VMEM((8 * slim, width), jnp.float32),
+            pltpu.SemaphoreType.DMA((count,)),
+        ],
+        cost_estimate=pl.CostEstimate(flops=0, bytes_accessed=2_400_000, transcendentals=0),
+        name="spread",
+    )(low, *pieces, after)
 
 
 def rows_kernel(blocks_ref, first_ref, weight_ref, gathered_ref, out_ref, start_ref):
@@ -364,7 +382,7 @@
 def last_kernel(
     scale,
     place_ref, here_ref, gram_ref, gram_twin_ref, mine_ref, twin_ref, weight_ref, gathered_ref,
-    modes_ref, own_ref, interior_ref, factor_ref, left_ref, right_ref, image_ref, dofs_ref,
+    modes_ref, own_ref, quotient_ref, interior_ref, factor_ref, left_ref, right_ref, image_ref, dofs_ref,
     local_ref, result_ref, image_sems, mode_sem, dofs_sem, result_sems,
 ):
     count = 2 + KB
@@ -388,6 +406,9 @@
 
     load_modes.start()
     load_dofs.start()
+    width = gram_ref.shape[1]
+    sums = gram_ref[width:, :] + gram_twin_ref[width:, :]
+    quotient_ref[...] = sums[0:1, :] / sums[1:2, :]
     factor_kernel(scale, gram_ref, gram_twin_ref, factor_ref, left_ref, right_ref)
     for k in range(count):
         target = image_ref.at[pl.ds(k * SB, SB), :]
@@ -419,16 +440,17 @@
 
 
 def last_products(place, here, gram, gram_twin, mine, twin, weight, gathered, modes, scale):
-    width = gram.shape[0]
+    width = gram.shape[1]
     rows, count = modes.shape
     scalars = pl.BlockSpec(memory_space=pltpu.SMEM)
     anywhere = pl.BlockSpec(memory_space=pl.ANY)
     return pl.pallas_call(
         lambda *refs: last_kernel(scale, *refs),
         in_specs=[scalars, scalars, WHOLE, WHOLE, anywhere, anywhere, WHOLE, anywhere, anywhere],
-        out_specs=(WHOLE, anywhere),
+        out_specs=(WHOLE, WHOLE, anywhere),
         out_shape=(
             jax.ShapeDtypeStruct((2 * SB, width), jnp.float32),
+            jax.ShapeDtypeStruct((1, width), jnp.float32),
             jax.ShapeDtypeStruct((rows, width), jnp.bfloat16),
         ),
         scratch_shapes=[
@@ -477,17 +499,19 @@
     def from_twin(x):
         return lax.ppermute(x, "sub", [(i, i ^ 1) for i in range(sub_count)])
 
-    dof_ids = jnp.arange(SB, dtype=jnp.int32)
-    live_dofs = (dof_ids[None, :] < sep_len[0][:, None]).reshape(local_dofs, 1)
+    share = local_dofs // sep_count
     partial = lax.dot_general(
         coupling[0], shapes, (((0,), (0,)), ((), ())), preferred_element_type=jnp.float32
     )
-    partial = jnp.where(live_dofs, partial, 0.0).astype(jnp.bfloat16)
+    partial = partial.astype(jnp.bfloat16)
     shares = lax.all_to_all(
-        partial.reshape(sep_count, local_dofs // sep_count, mode_total), "sep", 0, 0, tiled=True
-    )
-    own_projected = jnp.sum(shares.astype(jnp.float32), axis=0).astype(jnp.bfloat16)
-    share = local_dofs // sep_count
+        partial.reshape(sep_count, share, mode_total), "sep", 0, 0, tiled=True
+    )
+    first_dof = sep_index * share
+    length = lax.dynamic_index_in_dim(sep_len[0], first_dof // SB, 0, keepdims=False)
+    live = first_dof % SB + jnp.arange(share, dtype=jnp.int32) < length
+    own_projected = jnp.sum(shares.astype(jnp.float32), axis=0)
+    own_projected = jnp.where(live[:, None], own_projected, 0.0).astype(jnp.bfloat16)
     fold = mode_total // vec_width
     start_rows = lax.dynamic_slice_in_dim(init_vectors, core * SB, SB, 0).astype(jnp.bfloat16)
     start_rows = jnp.concatenate([start_rows[share * q : share * (q + 1)] for q in range(fold)], axis=1)
@@ -515,38 +539,31 @@
         perm = [(z * 2 + c, (z ^ distance) * 2 + c) for z in range(layers) for c in range(2)]
         return lax.ppermute(x, "sub", perm)
 
-    def spread_layers(rows):
+    def gather_half(rows, after):
         other = from_layer(rows, 4)
         upper = (layer & 4) > 0
         pair = jnp.stack([jnp.where(upper, other, rows), jnp.where(upper, rows, other)])
         pieces = [pair] + [from_layer(pair, distance) for distance in (1, 2, 3)]
-        odd, high = (layer & 1) > 0, (layer & 2) > 0
-        pieces = [jnp.where(odd, pieces[q ^ 1], pieces[q]) for q in range(4)]
-        pieces = [jnp.where(high, pieces[q ^ 2], pieces[q]) for q in range(4)]
-        return jnp.stack(pieces, axis=1).reshape(SB, vec_width)
-
-    def gather_half(part):
-        return gather_blocks(part, "sep").reshape(total_rows // 2, vec_width)
-
-    first_half = gather_half(spread_layers(first_rows))
+        spread = spread_rows((layer & 3)[None], pieces, after, sep_count)
+        whole = lax.all_to_all(spread, "sep", 0, 0, tiled=True)
+        return whole.reshape(total_rows // 2, vec_width), spread
+
+    first_half, _ = gather_half(first_rows, operator_half)
     both_rows = dot_f32(operator_half, first_half)
     second_rows = both_rows[:slim] + from_twin(both_rows[slim:])
-    second_part = spread_layers(second_rows)
-    raw_half = gather_half(second_part)
-
-    first_gram = gram_of(first_half, second_part)
+    raw_half, second_spread = gather_half(second_rows, second_rows)
+
+    first_gram = gram_of(first_half, second_spread)
     first_factor = inverse_transposed_factor(first_gram, from_twin(first_gram), scaling)
-
-    image_half, second_gram = image_and_gram(raw_half, first_factor)
-    sums = quotient_sums(first_half, first_factor, image_half, second_gram)
-    sums = sums + from_twin(sums)
-    quotient = sums[0] / sums[1]
+    iterate_half = iterate_of(first_half, first_factor)
+
+    image_half, second_sums = image_and_sums(raw_half, iterate_half, first_factor)
     wanted = jnp.concatenate([2 * sep_index + jnp.arange(2, dtype=jnp.int32), blocks])
-    separator_modes, interior = last_products(
+    separator_modes, quotient, interior = last_products(
         wanted >> 1,
         ((wanted & 1) == core).astype(jnp.int32),
-        second_gram,
-        from_twin(second_gram),
+        second_sums,
+        from_twin(second_sums),
         image_half,
         from_twin(image_half),
         mode_weight,
@@ -554,7 +571,7 @@
         shapes,
         scaling,
     )
-    return (separator_modes, quotient, interior[None])
+    return (separator_modes, quotient[0], interior[None])
 
 
 def solution(mesh):

time: 239 us -> 236 us (0.987)
  blocking collectives: 0 us -> 30.2 us
  waiting for transfers between devices: 93.6 us -> 70.7 us
  starting transfers between devices: 63.6 us -> 51.6 us
  local copies, waits for them, and re-layouts: 12.9 us -> 17.4 us
    all_to_all x0 -> x1, blocking collectives: none -> 30.2 us  [gather_half(): whole = lax.all_to_all(spread, 'sep', 0, 0, tiled=True)]
    all_to_all x3 -> x1, waiting for transfers between devices: 47.1 us -> 24.6 us  [gather_blocks(): return lax.all_to_all(spread, axis, 0, 0, tiled=True)]
    all_to_all x3 -> x1, starting transfers between devices: 13.6 us -> 4.57 us  [gather_blocks(): return lax.all_to_all(spread, axis, 0, 0, tiled=True)]
    ppermute x7 -> x6, starting transfers between devices: 24.3 us -> 17.1 us  [from_twin(): return lax.ppermute(x, 'sub', [(i, i ^ 1) for i in range(sub_count)])]
    unnamed x28 -> x49, local copies, waits for them, and re-layouts: 5.4 us -> 12.5 us
    all_to_all x1 -> x2, starting transfers between devices: 7.58 us -> 12.2 us  [the longest x1 7.72 us: per_device(): lax.all_to_all(partial.reshape(sep_count, share, mode_total), 'sep', 0, 0...]
    broadcast_in_dim x3 -> x1, local copies, waits for them, and re-layouts: 4.78 us -> 1.6 us  [gather_blocks(): spread = jnp.broadcast_to(x[None], (count,) + x.shape)]
    pallas_call x2 -> x4, Pallas kernels: 10.1 us -> 13.2 us  [the longest x1 6.79 us: image_and_sums(): pl.pallas_call(image_kernel, out_shape=(jax.ShapeDtypeStruct((rows, width...]
  transfers between devices with their start and end apart: 20 -> 18, of which waited for: 15 -> 13; matrix products, arithmetic and copies ran while one was open for 1% -> 2% of each run, Pallas kernels for 9% -> 7%
where the time goes in v2:
time: 236 us; the launch traced here: 235 us
  waiting for transfers between devices  70.7 us (30%)
  Pallas kernels  55.9 us (24%)
  starting transfers between devices  51.6 us (22%)
  blocking collectives  30.2 us (13%)
  local copies, waits for them, and re-layouts  17.4 us (7%)
  matrix products  6.6 us (3%)
    all_to_all x1, blocking collectives, gather_half(): whole = lax.all_to_all(spread, 'sep', 0, 0, tiled=True)  30.2 us
    all_to_all x1, waiting for transfers between devices, gather_blocks(): return lax.all_to_all(spread, axis, 0, 0, tiled=True)  24.6 us
    pallas_call x1, Pallas kernels, last_products(): pl.pallas_call(lambda *refs: last_kernel(scale, *refs), in_specs=[scalars...  21.3 us
    ppermute x6, starting transfers between devices, from_twin(): return lax.ppermute(x, 'sub', [(i, i ^ 1) for i in range(sub_count)])  17.1 us
    ppermute x8, waiting for transfers between devices, from_layer(): return lax.ppermute(x, 'sub', perm)  15.3 us
    pallas_call x1, Pallas kernels, inverse_transposed_factor(): pl.pallas_call(lambda *refs: factor_kernel(scale, *refs), out_shape=jax.S...  14.2 us
    all_to_all x1, waiting for transfers between devices, per_device(): lax.all_to_all(partial.reshape(sep_count, share, mode_total), 'sep', 0, 0...  13.3 us
    unnamed x49, local copies, waits for them, and re-layouts  12.5 us
  transfers between devices with their start and end apart: 18, of which 13 were waited for; matrix products, arithmetic and copies ran while one was open for 2% of the time, Pallas kernels for 7%

profile of v2, /device:TPU:1, one launch (start us, length us, event | category | flops | bytes accessed | tf_op | source)
XLA Modules:
  0.0 235.3 jit_solution(14871892036746002439)
XLA Ops:
  0.6 1.6 copy-done
  2.2 5.5 %fusion.2 = bf16[512,1024]{1,0:T(8,128)(2,1)} fusion(bf16[1,2048,512]{2,1,0:T(8,128)(2,1)S(1)} %copy-done, bf16[1,2048,1024]{2,1,0:T(8,128)(2,1)} %param.8), kind=kOutput, calls=%fused_computation.3 | convolution fusion | flops 2148007936 | bytes 7340032 | tf_op jit(solution)/shard_map/dot_general | solution.py:503
  7.7 7.7 %all-to-all-start = ((bf16[16,32,1024]{2,1,0:T(8,128)(2,1)}), bf16[16,32,1024]{2,1,0:T(8,128)(2,1)S(1)}, u32[]{:S(2)}, u32[]{:S(2)}) async-start(bf16[16,32,1024]{2,1,0:T(8,128)(2,1)} %bitcast.40), calls=%async_computation | async-start | bytes 2097152 | tf_op jit(solution)/shard_map/all_to_all | solution.py:507
  16.7 0.9 dynamic-slice_convert_fusion
  17.7 13.3 %all-to-all-done = bf16[16,32,1024]{2,1,0:T(8,128)(2,1)S(1)} async-done(((bf16[16,32,1024]{2,1,0:T(8,128)(2,1)}), bf16[16,32,1024]{2,1,0:T(8,128)(2,1)S(1)}, u32[]{:S(2)}, u32[]{:S(2)}) %all-to-all-start) | async-done | bytes 1048608 | tf_op jit(solution)/shard_map/all_to_all | solution.py:507
  31.2 1.6 broadcast_in_dim.42
  32.8 4.6 %all-to-all-start.1 = ((bf16[16,64,1024]{2,1,0:T(8,128)(2,1)}), bf16[16,64,1024]{2,1,0:T(8,128)(2,1)}, u32[]{:S(2)}, u32[]{:S(2)}) async-start(bf16[16,64,1024]{2,1,0:T(8,128)(2,1)} %broadcast_in_dim.42), calls=%async_computation.1 | async-start | bytes 4194304 | tf_op jit(solution)/shard_map/all_to_all | solution.py:480
  38.1 24.6 %all-to-all-done.1.gathered_ref.refs_7_ = bf16[16,64,1024]{2,1,0:T(8,128)(2,1)} async-done(((bf16[16,64,1024]{2,1,0:T(8,128)(2,1)}), bf16[16,64,1024]{2,1,0:T(8,128)(2,1)}, u32[]{:S(2)}, u32[]{:S(2)}) %all-to-all-start.1) | async-done | bytes 2097184 | tf_op jit(solution)/shard_map/all_to_all | solution.py:480
  62.7 3.8 %rows.1 = (bf16[16,16,640]{2,1,0:T(8,128)(2,1)S(1)}, bf16[16,128,256]{2,1,0:T(8,128)(2,1)S(1)}) custom-call(s32[4]{0:T(128)S(1)} %bitcast.36, s32[1]{0:T(128)} %bitcast.2.first_ref, f32[1,1024]{1,0:T(1,128)S(1)} %compare_select_fusion.weight_ref.refs_6_, bf16[16,64,1024]{2,1,0:T(8,128)(2,1)} %all-to-all-done.1.gathered_ref.refs_7_), custom_call_target="tpu_custom_call" | custom-call | flops 800000000 | bytes 2700000 | tf_op jit(solution)/shard_map/rows/pallas_call | solution.py:314
  66.5 0.7 copy-done.6
  67.2 5.7 %collective-permute-start = (bf16[2048,256]{1,0:T(8,128)(2,1)S(1)}, bf16[2048,256]{1,0:T(8,128)(2,1)}, u32[]{:S(2)}, u32[]{:S(2)}) collective-permute-start(bf16[2048,256]{1,0:T(8,128)(2,1)S(1)} %bitcast.34), channel_id=1, source_target_pairs={{0,16},{16,0},{32,48},{48,32},{64,80},{80,64},{96,112},{112,96},{1... | collective-permute-start | bytes 3145736 | tf_op jit(solution)/shard_map/ppermute | solution.py:500
  72.9 8.6 %all-to-all-start.2 = ((bf16[16,16,640]{2,1,0:T(8,128)(2,1)}), bf16[16,16,640]{2,1,0:T(8,128)(2,1)S(1)}, u32[]{:S(2)}, u32[]{:S(2)}) async-start(bf16[16,16,640]{2,1,0:T(8,128)(2,1)} %copy-done.6), calls=%async_computation.2 | async-start | bytes 655360 | tf_op jit(solution)/shard_map/all_to_all | solution.py:528
  81.5 1.7 constant_dynamic-slice_fusion.flex_ref
  83.2 11.4 %all-to-all-done.2.incoming_ref = bf16[16,16,640]{2,1,0:T(8,128)(2,1)S(1)} async-done(((bf16[16,16,640]{2,1,0:T(8,128)(2,1)}), bf16[16,16,640]{2,1,0:T(8,128)(2,1)S(1)}, u32[]{:S(2)}, u32[]{:S(2)}) %all-to-all-start.2) | async-done | bytes 327712 | tf_op jit(solution)/shard_map/all_to_all | solution.py:528
  94.7 0.9 copy-done.5
  95.7 2.0 build.1
  97.7 1.0 collective-permute-start.2
  98.7 0.8 collective-permute-start.1
  99.4 5.0 %collective-permute-done.2 = f32[16,256]{1,0:T(8,128)S(1)} collective-permute-done((f32[16,256]{1,0:T(8,128)S(1)}, f32[16,256]{1,0:T(8,128)S(1)}, u32[]{:S(2)}, u32[]{:S(2)}) %collective-permute-start.2) | collective-permute-done | bytes 16416 | tf_op jit(solution)/shard_map/ppermute | solution.py:540
  105.2 2.9 %collective-permute-start.3 = (f32[2,16,256]{2,1,0:T(8,128)S(1)}, f32[2,16,256]{2,1,0:T(8,128)S(1)}, u32[]{:S(2)}, u32[]{:S(2)}) collective-permute-start(f32[2,16,256]{2,1,0:T(8,128)S(1)} %pad_maximum_fusion.own_ref), channel_id=1, source_target_pairs={{0,32},{16,48},{32,0},{48,16},{64,96},{80,112},{96,64},{112,80},{1... | collective-permute-start | bytes 98312 | tf_op jit(solution)/shard_map/ppermute | solution.py:540
  108.1 1.1 collective-permute-done.5.three_ref
  110.4 2.3 spread.2
  112.7 30.2 %all_to_all.25 = f32[16,128,256]{2,1,0:T(8,128)S(1)} all-to-all(f32[16,128,256]{2,1,0:T(8,128)} %spread.2), channel_id=1, replica_groups=mesh['sub'=16,'sep'=16] {'sep'}, dimensions={0} | all-to-all | bytes 4194304 | tf_op jit(solution)/shard_map/all_to_all | solution.py:548
  142.9 1.1 fusion.8
  144.1 1.3 copy-done.1
  145.4 3.0 %collective-permute-start.6 = (f32[16,256]{1,0:T(8,128)S(1)}, f32[16,256]{1,0:T(8,128)S(1)}, u32[]{:S(2)}, u32[]{:S(2)}) collective-permute-start(f32[16,256]{1,0:T(8,128)S(1)} %slice.34), channel_id=1, source_target_pairs={{0,16},{16,0},{32,48},{48,32},{64,80},{80,64},{96,112},{112,96},{1... | collective-permute-start | bytes 49160 | tf_op jit(solution)/shard_map/ppermute | solution.py:500
  148.4 0.8 collective-permute-done.6
  149.3 0.9 collective-permute-start.7
  150.1 5.6 %collective-permute-done.7 = f32[16,256]{1,0:T(8,128)S(1)} collective-permute-done((f32[16,256]{1,0:T(8,128)S(1)}, f32[16,256]{1,0:T(8,128)S(1)}, u32[]{:S(2)}, u32[]{:S(2)}) %collective-permute-start.7) | collective-permute-done | bytes 16416 | tf_op jit(solution)/shard_map/ppermute | solution.py:540
  155.8 2.3 collective-permute-start.10
  158.5 0.9 collective-permute-start.8
  159.4 1.0 collective-permute-done.10.three_ref
  160.4 1.9 collective-permute-done.9.two_ref
  163.6 2.3 spread.3.after_ref
  165.9 4.4 %all-to-all-start.4 = ((f32[16,128,256]{2,1,0:T(8,128)}), f32[16,128,256]{2,1,0:T(8,128)}, u32[]{:S(2)}, u32[]{:S(2)}) async-start(f32[16,128,256]{2,1,0:T(8,128)} %spread.3.after_ref), calls=%async_computation.4 | async-start | bytes 4194304 | tf_op jit(solution)/shard_map/all_to_all | solution.py:548
  170.4 1.6 copy-done.2
  172.0 1.6 copy-done.4
  173.6 1.3 gram.1.refs_0_
  174.9 2.4 %collective-permute-start.11 = (f32[256,256]{1,0:T(8,128)S(1)}, f32[256,256]{1,0:T(8,128)S(1)}, u32[]{:S(2)}, u32[]{:S(2)}) collective-permute-start(f32[256,256]{1,0:T(8,128)S(1)} %gram.1.refs_0_), channel_id=1, source_target_pairs={{0,16},{16,0},{32,48},{48,32},{64,80},{80,64},{96,112},{112,96},{1... | collective-permute-start | bytes 786440 | tf_op jit(solution)/shard_map/ppermute | solution.py:500
  177.3 1.2 collective-permute-done.11.refs_1_
  178.5 14.2 %factor.1.factor_ref = f32[256,256]{1,0:T(8,128)S(1)} custom-call(f32[256,256]{1,0:T(8,128)S(1)} %gram.1.refs_0_, f32[256,256]{1,0:T(8,128)S(1)} %collective-permute-done.11.refs_1_), custom_call_target="tpu_custom_call" | custom-call | flops 12000000000 | bytes 800000 | tf_op jit(solution)/shard_map/factor/pallas_call | solution.py:132
  192.6 1.8 iterate.1.iterate_ref
  194.5 1.3 copy-done.9
  196.0 1.6 copy-done.10
  197.6 6.8 %image.1 = (f32[2048,256]{1,0:T(8,128)S(1)}, f32[264,256]{1,0:T(8,128)S(1)}) custom-call(f32[2048,256]{1,0:T(8,128)} %bitcast.15.raw_ref, f32[2048,256]{1,0:T(8,128)S(1)} %copy-done.10, f32[256,256]{1,0:T(8,128)S(1)} %factor.1.factor_ref), custom_call_target="tpu_custom_call" | custom-call | flops 3000000000 | bytes 7000000 | tf_op jit(solution)/shard_map/image/pallas_call | solution.py:220
  204.4 5.2 %collective-permute-start.13 = (f32[2048,256]{1,0:T(8,128)S(1)}, f32[2048,256]{1,0:T(8,128)S(1)}, u32[]{:S(2)}, u32[]{:S(2)}) collective-permute-start(f32[2048,256]{1,0:T(8,128)S(1)} %get-tuple-element.19.refs_4_), channel_id=1, source_target_pairs={{0,16},{16,0},{32,48},{48,32},{64,80},{80,64},{96,112},{112,96},{1... | collective-permute-start | bytes 6291464 | tf_op jit(solution)/shard_map/ppermute | solution.py:500
  209.8 3.9 %collective-permute-done.12.refs_3_ = f32[264,256]{1,0:T(8,128)S(1)} collective-permute-done((f32[264,256]{1,0:T(8,128)S(1)}, f32[264,256]{1,0:T(8,128)S(1)}, u32[]{:S(2)}, u32[]{:S(2)}) %collective-permute-start.12) | collective-permute-done | bytes 270368 | tf_op jit(solution)/shard_map/ppermute | solution.py:500
  213.7 21.3 %last.1 = (f32[256,256]{1,0:T(8,128)}, f32[1,256]{1,0:T(1,128)}, bf16[2048,256]{1,0:T(8,128)(2,1)}) custom-call(s32[6]{0:T(128)S(1)} %broadcast_shift-right-arithmetic_fusion.refs_0_, s32[6]{0:T(128)S(1)} %compare_convert_fusion.refs_1_, f32[264,256]{1,0:T(8,128)S(1)} %get-tuple-element.18.refs_2_, f32[264,256]{1,0:T(8,128)S(1)} %collective-permute-done.12.refs_3_, ...), custom_call_target="tpu_custom_call" | custom-call | flops 16000000000 | bytes 8000000 | tf_op jit(solution)/shard_map/last/pallas_call | solution.py:447
  (71 shorter events, 5.8 us)
Async XLA Ops:
  0.6 1.6 copy-start
  7.7 7.8 %copy-start.23 = (s32[1,4]{1,0:T(1,128)S(1)}, s32[1,4]{1,0:T(1,128)}, u32[]{:S(2)}) copy-start(s32[1,4]{1,0:T(1,128)} %param.13) | copy-start | bytes 52
  7.7 23.2 %all-to-all-start = ((bf16[16,32,1024]{2,1,0:T(8,128)(2,1)}), bf16[16,32,1024]{2,1,0:T(8,128)(2,1)S(1)}, u32[]{:S(2)}, u32[]{:S(2)}) async-start(bf16[16,32,1024]{2,1,0:T(8,128)(2,1)} %bitcast.40), calls=%async_computation | async-start | bytes 2097152 | tf_op jit(solution)/shard_map/all_to_all | solution.py:507
  32.8 5.2 %copy-start.22 = (f32[1,1024]{1,0:T(1,128)S(1)}, f32[1,1024]{1,0:T(1,128)}, u32[]{:S(2)}) copy-start(f32[1,1024]{1,0:T(1,128)} %param.10) | copy-start | bytes 12292
  32.8 29.8 %copy-start.7 = (s32[1,4]{1,0:T(1,128)S(1)}, s32[1,4]{1,0:T(1,128)}, u32[]{:S(2)}) copy-start(s32[1,4]{1,0:T(1,128)} %param.12) | copy-start | bytes 52
  32.8 29.8 %all-to-all-start.1 = ((bf16[16,64,1024]{2,1,0:T(8,128)(2,1)}), bf16[16,64,1024]{2,1,0:T(8,128)(2,1)}, u32[]{:S(2)}, u32[]{:S(2)}) async-start(bf16[16,64,1024]{2,1,0:T(8,128)(2,1)} %broadcast_in_dim.42), calls=%async_computation.1 | async-start | bytes 4194304 | tf_op jit(solution)/shard_map/all_to_all | solution.py:480
  66.5 0.7 copy-start.6
  67.2 27.5 %collective-permute-start = (bf16[2048,256]{1,0:T(8,128)(2,1)S(1)}, bf16[2048,256]{1,0:T(8,128)(2,1)}, u32[]{:S(2)}, u32[]{:S(2)}) collective-permute-start(bf16[2048,256]{1,0:T(8,128)(2,1)S(1)} %bitcast.34), channel_id=1, source_target_pairs={{0,16},{16,0},{32,48},{48,32},{64,80},{80,64},{96,112},{112,96},{1... | collective-permute-start | bytes 3145736 | tf_op jit(solution)/shard_map/ppermute | solution.py:500
  72.9 21.7 %all-to-all-start.2 = ((bf16[16,16,640]{2,1,0:T(8,128)(2,1)}), bf16[16,16,640]{2,1,0:T(8,128)(2,1)S(1)}, u32[]{:S(2)}, u32[]{:S(2)}) async-start(bf16[16,16,640]{2,1,0:T(8,128)(2,1)} %copy-done.6), calls=%async_computation.2 | async-start | bytes 655360 | tf_op jit(solution)/shard_map/all_to_all | solution.py:528
  94.7 1.0 copy-start.5
  97.7 6.8 %collective-permute-start.2 = (f32[16,256]{1,0:T(8,128)S(1)}, f32[16,256]{1,0:T(8,128)S(1)}, u32[]{:S(2)}, u32[]{:S(2)}) collective-permute-start(f32[16,256]{1,0:T(8,128)S(1)} %get-tuple-element.17), channel_id=1, source_target_pairs={{0,128},{16,144},{32,160},{48,176},{64,192},{80,208},{96,224},{112... | collective-permute-start | bytes 49160 | tf_op jit(solution)/shard_map/ppermute | solution.py:540
  98.7 9.4 %collective-permute-start.1 = (f32[16,2048]{1,0:T(8,128)S(1)}, f32[16,2048]{1,0:T(8,128)S(1)}, u32[]{:S(2)}, u32[]{:S(2)}) collective-permute-start(f32[16,2048]{1,0:T(8,128)S(1)} %get-tuple-element.16), channel_id=1, source_target_pairs={{0,16},{16,0},{32,48},{48,32},{64,80},{80,64},{96,112},{112,96},{1... | collective-permute-start | bytes 393224 | tf_op jit(solution)/shard_map/ppermute | solution.py:500
  104.4 5.4 %copy-start.14 = (f32[2,16,256]{2,1,0:T(8,128)}, f32[2,16,256]{2,1,0:T(8,128)S(1)}, u32[]{:S(2)}) copy-start(f32[2,16,256]{2,1,0:T(8,128)S(1)} %pad_maximum_fusion.own_ref) | copy-start | bytes 98308
  104.4 4.7 %collective-permute-start.5 = (f32[2,16,256]{2,1,0:T(8,128)S(1)}, f32[2,16,256]{2,1,0:T(8,128)S(1)}, u32[]{:S(2)}, u32[]{:S(2)}) collective-permute-start(f32[2,16,256]{2,1,0:T(8,128)S(1)} %pad_maximum_fusion.own_ref), channel_id=1, source_target_pairs={{0,96},{16,112},{32,64},{48,80},{64,32},{80,48},{96,0},{112,16},{1... | collective-permute-start | bytes 98312 | tf_op jit(solution)/shard_map/ppermute | solution.py:540
  105.2 4.0 %collective-permute-start.4 = (f32[2,16,256]{2,1,0:T(8,128)S(1)}, f32[2,16,256]{2,1,0:T(8,128)S(1)}, u32[]{:S(2)}, u32[]{:S(2)}) collective-permute-start(f32[2,16,256]{2,1,0:T(8,128)S(1)} %pad_maximum_fusion.own_ref), channel_id=1, source_target_pairs={{0,64},{16,80},{32,96},{48,112},{64,0},{80,16},{96,32},{112,48},{1... | collective-permute-start | bytes 98312 | tf_op jit(solution)/shard_map/ppermute | solution.py:540
  105.2 4.7 %collective-permute-start.3 = (f32[2,16,256]{2,1,0:T(8,128)S(1)}, f32[2,16,256]{2,1,0:T(8,128)S(1)}, u32[]{:S(2)}, u32[]{:S(2)}) collective-permute-start(f32[2,16,256]{2,1,0:T(8,128)S(1)} %pad_maximum_fusion.own_ref), channel_id=1, source_target_pairs={{0,32},{16,48},{32,0},{48,16},{64,96},{80,112},{96,64},{112,80},{1... | collective-permute-start | bytes 98312 | tf_op jit(solution)/shard_map/ppermute | solution.py:540
  108.1 1.7 copy-start.11
  109.2 0.6 copy-start.16
  109.2 0.6 copy-start.17
  109.8 0.6 copy-start.19
  112.7 30.2 %copy-start.12 = (f32[32,2048]{1,0:T(8,128)S(1)}, f32[32,2048]{1,0:T(8,128)}, u32[]{:S(2)}) copy-start(f32[32,2048]{1,0:T(8,128)} %copy-done.11) | copy-start | bytes 786436
  144.0 1.3 copy-start.1
  145.4 3.9 %collective-permute-start.6 = (f32[16,256]{1,0:T(8,128)S(1)}, f32[16,256]{1,0:T(8,128)S(1)}, u32[]{:S(2)}, u32[]{:S(2)}) collective-permute-start(f32[16,256]{1,0:T(8,128)S(1)} %slice.34), channel_id=1, source_target_pairs={{0,16},{16,0},{32,48},{48,32},{64,80},{80,64},{96,112},{112,96},{1... | collective-permute-start | bytes 49160 | tf_op jit(solution)/shard_map/ppermute | solution.py:500
  149.3 13.1 %copy-start.13 = (f32[16,256]{1,0:T(8,128)}, f32[16,256]{1,0:T(8,128)S(1)}, u32[]{:S(2)}) copy-start(f32[16,256]{1,0:T(8,128)S(1)} %slice_add_fusion.after_ref) | copy-start | bytes 49156
  149.3 6.5 %collective-permute-start.7 = (f32[16,256]{1,0:T(8,128)S(1)}, f32[16,256]{1,0:T(8,128)S(1)}, u32[]{:S(2)}, u32[]{:S(2)}) collective-permute-start(f32[16,256]{1,0:T(8,128)S(1)} %slice_add_fusion.after_ref), channel_id=1, source_target_pairs={{0,128},{16,144},{32,160},{48,176},{64,192},{80,208},{96,224},{112... | collective-permute-start | bytes 49160 | tf_op jit(solution)/shard_map/ppermute | solution.py:540
  155.8 6.6 %copy-start.15 = (f32[2,16,256]{2,1,0:T(8,128)}, f32[2,16,256]{2,1,0:T(8,128)S(1)}, u32[]{:S(2)}) copy-start(f32[2,16,256]{2,1,0:T(8,128)S(1)} %pad_maximum_fusion.1.own_ref) | copy-start | bytes 98308
  155.8 4.7 %collective-permute-start.10 = (f32[2,16,256]{2,1,0:T(8,128)S(1)}, f32[2,16,256]{2,1,0:T(8,128)S(1)}, u32[]{:S(2)}, u32[]{:S(2)}) collective-permute-start(f32[2,16,256]{2,1,0:T(8,128)S(1)} %pad_maximum_fusion.1.own_ref), channel_id=1, source_target_pairs={{0,96},{16,112},{32,64},{48,80},{64,32},{80,48},{96,0},{112,16},{1... | collective-permute-start | bytes 98312 | tf_op jit(solution)/shard_map/ppermute | solution.py:540
  158.1 4.3 %collective-permute-start.9 = (f32[2,16,256]{2,1,0:T(8,128)S(1)}, f32[2,16,256]{2,1,0:T(8,128)S(1)}, u32[]{:S(2)}, u32[]{:S(2)}) collective-permute-start(f32[2,16,256]{2,1,0:T(8,128)S(1)} %pad_maximum_fusion.1.own_ref), channel_id=1, source_target_pairs={{0,64},{16,80},{32,96},{48,112},{64,0},{80,16},{96,32},{112,48},{1... | collective-permute-start | bytes 98312 | tf_op jit(solution)/shard_map/ppermute | solution.py:540
  158.5 3.9 %collective-permute-start.8 = (f32[2,16,256]{2,1,0:T(8,128)S(1)}, f32[2,16,256]{2,1,0:T(8,128)S(1)}, u32[]{:S(2)}, u32[]{:S(2)}) collective-permute-start(f32[2,16,256]{2,1,0:T(8,128)S(1)} %pad_maximum_fusion.1.own_ref), channel_id=1, source_target_pairs={{0,32},{16,48},{32,0},{48,16},{64,96},{80,112},{96,64},{112,80},{1... | collective-permute-start | bytes 98312 | tf_op jit(solution)/shard_map/ppermute | solution.py:540
  160.4 2.0 copy-start.18
  162.4 0.6 copy-start.20
  163.0 0.6 copy-start.21
  165.9 30.1 %all-to-all-start.4 = ((f32[16,128,256]{2,1,0:T(8,128)}), f32[16,128,256]{2,1,0:T(8,128)}, u32[]{:S(2)}, u32[]{:S(2)}) async-start(f32[16,128,256]{2,1,0:T(8,128)} %spread.3.after_ref), calls=%async_computation.4 | async-start | bytes 4194304 | tf_op jit(solution)/shard_map/all_to_all | solution.py:548
  170.4 1.6 copy-start.2
  172.0 1.6 copy-start.4
  174.9 17.7 %copy-start.3 = (f32[16,128,256]{2,1,0:T(8,128)S(1)}, f32[16,128,256]{2,1,0:T(8,128)}, u32[]{:S(2)}) copy-start(f32[16,128,256]{2,1,0:T(8,128)} %copy-done.1) | copy-start | bytes 6291460
  174.9 3.6 %collective-permute-start.11 = (f32[256,256]{1,0:T(8,128)S(1)}, f32[256,256]{1,0:T(8,128)S(1)}, u32[]{:S(2)}, u32[]{:S(2)}) collective-permute-start(f32[256,256]{1,0:T(8,128)S(1)} %gram.1.refs_0_), channel_id=1, source_target_pairs={{0,16},{16,0},{32,48},{48,32},{64,80},{80,64},{96,112},{112,96},{1... | collective-permute-start | bytes 786440 | tf_op jit(solution)/shard_map/ppermute | solution.py:500
  194.4 1.3 copy-start.9
  196.0 1.6 copy-start.10
  197.6 16.1 %copy-start.8 = (bf16[1,2048,1024]{2,1,0:T(8,128)(2,1)S(1)}, bf16[1,2048,1024]{2,1,0:T(8,128)(2,1)}, u32[]{:S(2)}) copy-start(bf16[1,2048,1024]{2,1,0:T(8,128)(2,1)} %param.8) | copy-start | bytes 12582916
  204.4 9.3 %collective-permute-start.13 = (f32[2048,256]{1,0:T(8,128)S(1)}, f32[2048,256]{1,0:T(8,128)S(1)}, u32[]{:S(2)}, u32[]{:S(2)}) collective-permute-start(f32[2048,256]{1,0:T(8,128)S(1)} %get-tuple-element.19.refs_4_), channel_id=1, source_target_pairs={{0,16},{16,0},{32,48},{48,32},{64,80},{80,64},{96,112},{112,96},{1... | collective-permute-start | bytes 6291464 | tf_op jit(solution)/shard_map/ppermute | solution.py:500
  209.6 4.2 %collective-permute-start.12 = (f32[264,256]{1,0:T(8,128)S(1)}, f32[264,256]{1,0:T(8,128)S(1)}, u32[]{:S(2)}, u32[]{:S(2)}) collective-permute-start(f32[264,256]{1,0:T(8,128)S(1)} %get-tuple-element.18.refs_2_), channel_id=1, source_target_pairs={{0,16},{16,0},{32,48},{48,32},{64,80},{80,64},{96,112},{112,96},{1... | collective-permute-start | bytes 811016 | tf_op jit(solution)/shard_map/ppermute | solution.py:500

commit v3 on v2

--- a/solution.py
+++ b/solution.py
@@ -201,12 +201,17 @@
     )(first, factor)
 
 
-def image_kernel(raw_ref, iterate_ref, factor_ref, image_ref, out_ref, even_ref, odd_ref):
+def image_kernel(
+    place_ref, raw_ref, iterate_ref, factor_ref, image_ref, picks_ref, out_ref, even_ref, odd_ref
+):
     width = even_ref.shape[0]
     even_ref[...] = jnp.zeros_like(even_ref)
     odd_ref[...] = jnp.zeros_like(odd_ref)
     image = dot_f32(raw_ref[...], factor_ref[...])
     image_ref[...] = image
+    for k in range(1 + KB):
+        source = pl.ds(pl.multiple_of(place_ref[k] * SB, SB), SB)
+        picks_ref[k * SB : (k + 1) * SB, :] = image_ref[source, :]
     gram_step(image, even_ref, odd_ref)
     iterate = iterate_ref[...]
     out_ref[width:, :] = jnp.zeros((out_ref.shape[0] - width, width), jnp.float32)
@@ -215,23 +220,24 @@
     out_ref[:width, :] = even_ref[...] + odd_ref[...] + odd_ref[...].T
 
 
-def image_and_sums(raw, iterate, factor):
+def image_and_sums(place, raw, iterate, factor):
     rows, width = raw.shape
     return pl.pallas_call(
         image_kernel,
         out_shape=(
             jax.ShapeDtypeStruct((rows, width), jnp.float32),
+            jax.ShapeDtypeStruct(((1 + KB) * SB, width), jnp.float32),
             jax.ShapeDtypeStruct((width + 8, width), jnp.float32),
         ),
-        in_specs=[WHOLE, WHOLE, WHOLE],
-        out_specs=(WHOLE, WHOLE),
+        in_specs=[pl.BlockSpec(memory_space=pltpu.SMEM), WHOLE, WHOLE, WHOLE],
+        out_specs=(WHOLE, WHOLE, WHOLE),
         scratch_shapes=[pltpu.VMEM((width, width), jnp.float32)] * 2,
         compiler_params=pltpu.CompilerParams(vmem_limit_bytes=VMEM_BYTES),
         cost_estimate=pl.CostEstimate(
             flops=3_000_000_000, bytes_accessed=7_000_000, transcendentals=0
         ),
         name="image",
-    )(raw, iterate, factor)
+    )(place, raw, iterate, factor)
 
 
 def spread_kernel(low_ref, own_ref, one_ref, two_ref, three_ref, after_ref, out_ref, part_ref, sems):
@@ -402,7 +408,8 @@
 
         @pl.when(here_ref[k] != 1)
         def _():
-            pltpu.make_async_copy(twin_ref.at[source, :], target, image_sems.at[k]).start()
+            picked = pl.ds((0 if k < 2 else k - 1) * SB, SB)
+            pltpu.make_async_copy(twin_ref.at[picked, :], target, image_sems.at[k]).start()
 
     load_modes.start()
     load_dofs.start()
@@ -557,7 +564,10 @@
     first_factor = inverse_transposed_factor(first_gram, from_twin(first_gram), scaling)
     iterate_half = iterate_of(first_half, first_factor)
 
-    image_half, second_sums = image_and_sums(raw_half, iterate_half, first_factor)
+    twin_blocks = lax.dynamic_slice_in_dim(map_all, (sub_index ^ 1) * KB, KB, 0)
+    image_half, picks, second_sums = image_and_sums(
+        jnp.concatenate([sep_index[None], twin_blocks >> 1]), raw_half, iterate_half, first_factor
+    )
     wanted = jnp.concatenate([2 * sep_index + jnp.arange(2, dtype=jnp.int32), blocks])
     separator_modes, quotient, interior = last_products(
         wanted >> 1,
@@ -565,7 +575,7 @@
         second_sums,
         from_twin(second_sums),
         image_half,
-        from_twin(image_half),
+        from_twin(picks),
         mode_weight,
         gathered,
         shapes,

time: 236 us -> 234 us (level)
  waiting for transfers between devices: 70.7 us -> 67.8 us
  transfers between devices with their start and end apart: 18 -> 18, of which waited for: 13 -> 12; matrix products, arithmetic and copies ran while one was open for 2% -> 2% of each run, Pallas kernels for 7% -> 7%
where the time goes in v3:
time: 234 us; the launch traced here: 233 us
  waiting for transfers between devices  67.8 us (29%)
  Pallas kernels  55.8 us (24%)
  starting transfers between devices  51.8 us (22%)
  blocking collectives  30.2 us (13%)
  local copies, waits for them, and re-layouts  17.4 us (7%)
  matrix products  6.6 us (3%)
    all_to_all x1, blocking collectives, gather_half(): whole = lax.all_to_all(spread, 'sep', 0, 0, tiled=True)  30.2 us
    all_to_all x1, waiting for transfers between devices, gather_blocks(): return lax.all_to_all(spread, axis, 0, 0, tiled=True)  24.6 us
    pallas_call x1, Pallas kernels, last_products(): pl.pallas_call(lambda *refs: last_kernel(scale, *refs), in_specs=[scalars...  21.3 us
    ppermute x6, starting transfers between devices, from_twin(): return lax.ppermute(x, 'sub', [(i, i ^ 1) for i in range(sub_count)])  17.4 us
    ppermute x8, waiting for transfers between devices, from_layer(): return lax.ppermute(x, 'sub', perm)  14.8 us
    pallas_call x1, Pallas kernels, inverse_transposed_factor(): pl.pallas_call(lambda *refs: factor_kernel(scale, *refs), out_shape=jax.S...  14.2 us
    all_to_all x1, waiting for transfers between devices, per_device(): lax.all_to_all(partial.reshape(sep_count, share, mode_total), 'sep', 0, 0...  13.3 us
    unnamed x49, local copies, waits for them, and re-layouts  12.5 us
  transfers between devices with their start and end apart: 18, of which 12 were waited for; matrix products, arithmetic and copies ran while one was open for 2% of the time, Pallas kernels for 7%

profile of v3, /device:TPU:1, one launch (start us, length us, event | category | flops | bytes accessed | tf_op | source)
XLA Modules:
  0.0 232.7 jit_solution(2189674016915072364)
XLA Ops:
  0.6 1.6 copy-done
  2.2 5.5 %fusion.2 = bf16[512,1024]{1,0:T(8,128)(2,1)} fusion(bf16[1,2048,512]{2,1,0:T(8,128)(2,1)S(1)} %copy-done, bf16[1,2048,1024]{2,1,0:T(8,128)(2,1)} %param.8), kind=kOutput, calls=%fused_computation.3 | convolution fusion | flops 2148007936 | bytes 7340032 | tf_op jit(solution)/shard_map/dot_general | solution.py:510
  7.7 7.7 %all-to-all-start = ((bf16[16,32,1024]{2,1,0:T(8,128)(2,1)}), bf16[16,32,1024]{2,1,0:T(8,128)(2,1)S(1)}, u32[]{:S(2)}, u32[]{:S(2)}) async-start(bf16[16,32,1024]{2,1,0:T(8,128)(2,1)} %bitcast.41), calls=%async_computation | async-start | bytes 2097152 | tf_op jit(solution)/shard_map/all_to_all | solution.py:514
  16.7 0.9 dynamic-slice_convert_fusion
  17.7 13.3 %all-to-all-done = bf16[16,32,1024]{2,1,0:T(8,128)(2,1)S(1)} async-done(((bf16[16,32,1024]{2,1,0:T(8,128)(2,1)}), bf16[16,32,1024]{2,1,0:T(8,128)(2,1)S(1)}, u32[]{:S(2)}, u32[]{:S(2)}) %all-to-all-start) | async-done | bytes 1048608 | tf_op jit(solution)/shard_map/all_to_all | solution.py:514
  31.2 1.6 broadcast_in_dim.45
  32.8 4.6 %all-to-all-start.1 = ((bf16[16,64,1024]{2,1,0:T(8,128)(2,1)}), bf16[16,64,1024]{2,1,0:T(8,128)(2,1)}, u32[]{:S(2)}, u32[]{:S(2)}) async-start(bf16[16,64,1024]{2,1,0:T(8,128)(2,1)} %broadcast_in_dim.45), calls=%async_computation.1 | async-start | bytes 4194304 | tf_op jit(solution)/shard_map/all_to_all | solution.py:487
  38.1 24.6 %all-to-all-done.1.gathered_ref.refs_7_ = bf16[16,64,1024]{2,1,0:T(8,128)(2,1)} async-done(((bf16[16,64,1024]{2,1,0:T(8,128)(2,1)}), bf16[16,64,1024]{2,1,0:T(8,128)(2,1)}, u32[]{:S(2)}, u32[]{:S(2)}) %all-to-all-start.1) | async-done | bytes 2097184 | tf_op jit(solution)/shard_map/all_to_all | solution.py:487
  62.7 3.8 %rows.1 = (bf16[16,16,640]{2,1,0:T(8,128)(2,1)S(1)}, bf16[16,128,256]{2,1,0:T(8,128)(2,1)S(1)}) custom-call(s32[4]{0:T(128)S(1)} %bitcast.37, s32[1]{0:T(128)} %bitcast.2.first_ref, f32[1,1024]{1,0:T(1,128)S(1)} %compare_select_fusion.weight_ref.refs_6_, bf16[16,64,1024]{2,1,0:T(8,128)(2,1)} %all-to-all-done.1.gathered_ref.refs_7_), custom_call_target="tpu_custom_call" | custom-call | flops 800000000 | bytes 2700000 | tf_op jit(solution)/shard_map/rows/pallas_call | solution.py:320
  67.2 5.7 %collective-permute-start = (bf16[2048,256]{1,0:T(8,128)(2,1)S(1)}, bf16[2048,256]{1,0:T(8,128)(2,1)}, u32[]{:S(2)}, u32[]{:S(2)}) collective-permute-start(bf16[2048,256]{1,0:T(8,128)(2,1)S(1)} %bitcast.35), channel_id=1, source_target_pairs={{0,16},{16,0},{32,48},{48,32},{64,80},{80,64},{96,112},{112,96},{1... | collective-permute-start | bytes 3145736 | tf_op jit(solution)/shard_map/ppermute | solution.py:507
  72.9 8.6 %all-to-all-start.2 = ((bf16[16,16,640]{2,1,0:T(8,128)(2,1)}), bf16[16,16,640]{2,1,0:T(8,128)(2,1)S(1)}, u32[]{:S(2)}, u32[]{:S(2)}) async-start(bf16[16,16,640]{2,1,0:T(8,128)(2,1)} %copy-done.6), calls=%async_computation.2 | async-start | bytes 655360 | tf_op jit(solution)/shard_map/all_to_all | solution.py:535
  81.5 1.7 constant_dynamic-slice_fusion.flex_ref
  83.2 11.4 %all-to-all-done.2.incoming_ref = bf16[16,16,640]{2,1,0:T(8,128)(2,1)S(1)} async-done(((bf16[16,16,640]{2,1,0:T(8,128)(2,1)}), bf16[16,16,640]{2,1,0:T(8,128)(2,1)S(1)}, u32[]{:S(2)}, u32[]{:S(2)}) %all-to-all-start.2) | async-done | bytes 327712 | tf_op jit(solution)/shard_map/all_to_all | solution.py:535
  94.7 0.9 copy-done.5
  95.7 2.0 build.1
  97.7 1.0 collective-permute-start.2
  98.7 0.8 collective-permute-start.1
  99.5 5.0 %collective-permute-done.2 = f32[16,256]{1,0:T(8,128)S(1)} collective-permute-done((f32[16,256]{1,0:T(8,128)S(1)}, f32[16,256]{1,0:T(8,128)S(1)}, u32[]{:S(2)}, u32[]{:S(2)}) %collective-permute-start.2) | collective-permute-done | bytes 16416 | tf_op jit(solution)/shard_map/ppermute | solution.py:547
  104.5 0.7 collective-permute-start.5
  105.2 2.9 %collective-permute-start.3 = (f32[2,16,256]{2,1,0:T(8,128)S(1)}, f32[2,16,256]{2,1,0:T(8,128)S(1)}, u32[]{:S(2)}, u32[]{:S(2)}) collective-permute-start(f32[2,16,256]{2,1,0:T(8,128)S(1)} %pad_maximum_fusion.own_ref), channel_id=1, source_target_pairs={{0,32},{16,48},{32,0},{48,16},{64,96},{80,112},{96,64},{112,80},{1... | collective-permute-start | bytes 98312 | tf_op jit(solution)/shard_map/ppermute | solution.py:547
  108.1 1.1 collective-permute-done.5.three_ref
  110.5 2.3 spread.2
  112.8 30.2 %all_to_all.25 = f32[16,128,256]{2,1,0:T(8,128)S(1)} all-to-all(f32[16,128,256]{2,1,0:T(8,128)} %spread.2), channel_id=1, replica_groups=mesh['sub'=16,'sep'=16] {'sep'}, dimensions={0} | all-to-all | bytes 4194304 | tf_op jit(solution)/shard_map/all_to_all | solution.py:555
  143.0 1.1 fusion.8
  144.1 1.3 copy-done.1
  145.4 3.0 %collective-permute-start.6 = (f32[16,256]{1,0:T(8,128)S(1)}, f32[16,256]{1,0:T(8,128)S(1)}, u32[]{:S(2)}, u32[]{:S(2)}) collective-permute-start(f32[16,256]{1,0:T(8,128)S(1)} %slice.34), channel_id=1, source_target_pairs={{0,16},{16,0},{32,48},{48,32},{64,80},{80,64},{96,112},{112,96},{1... | collective-permute-start | bytes 49160 | tf_op jit(solution)/shard_map/ppermute | solution.py:507
  148.4 0.8 collective-permute-done.6
  149.3 0.9 collective-permute-start.7
  150.1 5.6 %collective-permute-done.7 = f32[16,256]{1,0:T(8,128)S(1)} collective-permute-done((f32[16,256]{1,0:T(8,128)S(1)}, f32[16,256]{1,0:T(8,128)S(1)}, u32[]{:S(2)}, u32[]{:S(2)}) %collective-permute-start.7) | collective-permute-done | bytes 16416 | tf_op jit(solution)/shard_map/ppermute | solution.py:547
  155.8 2.2 collective-permute-start.10
  158.5 0.9 collective-permute-start.8
  159.4 1.0 collective-permute-done.10.three_ref
  160.5 1.4 collective-permute-done.9.two_ref
  163.1 2.3 spread.3.after_ref
  165.4 4.4 %all-to-all-start.4 = ((f32[16,128,256]{2,1,0:T(8,128)}), f32[16,128,256]{2,1,0:T(8,128)}, u32[]{:S(2)}, u32[]{:S(2)}) async-start(f32[16,128,256]{2,1,0:T(8,128)} %spread.3.after_ref), calls=%async_computation.4 | async-start | bytes 4194304 | tf_op jit(solution)/shard_map/all_to_all | solution.py:555
  169.9 1.6 copy-done.2
  171.5 1.6 copy-done.4
  173.1 1.3 gram.1.refs_0_
  174.4 2.9 %collective-permute-start.11 = (f32[256,256]{1,0:T(8,128)S(1)}, f32[256,256]{1,0:T(8,128)S(1)}, u32[]{:S(2)}, u32[]{:S(2)}) collective-permute-start(f32[256,256]{1,0:T(8,128)S(1)} %gram.1.refs_0_), channel_id=1, source_target_pairs={{0,16},{16,0},{32,48},{48,32},{64,80},{80,64},{96,112},{112,96},{1... | collective-permute-start | bytes 786440 | tf_op jit(solution)/shard_map/ppermute | solution.py:507
  177.5 1.0 collective-permute-done.11.refs_1_
  178.5 14.2 %factor.1.factor_ref = f32[256,256]{1,0:T(8,128)S(1)} custom-call(f32[256,256]{1,0:T(8,128)S(1)} %gram.1.refs_0_, f32[256,256]{1,0:T(8,128)S(1)} %collective-permute-done.11.refs_1_), custom_call_target="tpu_custom_call" | custom-call | flops 12000000000 | bytes 800000 | tf_op jit(solution)/shard_map/factor/pallas_call | solution.py:132
  192.7 1.8 iterate.1.iterate_ref
  194.5 1.3 copy-done.9
  195.8 1.6 copy-done.10
  197.4 6.7 %image.1 = (f32[2048,256]{1,0:T(8,128)S(1)}, f32[640,256]{1,0:T(8,128)S(1)}, f32[264,256]{1,0:T(8,128)S(1)}) custom-call(s32[5]{0:T(128)S(1)} %pad_add_fusion.1.place_ref, f32[2048,256]{1,0:T(8,128)} %bitcast.16.raw_ref, f32[2048,256]{1,0:T(8,128)S(1)} %copy-done.10, f32[256,256]{1,0:T(8,128)S(1)} %factor.1.factor_ref), custom_call_target="tpu_custom_call" | custom-call | flops 3000000000 | bytes 7000000 | tf_op jit(solution)/shard_map/image/pallas_call | solution.py:225
  204.2 4.9 %collective-permute-start.13 = (f32[640,256]{1,0:T(8,128)S(1)}, f32[640,256]{1,0:T(8,128)S(1)}, u32[]{:S(2)}, u32[]{:S(2)}) collective-permute-start(f32[640,256]{1,0:T(8,128)S(1)} %get-tuple-element.21), channel_id=1, source_target_pairs={{0,16},{16,0},{32,48},{48,32},{64,80},{80,64},{96,112},{112,96},{1... | collective-permute-start | bytes 1966088 | tf_op jit(solution)/shard_map/ppermute | solution.py:507
  209.3 1.9 collective-permute-done.12.refs_3_
  211.2 21.3 %last.1 = (f32[256,256]{1,0:T(8,128)}, f32[1,256]{1,0:T(1,128)}, bf16[2048,256]{1,0:T(8,128)(2,1)}) custom-call(s32[6]{0:T(128)S(1)} %broadcast_shift-right-arithmetic_fusion.refs_0_, s32[6]{0:T(128)S(1)} %compare_convert_fusion.refs_1_, f32[264,256]{1,0:T(8,128)S(1)} %get-tuple-element.19.refs_2_, f32[264,256]{1,0:T(8,128)S(1)} %collective-permute-done.12.refs_3_, ...), custom_call_target="tpu_custom_call" | custom-call | flops 16000000000 | bytes 8000000 | tf_op jit(solution)/shard_map/last/pallas_call | solution.py:454
  (73 shorter events, 5.8 us)
Async XLA Ops:
  0.6 1.6 copy-start
  7.7 7.8 %copy-start.23 = (s32[1,4]{1,0:T(1,128)S(1)}, s32[1,4]{1,0:T(1,128)}, u32[]{:S(2)}) copy-start(s32[1,4]{1,0:T(1,128)} %param.13) | copy-start | bytes 52
  7.7 23.2 %all-to-all-start = ((bf16[16,32,1024]{2,1,0:T(8,128)(2,1)}), bf16[16,32,1024]{2,1,0:T(8,128)(2,1)S(1)}, u32[]{:S(2)}, u32[]{:S(2)}) async-start(bf16[16,32,1024]{2,1,0:T(8,128)(2,1)} %bitcast.41), calls=%async_computation | async-start | bytes 2097152 | tf_op jit(solution)/shard_map/all_to_all | solution.py:514
  32.8 5.2 %copy-start.22 = (f32[1,1024]{1,0:T(1,128)S(1)}, f32[1,1024]{1,0:T(1,128)}, u32[]{:S(2)}) copy-start(f32[1,1024]{1,0:T(1,128)} %param.10) | copy-start | bytes 12292
  32.8 29.8 %copy-start.7 = (s32[1,4]{1,0:T(1,128)S(1)}, s32[1,4]{1,0:T(1,128)}, u32[]{:S(2)}) copy-start(s32[1,4]{1,0:T(1,128)} %param.12) | copy-start | bytes 52
  32.8 29.8 %all-to-all-start.1 = ((bf16[16,64,1024]{2,1,0:T(8,128)(2,1)}), bf16[16,64,1024]{2,1,0:T(8,128)(2,1)}, u32[]{:S(2)}, u32[]{:S(2)}) async-start(bf16[16,64,1024]{2,1,0:T(8,128)(2,1)} %broadcast_in_dim.45), calls=%async_computation.1 | async-start | bytes 4194304 | tf_op jit(solution)/shard_map/all_to_all | solution.py:487
  66.5 0.7 copy-start.6
  67.2 27.5 %collective-permute-start = (bf16[2048,256]{1,0:T(8,128)(2,1)S(1)}, bf16[2048,256]{1,0:T(8,128)(2,1)}, u32[]{:S(2)}, u32[]{:S(2)}) collective-permute-start(bf16[2048,256]{1,0:T(8,128)(2,1)S(1)} %bitcast.35), channel_id=1, source_target_pairs={{0,16},{16,0},{32,48},{48,32},{64,80},{80,64},{96,112},{112,96},{1... | collective-permute-start | bytes 3145736 | tf_op jit(solution)/shard_map/ppermute | solution.py:507
  72.9 21.7 %all-to-all-start.2 = ((bf16[16,16,640]{2,1,0:T(8,128)(2,1)}), bf16[16,16,640]{2,1,0:T(8,128)(2,1)S(1)}, u32[]{:S(2)}, u32[]{:S(2)}) async-start(bf16[16,16,640]{2,1,0:T(8,128)(2,1)} %copy-done.6), calls=%async_computation.2 | async-start | bytes 655360 | tf_op jit(solution)/shard_map/all_to_all | solution.py:535
  94.7 1.0 copy-start.5
  97.7 6.8 %collective-permute-start.2 = (f32[16,256]{1,0:T(8,128)S(1)}, f32[16,256]{1,0:T(8,128)S(1)}, u32[]{:S(2)}, u32[]{:S(2)}) collective-permute-start(f32[16,256]{1,0:T(8,128)S(1)} %get-tuple-element.18), channel_id=1, source_target_pairs={{0,128},{16,144},{32,160},{48,176},{64,192},{80,208},{96,224},{112... | collective-permute-start | bytes 49160 | tf_op jit(solution)/shard_map/ppermute | solution.py:547
  98.7 9.4 %collective-permute-start.1 = (f32[16,2048]{1,0:T(8,128)S(1)}, f32[16,2048]{1,0:T(8,128)S(1)}, u32[]{:S(2)}, u32[]{:S(2)}) collective-permute-start(f32[16,2048]{1,0:T(8,128)S(1)} %get-tuple-element.17), channel_id=1, source_target_pairs={{0,16},{16,0},{32,48},{48,32},{64,80},{80,64},{96,112},{112,96},{1... | collective-permute-start | bytes 393224 | tf_op jit(solution)/shard_map/ppermute | solution.py:507
  104.5 5.4 %copy-start.14 = (f32[2,16,256]{2,1,0:T(8,128)}, f32[2,16,256]{2,1,0:T(8,128)S(1)}, u32[]{:S(2)}) copy-start(f32[2,16,256]{2,1,0:T(8,128)S(1)} %pad_maximum_fusion.own_ref) | copy-start | bytes 98308
  104.5 4.7 %collective-permute-start.5 = (f32[2,16,256]{2,1,0:T(8,128)S(1)}, f32[2,16,256]{2,1,0:T(8,128)S(1)}, u32[]{:S(2)}, u32[]{:S(2)}) collective-permute-start(f32[2,16,256]{2,1,0:T(8,128)S(1)} %pad_maximum_fusion.own_ref), channel_id=1, source_target_pairs={{0,96},{16,112},{32,64},{48,80},{64,32},{80,48},{96,0},{112,16},{1... | collective-permute-start | bytes 98312 | tf_op jit(solution)/shard_map/ppermute | solution.py:547
  105.2 4.0 %collective-permute-start.4 = (f32[2,16,256]{2,1,0:T(8,128)S(1)}, f32[2,16,256]{2,1,0:T(8,128)S(1)}, u32[]{:S(2)}, u32[]{:S(2)}) collective-permute-start(f32[2,16,256]{2,1,0:T(8,128)S(1)} %pad_maximum_fusion.own_ref), channel_id=1, source_target_pairs={{0,64},{16,80},{32,96},{48,112},{64,0},{80,16},{96,32},{112,48},{1... | collective-permute-start | bytes 98312 | tf_op jit(solution)/shard_map/ppermute | solution.py:547
  105.2 4.7 %collective-permute-start.3 = (f32[2,16,256]{2,1,0:T(8,128)S(1)}, f32[2,16,256]{2,1,0:T(8,128)S(1)}, u32[]{:S(2)}, u32[]{:S(2)}) collective-permute-start(f32[2,16,256]{2,1,0:T(8,128)S(1)} %pad_maximum_fusion.own_ref), channel_id=1, source_target_pairs={{0,32},{16,48},{32,0},{48,16},{64,96},{80,112},{96,64},{112,80},{1... | collective-permute-start | bytes 98312 | tf_op jit(solution)/shard_map/ppermute | solution.py:547
  108.1 1.7 copy-start.11
  109.2 0.6 copy-start.16
  109.2 0.6 copy-start.17
  109.9 0.6 copy-start.19
  112.8 30.2 %copy-start.12 = (f32[32,2048]{1,0:T(8,128)S(1)}, f32[32,2048]{1,0:T(8,128)}, u32[]{:S(2)}) copy-start(f32[32,2048]{1,0:T(8,128)} %copy-done.11) | copy-start | bytes 786436
  144.1 1.3 copy-start.1
  145.4 3.9 %collective-permute-start.6 = (f32[16,256]{1,0:T(8,128)S(1)}, f32[16,256]{1,0:T(8,128)S(1)}, u32[]{:S(2)}, u32[]{:S(2)}) collective-permute-start(f32[16,256]{1,0:T(8,128)S(1)} %slice.34), channel_id=1, source_target_pairs={{0,16},{16,0},{32,48},{48,32},{64,80},{80,64},{96,112},{112,96},{1... | collective-permute-start | bytes 49160 | tf_op jit(solution)/shard_map/ppermute | solution.py:507
  149.3 12.6 %copy-start.13 = (f32[16,256]{1,0:T(8,128)}, f32[16,256]{1,0:T(8,128)S(1)}, u32[]{:S(2)}) copy-start(f32[16,256]{1,0:T(8,128)S(1)} %slice_add_fusion.after_ref) | copy-start | bytes 49156
  149.3 6.5 %collective-permute-start.7 = (f32[16,256]{1,0:T(8,128)S(1)}, f32[16,256]{1,0:T(8,128)S(1)}, u32[]{:S(2)}, u32[]{:S(2)}) collective-permute-start(f32[16,256]{1,0:T(8,128)S(1)} %slice_add_fusion.after_ref), channel_id=1, source_target_pairs={{0,128},{16,144},{32,160},{48,176},{64,192},{80,208},{96,224},{112... | collective-permute-start | bytes 49160 | tf_op jit(solution)/shard_map/ppermute | solution.py:547
  155.8 6.1 %copy-start.15 = (f32[2,16,256]{2,1,0:T(8,128)}, f32[2,16,256]{2,1,0:T(8,128)S(1)}, u32[]{:S(2)}) copy-start(f32[2,16,256]{2,1,0:T(8,128)S(1)} %pad_maximum_fusion.1.own_ref) | copy-start | bytes 98308
  155.8 4.7 %collective-permute-start.10 = (f32[2,16,256]{2,1,0:T(8,128)S(1)}, f32[2,16,256]{2,1,0:T(8,128)S(1)}, u32[]{:S(2)}, u32[]{:S(2)}) collective-permute-start(f32[2,16,256]{2,1,0:T(8,128)S(1)} %pad_maximum_fusion.1.own_ref), channel_id=1, source_target_pairs={{0,96},{16,112},{32,64},{48,80},{64,32},{80,48},{96,0},{112,16},{1... | collective-permute-start | bytes 98312 | tf_op jit(solution)/shard_map/ppermute | solution.py:547
  158.0 3.9 %collective-permute-start.9 = (f32[2,16,256]{2,1,0:T(8,128)S(1)}, f32[2,16,256]{2,1,0:T(8,128)S(1)}, u32[]{:S(2)}, u32[]{:S(2)}) collective-permute-start(f32[2,16,256]{2,1,0:T(8,128)S(1)} %pad_maximum_fusion.1.own_ref), channel_id=1, source_target_pairs={{0,64},{16,80},{32,96},{48,112},{64,0},{80,16},{96,32},{112,48},{1... | collective-permute-start | bytes 98312 | tf_op jit(solution)/shard_map/ppermute | solution.py:547
  158.5 3.4 %collective-permute-start.8 = (f32[2,16,256]{2,1,0:T(8,128)S(1)}, f32[2,16,256]{2,1,0:T(8,128)S(1)}, u32[]{:S(2)}, u32[]{:S(2)}) collective-permute-start(f32[2,16,256]{2,1,0:T(8,128)S(1)} %pad_maximum_fusion.1.own_ref), channel_id=1, source_target_pairs={{0,32},{16,48},{32,0},{48,16},{64,96},{80,112},{96,64},{112,80},{1... | collective-permute-start | bytes 98312 | tf_op jit(solution)/shard_map/ppermute | solution.py:547
  160.5 1.5 copy-start.18
  161.9 0.6 copy-start.20
  162.5 0.6 copy-start.21
  165.4 30.4 %all-to-all-start.4 = ((f32[16,128,256]{2,1,0:T(8,128)}), f32[16,128,256]{2,1,0:T(8,128)}, u32[]{:S(2)}, u32[]{:S(2)}) async-start(f32[16,128,256]{2,1,0:T(8,128)} %spread.3.after_ref), calls=%async_computation.4 | async-start | bytes 4194304 | tf_op jit(solution)/shard_map/all_to_all | solution.py:555
  169.9 1.6 copy-start.2
  171.5 1.6 copy-start.4
  174.4 4.1 %collective-permute-start.11 = (f32[256,256]{1,0:T(8,128)S(1)}, f32[256,256]{1,0:T(8,128)S(1)}, u32[]{:S(2)}, u32[]{:S(2)}) collective-permute-start(f32[256,256]{1,0:T(8,128)S(1)} %gram.1.refs_0_), channel_id=1, source_target_pairs={{0,16},{16,0},{32,48},{48,32},{64,80},{80,64},{96,112},{112,96},{1... | collective-permute-start | bytes 786440 | tf_op jit(solution)/shard_map/ppermute | solution.py:507
  177.5 15.2 %copy-start.3 = (f32[16,128,256]{2,1,0:T(8,128)S(1)}, f32[16,128,256]{2,1,0:T(8,128)}, u32[]{:S(2)}) copy-start(f32[16,128,256]{2,1,0:T(8,128)} %copy-done.1) | copy-start | bytes 6291460
  194.5 1.3 copy-start.9
  195.8 1.6 copy-start.10
  197.4 13.8 %copy-start.8 = (bf16[1,2048,1024]{2,1,0:T(8,128)(2,1)S(1)}, bf16[1,2048,1024]{2,1,0:T(8,128)(2,1)}, u32[]{:S(2)}) copy-start(bf16[1,2048,1024]{2,1,0:T(8,128)(2,1)} %param.8) | copy-start | bytes 12582916
  204.2 7.0 %collective-permute-start.13 = (f32[640,256]{1,0:T(8,128)S(1)}, f32[640,256]{1,0:T(8,128)S(1)}, u32[]{:S(2)}, u32[]{:S(2)}) collective-permute-start(f32[640,256]{1,0:T(8,128)S(1)} %get-tuple-element.21), channel_id=1, source_target_pairs={{0,16},{16,0},{32,48},{48,32},{64,80},{80,64},{96,112},{112,96},{1... | collective-permute-start | bytes 1966088 | tf_op jit(solution)/shard_map/ppermute | solution.py:507
  209.1 2.1 collective-permute-start.12

commit v4 on v3

--- a/solution.py
+++ b/solution.py
@@ -267,6 +267,7 @@
             pltpu.VMEM((8 * slim, width), jnp.float32),
             pltpu.SemaphoreType.DMA((count,)),
         ],
+        compiler_params=pltpu.CompilerParams(vmem_limit_bytes=4 * 1024 * 1024),
         cost_estimate=pl.CostEstimate(flops=0, bytes_accessed=2_400_000, transcendentals=0),
         name="spread",
     )(low, *pieces, after)
@@ -553,14 +554,14 @@
         pieces = [pair] + [from_layer(pair, distance) for distance in (1, 2, 3)]
         spread = spread_rows((layer & 3)[None], pieces, after, sep_count)
         whole = lax.all_to_all(spread, "sep", 0, 0, tiled=True)
-        return whole.reshape(total_rows // 2, vec_width), spread
+        return whole.reshape(total_rows // 2, vec_width), pieces[1]
 
     first_half, _ = gather_half(first_rows, operator_half)
     both_rows = dot_f32(operator_half, first_half)
     second_rows = both_rows[:slim] + from_twin(both_rows[slim:])
-    raw_half, second_spread = gather_half(second_rows, second_rows)
-
-    first_gram = gram_of(first_half, second_spread)
+    raw_half, second_piece = gather_half(second_rows, second_rows)
+
+    first_gram = gram_of(first_half, second_piece)
     first_factor = inverse_transposed_factor(first_gram, from_twin(first_gram), scaling)
     iterate_half = iterate_of(first_half, first_factor)
 

time: 234 us -> 234 us (level)
    unnamed x49 -> x27, local copies, waits for them, and re-layouts: 12.5 us -> 10.6 us
  transfers between devices with their start and end apart: 18 -> 18, of which waited for: 12 -> 13; matrix products, arithmetic and copies ran while one was open for 2% -> 2% of each run, Pallas kernels for 7% -> 7%
where the time goes in v4:
time: 234 us; the launch traced here: 233 us
  waiting for transfers between devices  68.6 us (29%)
  Pallas kernels  57 us (24%)
  starting transfers between devices  52.7 us (23%)
  blocking collectives  29.8 us (13%)
  local copies, waits for them, and re-layouts  15.5 us (7%)
  matrix products  6.6 us (3%)
    all_to_all x1, blocking collectives, gather_half(): whole = lax.all_to_all(spread, 'sep', 0, 0, tiled=True)  29.8 us
    all_to_all x1, waiting for transfers between devices, gather_blocks(): return lax.all_to_all(spread, axis, 0, 0, tiled=True)  24.6 us
    pallas_call x1, Pallas kernels, last_products(): pl.pallas_call(lambda *refs: last_kernel(scale, *refs), in_specs=[scalars...  21.3 us
    ppermute x6, starting transfers between devices, from_twin(): return lax.ppermute(x, 'sub', [(i, i ^ 1) for i in range(sub_count)])  18.3 us
    ppermute x8, waiting for transfers between devices, from_layer(): return lax.ppermute(x, 'sub', perm)  14.8 us
    pallas_call x1, Pallas kernels, inverse_transposed_factor(): pl.pallas_call(lambda *refs: factor_kernel(scale, *refs), out_shape=jax.S...  14.2 us
    all_to_all x1, waiting for transfers between devices, per_device(): lax.all_to_all(partial.reshape(sep_count, share, mode_total), 'sep', 0, 0...  13.3 us
    all_to_all x1, waiting for transfers between devices, per_device(): incoming = lax.all_to_all(outgoing, 'sub', 0, 0, tiled=True)  11.4 us
  transfers between devices with their start and end apart: 18, of which 13 were waited for; matrix products, arithmetic and copies ran while one was open for 2% of the time, Pallas kernels for 7%

profile of v4, /device:TPU:1, one launch (start us, length us, event | category | flops | bytes accessed | tf_op | source)
XLA Modules:
  0.0 233.2 jit_solution(17703198471920085052)
XLA Ops:
  0.6 1.6 copy-done
  2.2 5.5 %fusion.2 = bf16[512,1024]{1,0:T(8,128)(2,1)} fusion(bf16[1,2048,512]{2,1,0:T(8,128)(2,1)S(1)} %copy-done, bf16[1,2048,1024]{2,1,0:T(8,128)(2,1)} %param.8), kind=kOutput, calls=%fused_computation.3 | convolution fusion | flops 2148007936 | bytes 7340032 | tf_op jit(solution)/shard_map/dot_general | solution.py:511
  7.7 7.7 %all-to-all-start = ((bf16[16,32,1024]{2,1,0:T(8,128)(2,1)}), bf16[16,32,1024]{2,1,0:T(8,128)(2,1)S(1)}, u32[]{:S(2)}, u32[]{:S(2)}) async-start(bf16[16,32,1024]{2,1,0:T(8,128)(2,1)} %bitcast.41), calls=%async_computation | async-start | bytes 2097152 | tf_op jit(solution)/shard_map/all_to_all | solution.py:515
  16.7 0.9 dynamic-slice_convert_fusion
  17.7 13.3 %all-to-all-done = bf16[16,32,1024]{2,1,0:T(8,128)(2,1)S(1)} async-done(((bf16[16,32,1024]{2,1,0:T(8,128)(2,1)}), bf16[16,32,1024]{2,1,0:T(8,128)(2,1)S(1)}, u32[]{:S(2)}, u32[]{:S(2)}) %all-to-all-start) | async-done | bytes 1048608 | tf_op jit(solution)/shard_map/all_to_all | solution.py:515
  31.2 1.6 broadcast_in_dim.45
  32.8 4.6 %all-to-all-start.1 = ((bf16[16,64,1024]{2,1,0:T(8,128)(2,1)}), bf16[16,64,1024]{2,1,0:T(8,128)(2,1)}, u32[]{:S(2)}, u32[]{:S(2)}) async-start(bf16[16,64,1024]{2,1,0:T(8,128)(2,1)} %broadcast_in_dim.45), calls=%async_computation.1 | async-start | bytes 4194304 | tf_op jit(solution)/shard_map/all_to_all | solution.py:488
  38.1 24.6 %all-to-all-done.1.gathered_ref.refs_7_ = bf16[16,64,1024]{2,1,0:T(8,128)(2,1)} async-done(((bf16[16,64,1024]{2,1,0:T(8,128)(2,1)}), bf16[16,64,1024]{2,1,0:T(8,128)(2,1)}, u32[]{:S(2)}, u32[]{:S(2)}) %all-to-all-start.1) | async-done | bytes 2097184 | tf_op jit(solution)/shard_map/all_to_all | solution.py:488
  62.7 3.8 %rows.1 = (bf16[16,16,640]{2,1,0:T(8,128)(2,1)S(1)}, bf16[16,128,256]{2,1,0:T(8,128)(2,1)S(1)}) custom-call(s32[4]{0:T(128)S(1)} %bitcast.37, s32[1]{0:T(128)} %bitcast.2.first_ref, f32[1,1024]{1,0:T(1,128)S(1)} %compare_select_fusion.weight_ref.refs_6_, bf16[16,64,1024]{2,1,0:T(8,128)(2,1)} %all-to-all-done.1.gathered_ref.refs_7_), custom_call_target="tpu_custom_call" | custom-call | flops 800000000 | bytes 2700000 | tf_op jit(solution)/shard_map/rows/pallas_call | solution.py:321
  67.2 5.7 %collective-permute-start = (bf16[2048,256]{1,0:T(8,128)(2,1)S(1)}, bf16[2048,256]{1,0:T(8,128)(2,1)}, u32[]{:S(2)}, u32[]{:S(2)}) collective-permute-start(bf16[2048,256]{1,0:T(8,128)(2,1)S(1)} %bitcast.35), channel_id=1, source_target_pairs={{0,16},{16,0},{32,48},{48,32},{64,80},{80,64},{96,112},{112,96},{1... | collective-permute-start | bytes 3145736 | tf_op jit(solution)/shard_map/ppermute | solution.py:508
  72.9 8.6 %all-to-all-start.2 = ((bf16[16,16,640]{2,1,0:T(8,128)(2,1)}), bf16[16,16,640]{2,1,0:T(8,128)(2,1)S(1)}, u32[]{:S(2)}, u32[]{:S(2)}) async-start(bf16[16,16,640]{2,1,0:T(8,128)(2,1)} %copy-done.6), calls=%async_computation.2 | async-start | bytes 655360 | tf_op jit(solution)/shard_map/all_to_all | solution.py:536
  81.5 1.7 constant_dynamic-slice_fusion.flex_ref
  83.2 11.4 %all-to-all-done.2.incoming_ref = bf16[16,16,640]{2,1,0:T(8,128)(2,1)S(1)} async-done(((bf16[16,16,640]{2,1,0:T(8,128)(2,1)}), bf16[16,16,640]{2,1,0:T(8,128)(2,1)S(1)}, u32[]{:S(2)}, u32[]{:S(2)}) %all-to-all-start.2) | async-done | bytes 327712 | tf_op jit(solution)/shard_map/all_to_all | solution.py:536
  94.7 0.9 copy-done.5
  95.7 2.0 build.1
  97.7 1.0 collective-permute-start.2
  98.7 0.8 collective-permute-start.1
  99.4 5.0 %collective-permute-done.2 = f32[16,256]{1,0:T(8,128)S(1)} collective-permute-done((f32[16,256]{1,0:T(8,128)S(1)}, f32[16,256]{1,0:T(8,128)S(1)}, u32[]{:S(2)}, u32[]{:S(2)}) %collective-permute-start.2) | collective-permute-done | bytes 16416 | tf_op jit(solution)/shard_map/ppermute | solution.py:548
  105.2 2.9 %collective-permute-start.3 = (f32[2,16,256]{2,1,0:T(8,128)S(1)}, f32[2,16,256]{2,1,0:T(8,128)S(1)}, u32[]{:S(2)}, u32[]{:S(2)}) collective-permute-start(f32[2,16,256]{2,1,0:T(8,128)S(1)} %pad_maximum_fusion.own_ref), channel_id=1, source_target_pairs={{0,32},{16,48},{32,0},{48,16},{64,96},{80,112},{96,64},{112,80},{1... | collective-permute-start | bytes 98312 | tf_op jit(solution)/shard_map/ppermute | solution.py:548
  108.1 1.1 collective-permute-done.5.three_ref
  109.8 2.9 %spread.2 = f32[16,128,256]{2,1,0:T(8,128)S(1)} custom-call(s32[1]{0:T(128)} %bitcast.8.low_ref, f32[2,16,256]{2,1,0:T(8,128)S(1)} %pad_maximum_fusion.own_ref, f32[2,16,256]{2,1,0:T(8,128)S(1)} %collective-permute-done.3.one_ref, f32[2,16,256]{2,1,0:T(8,128)S(1)} %collective-permute-done.4.two_ref, f32[2,16,256]{2,1,0:T(8,128)S(1)} %collective-permute-done.5.three_ref, ...), custom_call_target="tpu_custom_call" | custom-call | bytes 2400000 | tf_op jit(solution)/shard_map/spread/pallas_call | solution.py:261
  112.7 29.8 %all_to_all.25 = f32[16,128,256]{2,1,0:T(8,128)S(1)} all-to-all(f32[16,128,256]{2,1,0:T(8,128)S(1)} %spread.2), channel_id=1, replica_groups=mesh['sub'=16,'sep'=16] {'sep'}, dimensions={0} | all-to-all | bytes 4194304 | tf_op jit(solution)/shard_map/all_to_all | solution.py:556
  142.6 1.1 fusion.8
  143.7 1.4 copy-done.1
  145.1 3.0 %collective-permute-start.6 = (f32[16,256]{1,0:T(8,128)S(1)}, f32[16,256]{1,0:T(8,128)S(1)}, u32[]{:S(2)}, u32[]{:S(2)}) collective-permute-start(f32[16,256]{1,0:T(8,128)S(1)} %slice.34), channel_id=1, source_target_pairs={{0,16},{16,0},{32,48},{48,32},{64,80},{80,64},{96,112},{112,96},{1... | collective-permute-start | bytes 49160 | tf_op jit(solution)/shard_map/ppermute | solution.py:508
  148.1 0.8 collective-permute-done.6
  148.9 0.9 collective-permute-start.7
  149.8 5.6 %collective-permute-done.7 = f32[16,256]{1,0:T(8,128)S(1)} collective-permute-done((f32[16,256]{1,0:T(8,128)S(1)}, f32[16,256]{1,0:T(8,128)S(1)}, u32[]{:S(2)}, u32[]{:S(2)}) %collective-permute-start.7) | collective-permute-done | bytes 16416 | tf_op jit(solution)/shard_map/ppermute | solution.py:548
  155.4 2.2 collective-permute-start.10
  158.2 0.9 collective-permute-start.8
  159.1 1.0 collective-permute-done.10.three_ref
  160.1 1.4 collective-permute-done.9.two_ref
  161.5 2.9 %spread.3 = f32[16,128,256]{2,1,0:T(8,128)S(1)} custom-call(s32[1]{0:T(128)} %bitcast.8.low_ref, f32[2,16,256]{2,1,0:T(8,128)S(1)} %pad_maximum_fusion.1.own_ref, f32[2,16,256]{2,1,0:T(8,128)S(1)} %collective-permute-done.8.one_ref.after_ref, f32[2,16,256]{2,1,0:T(8,128)S(1)} %collective-permute-done.9.two_ref, ...), custom_call_target="tpu_custom_call" | custom-call | bytes 2400000 | tf_op jit(solution)/shard_map/spread/pallas_call | solution.py:261
  164.4 1.4 copy-done.4
  165.8 4.4 %all-to-all-start.4 = ((f32[16,128,256]{2,1,0:T(8,128)}), f32[16,128,256]{2,1,0:T(8,128)}, u32[]{:S(2)}, u32[]{:S(2)}) async-start(f32[16,128,256]{2,1,0:T(8,128)} %copy-done.4), calls=%async_computation.4 | async-start | bytes 4194304 | tf_op jit(solution)/shard_map/all_to_all | solution.py:556
  170.2 1.6 copy-done.2
  171.8 1.3 gram.1.refs_0_
  173.2 3.1 %collective-permute-start.11 = (f32[256,256]{1,0:T(8,128)S(1)}, f32[256,256]{1,0:T(8,128)S(1)}, u32[]{:S(2)}, u32[]{:S(2)}) collective-permute-start(f32[256,256]{1,0:T(8,128)S(1)} %gram.1.refs_0_), channel_id=1, source_target_pairs={{0,16},{16,0},{32,48},{48,32},{64,80},{80,64},{96,112},{112,96},{1... | collective-permute-start | bytes 786440 | tf_op jit(solution)/shard_map/ppermute | solution.py:508
  176.4 1.0 collective-permute-done.11.refs_1_
  177.4 14.2 %factor.1.factor_ref = f32[256,256]{1,0:T(8,128)S(1)} custom-call(f32[256,256]{1,0:T(8,128)S(1)} %gram.1.refs_0_, f32[256,256]{1,0:T(8,128)S(1)} %collective-permute-done.11.refs_1_), custom_call_target="tpu_custom_call" | custom-call | flops 12000000000 | bytes 800000 | tf_op jit(solution)/shard_map/factor/pallas_call | solution.py:132
  191.6 1.8 iterate.1.iterate_ref
  193.4 1.4 copy-done.9
  194.8 0.8 all-to-all-done.4
  195.6 1.6 copy-done.10
  197.2 6.7 %image.1 = (f32[2048,256]{1,0:T(8,128)S(1)}, f32[640,256]{1,0:T(8,128)S(1)}, f32[264,256]{1,0:T(8,128)S(1)}) custom-call(s32[5]{0:T(128)S(1)} %pad_add_fusion.1.place_ref, f32[2048,256]{1,0:T(8,128)} %bitcast.16.raw_ref, f32[2048,256]{1,0:T(8,128)S(1)} %copy-done.10, f32[256,256]{1,0:T(8,128)S(1)} %factor.1.factor_ref), custom_call_target="tpu_custom_call" | custom-call | flops 3000000000 | bytes 7000000 | tf_op jit(solution)/shard_map/image/pallas_call | solution.py:225
  203.9 5.6 %collective-permute-start.13 = (f32[640,256]{1,0:T(8,128)S(1)}, f32[640,256]{1,0:T(8,128)S(1)}, u32[]{:S(2)}, u32[]{:S(2)}) collective-permute-start(f32[640,256]{1,0:T(8,128)S(1)} %get-tuple-element.21), channel_id=1, source_target_pairs={{0,16},{16,0},{32,48},{48,32},{64,80},{80,64},{96,112},{112,96},{1... | collective-permute-start | bytes 1966088 | tf_op jit(solution)/shard_map/ppermute | solution.py:508
  209.8 1.9 collective-permute-done.12.refs_3_
  211.6 21.3 %last.1 = (f32[256,256]{1,0:T(8,128)}, f32[1,256]{1,0:T(1,128)}, bf16[2048,256]{1,0:T(8,128)(2,1)}) custom-call(s32[6]{0:T(128)S(1)} %broadcast_shift-right-arithmetic_fusion.refs_0_, s32[6]{0:T(128)S(1)} %compare_convert_fusion.refs_1_, f32[264,256]{1,0:T(8,128)S(1)} %get-tuple-element.19.refs_2_, f32[264,256]{1,0:T(8,128)S(1)} %collective-permute-done.12.refs_3_, ...), custom_call_target="tpu_custom_call" | custom-call | flops 16000000000 | bytes 8000000 | tf_op jit(solution)/shard_map/last/pallas_call | solution.py:455
  (51 shorter events, 4.7 us)
Async XLA Ops:
  0.6 1.6 copy-start
  7.7 7.8 %copy-start.12 = (s32[1,4]{1,0:T(1,128)S(1)}, s32[1,4]{1,0:T(1,128)}, u32[]{:S(2)}) copy-start(s32[1,4]{1,0:T(1,128)} %param.13) | copy-start | bytes 52
  7.7 23.2 %all-to-all-start = ((bf16[16,32,1024]{2,1,0:T(8,128)(2,1)}), bf16[16,32,1024]{2,1,0:T(8,128)(2,1)S(1)}, u32[]{:S(2)}, u32[]{:S(2)}) async-start(bf16[16,32,1024]{2,1,0:T(8,128)(2,1)} %bitcast.41), calls=%async_computation | async-start | bytes 2097152 | tf_op jit(solution)/shard_map/all_to_all | solution.py:515
  32.8 5.2 %copy-start.11 = (f32[1,1024]{1,0:T(1,128)S(1)}, f32[1,1024]{1,0:T(1,128)}, u32[]{:S(2)}) copy-start(f32[1,1024]{1,0:T(1,128)} %param.10) | copy-start | bytes 12292
  32.8 29.8 %copy-start.7 = (s32[1,4]{1,0:T(1,128)S(1)}, s32[1,4]{1,0:T(1,128)}, u32[]{:S(2)}) copy-start(s32[1,4]{1,0:T(1,128)} %param.12) | copy-start | bytes 52
  32.8 29.8 %all-to-all-start.1 = ((bf16[16,64,1024]{2,1,0:T(8,128)(2,1)}), bf16[16,64,1024]{2,1,0:T(8,128)(2,1)}, u32[]{:S(2)}, u32[]{:S(2)}) async-start(bf16[16,64,1024]{2,1,0:T(8,128)(2,1)} %broadcast_in_dim.45), calls=%async_computation.1 | async-start | bytes 4194304 | tf_op jit(solution)/shard_map/all_to_all | solution.py:488
  66.5 0.7 copy-start.6
  67.2 27.5 %collective-permute-start = (bf16[2048,256]{1,0:T(8,128)(2,1)S(1)}, bf16[2048,256]{1,0:T(8,128)(2,1)}, u32[]{:S(2)}, u32[]{:S(2)}) collective-permute-start(bf16[2048,256]{1,0:T(8,128)(2,1)S(1)} %bitcast.35), channel_id=1, source_target_pairs={{0,16},{16,0},{32,48},{48,32},{64,80},{80,64},{96,112},{112,96},{1... | collective-permute-start | bytes 3145736 | tf_op jit(solution)/shard_map/ppermute | solution.py:508
  72.9 21.7 %all-to-all-start.2 = ((bf16[16,16,640]{2,1,0:T(8,128)(2,1)}), bf16[16,16,640]{2,1,0:T(8,128)(2,1)S(1)}, u32[]{:S(2)}, u32[]{:S(2)}) async-start(bf16[16,16,640]{2,1,0:T(8,128)(2,1)} %copy-done.6), calls=%async_computation.2 | async-start | bytes 655360 | tf_op jit(solution)/shard_map/all_to_all | solution.py:536
  94.7 1.0 copy-start.5
  97.7 6.8 %collective-permute-start.2 = (f32[16,256]{1,0:T(8,128)S(1)}, f32[16,256]{1,0:T(8,128)S(1)}, u32[]{:S(2)}, u32[]{:S(2)}) collective-permute-start(f32[16,256]{1,0:T(8,128)S(1)} %get-tuple-element.18), channel_id=1, source_target_pairs={{0,128},{16,144},{32,160},{48,176},{64,192},{80,208},{96,224},{112... | collective-permute-start | bytes 49160 | tf_op jit(solution)/shard_map/ppermute | solution.py:548
  98.7 9.4 %collective-permute-start.1 = (f32[16,2048]{1,0:T(8,128)S(1)}, f32[16,2048]{1,0:T(8,128)S(1)}, u32[]{:S(2)}, u32[]{:S(2)}) collective-permute-start(f32[16,2048]{1,0:T(8,128)S(1)} %get-tuple-element.17), channel_id=1, source_target_pairs={{0,16},{16,0},{32,48},{48,32},{64,80},{80,64},{96,112},{112,96},{1... | collective-permute-start | bytes 393224 | tf_op jit(solution)/shard_map/ppermute | solution.py:508
  104.4 4.7 %collective-permute-start.5 = (f32[2,16,256]{2,1,0:T(8,128)S(1)}, f32[2,16,256]{2,1,0:T(8,128)S(1)}, u32[]{:S(2)}, u32[]{:S(2)}) collective-permute-start(f32[2,16,256]{2,1,0:T(8,128)S(1)} %pad_maximum_fusion.own_ref), channel_id=1, source_target_pairs={{0,96},{16,112},{32,64},{48,80},{64,32},{80,48},{96,0},{112,16},{1... | collective-permute-start | bytes 98312 | tf_op jit(solution)/shard_map/ppermute | solution.py:548
  105.2 4.0 %collective-permute-start.4 = (f32[2,16,256]{2,1,0:T(8,128)S(1)}, f32[2,16,256]{2,1,0:T(8,128)S(1)}, u32[]{:S(2)}, u32[]{:S(2)}) collective-permute-start(f32[2,16,256]{2,1,0:T(8,128)S(1)} %pad_maximum_fusion.own_ref), channel_id=1, source_target_pairs={{0,64},{16,80},{32,96},{48,112},{64,0},{80,16},{96,32},{112,48},{1... | collective-permute-start | bytes 98312 | tf_op jit(solution)/shard_map/ppermute | solution.py:548
  105.2 4.7 %collective-permute-start.3 = (f32[2,16,256]{2,1,0:T(8,128)S(1)}, f32[2,16,256]{2,1,0:T(8,128)S(1)}, u32[]{:S(2)}, u32[]{:S(2)}) collective-permute-start(f32[2,16,256]{2,1,0:T(8,128)S(1)} %pad_maximum_fusion.own_ref), channel_id=1, source_target_pairs={{0,32},{16,48},{32,0},{48,16},{64,96},{80,112},{96,64},{112,80},{1... | collective-permute-start | bytes 98312 | tf_op jit(solution)/shard_map/ppermute | solution.py:548
  143.7 1.4 copy-start.1
  145.1 3.9 %collective-permute-start.6 = (f32[16,256]{1,0:T(8,128)S(1)}, f32[16,256]{1,0:T(8,128)S(1)}, u32[]{:S(2)}, u32[]{:S(2)}) collective-permute-start(f32[16,256]{1,0:T(8,128)S(1)} %slice.34), channel_id=1, source_target_pairs={{0,16},{16,0},{32,48},{48,32},{64,80},{80,64},{96,112},{112,96},{1... | collective-permute-start | bytes 49160 | tf_op jit(solution)/shard_map/ppermute | solution.py:508
  148.9 6.5 %collective-permute-start.7 = (f32[16,256]{1,0:T(8,128)S(1)}, f32[16,256]{1,0:T(8,128)S(1)}, u32[]{:S(2)}, u32[]{:S(2)}) collective-permute-start(f32[16,256]{1,0:T(8,128)S(1)} %slice_add_fusion.after_ref), channel_id=1, source_target_pairs={{0,128},{16,144},{32,160},{48,176},{64,192},{80,208},{96,224},{112... | collective-permute-start | bytes 49160 | tf_op jit(solution)/shard_map/ppermute | solution.py:548
  155.4 4.7 %collective-permute-start.10 = (f32[2,16,256]{2,1,0:T(8,128)S(1)}, f32[2,16,256]{2,1,0:T(8,128)S(1)}, u32[]{:S(2)}, u32[]{:S(2)}) collective-permute-start(f32[2,16,256]{2,1,0:T(8,128)S(1)} %pad_maximum_fusion.1.own_ref), channel_id=1, source_target_pairs={{0,96},{16,112},{32,64},{48,80},{64,32},{80,48},{96,0},{112,16},{1... | collective-permute-start | bytes 98312 | tf_op jit(solution)/shard_map/ppermute | solution.py:548
  157.6 3.9 %collective-permute-start.9 = (f32[2,16,256]{2,1,0:T(8,128)S(1)}, f32[2,16,256]{2,1,0:T(8,128)S(1)}, u32[]{:S(2)}, u32[]{:S(2)}) collective-permute-start(f32[2,16,256]{2,1,0:T(8,128)S(1)} %pad_maximum_fusion.1.own_ref), channel_id=1, source_target_pairs={{0,64},{16,80},{32,96},{48,112},{64,0},{80,16},{96,32},{112,48},{1... | collective-permute-start | bytes 98312 | tf_op jit(solution)/shard_map/ppermute | solution.py:548
  158.2 3.3 %collective-permute-start.8 = (f32[2,16,256]{2,1,0:T(8,128)S(1)}, f32[2,16,256]{2,1,0:T(8,128)S(1)}, u32[]{:S(2)}, u32[]{:S(2)}) collective-permute-start(f32[2,16,256]{2,1,0:T(8,128)S(1)} %pad_maximum_fusion.1.own_ref), channel_id=1, source_target_pairs={{0,32},{16,48},{32,0},{48,16},{64,96},{80,112},{96,64},{112,80},{1... | collective-permute-start | bytes 98312 | tf_op jit(solution)/shard_map/ppermute | solution.py:548
  164.4 1.4 copy-start.4
  165.8 29.8 %all-to-all-start.4 = ((f32[16,128,256]{2,1,0:T(8,128)}), f32[16,128,256]{2,1,0:T(8,128)}, u32[]{:S(2)}, u32[]{:S(2)}) async-start(f32[16,128,256]{2,1,0:T(8,128)} %copy-done.4), calls=%async_computation.4 | async-start | bytes 4194304 | tf_op jit(solution)/shard_map/all_to_all | solution.py:556
  170.2 1.6 copy-start.2
  173.2 4.2 %collective-permute-start.11 = (f32[256,256]{1,0:T(8,128)S(1)}, f32[256,256]{1,0:T(8,128)S(1)}, u32[]{:S(2)}, u32[]{:S(2)}) collective-permute-start(f32[256,256]{1,0:T(8,128)S(1)} %gram.1.refs_0_), channel_id=1, source_target_pairs={{0,16},{16,0},{32,48},{48,32},{64,80},{80,64},{96,112},{112,96},{1... | collective-permute-start | bytes 786440 | tf_op jit(solution)/shard_map/ppermute | solution.py:508
  176.4 15.2 %copy-start.3 = (f32[16,128,256]{2,1,0:T(8,128)S(1)}, f32[16,128,256]{2,1,0:T(8,128)}, u32[]{:S(2)}) copy-start(f32[16,128,256]{2,1,0:T(8,128)} %copy-done.1) | copy-start | bytes 6291460
  193.4 1.4 copy-start.9
  195.6 1.6 copy-start.10
  197.2 14.5 %copy-start.8 = (bf16[1,2048,1024]{2,1,0:T(8,128)(2,1)S(1)}, bf16[1,2048,1024]{2,1,0:T(8,128)(2,1)}, u32[]{:S(2)}) copy-start(bf16[1,2048,1024]{2,1,0:T(8,128)(2,1)} %param.8) | copy-start | bytes 12582916
  203.9 7.7 %collective-permute-start.13 = (f32[640,256]{1,0:T(8,128)S(1)}, f32[640,256]{1,0:T(8,128)S(1)}, u32[]{:S(2)}, u32[]{:S(2)}) collective-permute-start(f32[640,256]{1,0:T(8,128)S(1)} %get-tuple-element.21), channel_id=1, source_target_pairs={{0,16},{16,0},{32,48},{48,32},{64,80},{80,64},{96,112},{112,96},{1... | collective-permute-start | bytes 1966088 | tf_op jit(solution)/shard_map/ppermute | solution.py:508
  209.5 2.1 collective-permute-start.12

commit v5 on v3

--- a/solution.py
+++ b/solution.py
@@ -183,8 +183,11 @@
     )(x, after)
 
 
-def iterate_kernel(first_ref, factor_ref, iterate_ref):
-    iterate_ref[...] = dot_f32(first_ref[...], factor_ref[...])
+def iterate_kernel(first_ref, factor_ref, iterate_ref, local_ref, sem):
+    local_ref[...] = dot_f32(first_ref[...], factor_ref[...])
+    store = pltpu.make_async_copy(local_ref, iterate_ref, sem)
+    store.start()
+    store.wait()
 
 
 def iterate_of(first, factor):
@@ -192,7 +195,8 @@
         iterate_kernel,
         out_shape=jax.ShapeDtypeStruct(first.shape, jnp.float32),
         in_specs=[WHOLE, WHOLE],
-        out_specs=WHOLE,
+        out_specs=pl.BlockSpec(memory_space=pl.ANY),
+        scratch_shapes=[pltpu.VMEM(first.shape, jnp.float32), pltpu.SemaphoreType.DMA],
         compiler_params=pltpu.CompilerParams(vmem_limit_bytes=VMEM_BYTES),
         cost_estimate=pl.CostEstimate(
             flops=2_000_000_000, bytes_accessed=4_000_000, transcendentals=0
@@ -202,8 +206,11 @@
 
 
 def image_kernel(
-    place_ref, raw_ref, iterate_ref, factor_ref, image_ref, picks_ref, out_ref, even_ref, odd_ref
+    place_ref, raw_ref, iterate_ref, factor_ref, image_ref, picks_ref, out_ref, even_ref, odd_ref,
+    local_ref, sem,
 ):
+    load = pltpu.make_async_copy(iterate_ref, local_ref, sem)
+    load.start()
     width = even_ref.shape[0]
     even_ref[...] = jnp.zeros_like(even_ref)
     odd_ref[...] = jnp.zeros_like(odd_ref)
@@ -213,7 +220,8 @@
         source = pl.ds(pl.multiple_of(place_ref[k] * SB, SB), SB)
         picks_ref[k * SB : (k + 1) * SB, :] = image_ref[source, :]
     gram_step(image, even_ref, odd_ref)
-    iterate = iterate_ref[...]
+    load.wait()
+    iterate = local_ref[...]
     out_ref[width:, :] = jnp.zeros((out_ref.shape[0] - width, width), jnp.float32)
     out_ref[width : width + 1, :] = jnp.sum(iterate * image, axis=0, keepdims=True)
     out_ref[width + 1 : width + 2, :] = jnp.sum(iterate * iterate, axis=0, keepdims=True)
@@ -229,9 +237,15 @@
             jax.ShapeDtypeStruct(((1 + KB) * SB, width), jnp.float32),
             jax.ShapeDtypeStruct((width + 8, width), jnp.float32),
         ),
-        in_specs=[pl.BlockSpec(memory_space=pltpu.SMEM), WHOLE, WHOLE, WHOLE],
+        in_specs=[
+            pl.BlockSpec(memory_space=pltpu.SMEM),
+            WHOLE,
+            pl.BlockSpec(memory_space=pl.ANY),
+            WHOLE,
+        ],
         out_specs=(WHOLE, WHOLE, WHOLE),
-        scratch_shapes=[pltpu.VMEM((width, width), jnp.float32)] * 2,
+        scratch_shapes=[pltpu.VMEM((width, width), jnp.float32)] * 2
+        + [pltpu.VMEM((rows, width), jnp.float32), pltpu.SemaphoreType.DMA],
         compiler_params=pltpu.CompilerParams(vmem_limit_bytes=VMEM_BYTES),
         cost_estimate=pl.CostEstimate(
             flops=3_000_000_000, bytes_accessed=7_000_000, transcendentals=0

time: 234 us -> 234 us (level)
  no operation moved by 1% of the time
where the time goes in v5:
time: 234 us
  waiting for transfers between devices  68.3 us (29%)
  Pallas kernels  56.4 us (24%)
  starting transfers between devices  51.6 us (22%)
  blocking collectives  30.2 us (13%)
  local copies, waits for them, and re-layouts  17.4 us (7%)
  matrix products  6.6 us (3%)
    all_to_all x1, blocking collectives, gather_half(): whole = lax.all_to_all(spread, 'sep', 0, 0, tiled=True)  30.2 us
    all_to_all x1, waiting for transfers between devices, gather_blocks(): return lax.all_to_all(spread, axis, 0, 0, tiled=True)  24.6 us
    pallas_call x1, Pallas kernels, last_products(): pl.pallas_call(lambda *refs: last_kernel(scale, *refs), in_specs=[scalars...  21.3 us
    ppermute x6, starting transfers between devices, from_twin(): return lax.ppermute(x, 'sub', [(i, i ^ 1) for i in range(sub_count)])  17.1 us
    ppermute x8, waiting for transfers between devices, from_layer(): return lax.ppermute(x, 'sub', perm)  15.3 us
    pallas_call x1, Pallas kernels, inverse_transposed_factor(): pl.pallas_call(lambda *refs: factor_kernel(scale, *refs), out_shape=jax.S...  14.2 us
    all_to_all x1, waiting for transfers between devices, per_device(): lax.all_to_all(partial.reshape(sep_count, share, mode_total), 'sep', 0, 0...  13.3 us
    unnamed x49, local copies, waits for them, and re-layouts  12.5 us
  transfers between devices with their start and end apart: 18, of which 12 were waited for; matrix products, arithmetic and copies ran while one was open for 2% of the time, Pallas kernels for 7%

profile of v5, /device:TPU:1, one launch (start us, length us, event | category | flops | bytes accessed | tf_op | source)
XLA Modules:
  0.0 233.5 jit_solution(1489924055589946355)
XLA Ops:
  0.6 1.6 copy-done
  2.2 5.5 %fusion.2 = bf16[512,1024]{1,0:T(8,128)(2,1)} fusion(bf16[1,2048,512]{2,1,0:T(8,128)(2,1)S(1)} %copy-done, bf16[1,2048,1024]{2,1,0:T(8,128)(2,1)} %param.8), kind=kOutput, calls=%fused_computation.3 | convolution fusion | flops 2148007936 | bytes 7340032 | tf_op jit(solution)/shard_map/dot_general | solution.py:524
  7.7 7.7 %all-to-all-start = ((bf16[16,32,1024]{2,1,0:T(8,128)(2,1)}), bf16[16,32,1024]{2,1,0:T(8,128)(2,1)S(1)}, u32[]{:S(2)}, u32[]{:S(2)}) async-start(bf16[16,32,1024]{2,1,0:T(8,128)(2,1)} %bitcast.41), calls=%async_computation | async-start | bytes 2097152 | tf_op jit(solution)/shard_map/all_to_all | solution.py:528
  16.7 0.9 dynamic-slice_convert_fusion
  17.7 13.3 %all-to-all-done = bf16[16,32,1024]{2,1,0:T(8,128)(2,1)S(1)} async-done(((bf16[16,32,1024]{2,1,0:T(8,128)(2,1)}), bf16[16,32,1024]{2,1,0:T(8,128)(2,1)S(1)}, u32[]{:S(2)}, u32[]{:S(2)}) %all-to-all-start) | async-done | bytes 1048608 | tf_op jit(solution)/shard_map/all_to_all | solution.py:528
  31.2 1.6 broadcast_in_dim.45
  32.8 4.6 %all-to-all-start.1 = ((bf16[16,64,1024]{2,1,0:T(8,128)(2,1)}), bf16[16,64,1024]{2,1,0:T(8,128)(2,1)}, u32[]{:S(2)}, u32[]{:S(2)}) async-start(bf16[16,64,1024]{2,1,0:T(8,128)(2,1)} %broadcast_in_dim.45), calls=%async_computation.1 | async-start | bytes 4194304 | tf_op jit(solution)/shard_map/all_to_all | solution.py:501
  38.1 24.6 %all-to-all-done.1.gathered_ref.refs_7_ = bf16[16,64,1024]{2,1,0:T(8,128)(2,1)} async-done(((bf16[16,64,1024]{2,1,0:T(8,128)(2,1)}), bf16[16,64,1024]{2,1,0:T(8,128)(2,1)}, u32[]{:S(2)}, u32[]{:S(2)}) %all-to-all-start.1) | async-done | bytes 2097184 | tf_op jit(solution)/shard_map/all_to_all | solution.py:501
  62.7 3.8 %rows.1 = (bf16[16,16,640]{2,1,0:T(8,128)(2,1)S(1)}, bf16[16,128,256]{2,1,0:T(8,128)(2,1)S(1)}) custom-call(s32[4]{0:T(128)S(1)} %bitcast.37, s32[1]{0:T(128)} %bitcast.2.first_ref, f32[1,1024]{1,0:T(1,128)S(1)} %compare_select_fusion.weight_ref.refs_6_, bf16[16,64,1024]{2,1,0:T(8,128)(2,1)} %all-to-all-done.1.gathered_ref.refs_7_), custom_call_target="tpu_custom_call" | custom-call | flops 800000000 | bytes 2700000 | tf_op jit(solution)/shard_map/rows/pallas_call | solution.py:334
  67.2 5.7 %collective-permute-start = (bf16[2048,256]{1,0:T(8,128)(2,1)S(1)}, bf16[2048,256]{1,0:T(8,128)(2,1)}, u32[]{:S(2)}, u32[]{:S(2)}) collective-permute-start(bf16[2048,256]{1,0:T(8,128)(2,1)S(1)} %bitcast.35), channel_id=1, source_target_pairs={{0,16},{16,0},{32,48},{48,32},{64,80},{80,64},{96,112},{112,96},{1... | collective-permute-start | bytes 3145736 | tf_op jit(solution)/shard_map/ppermute | solution.py:521
  72.9 8.6 %all-to-all-start.2 = ((bf16[16,16,640]{2,1,0:T(8,128)(2,1)}), bf16[16,16,640]{2,1,0:T(8,128)(2,1)S(1)}, u32[]{:S(2)}, u32[]{:S(2)}) async-start(bf16[16,16,640]{2,1,0:T(8,128)(2,1)} %copy-done.6), calls=%async_computation.2 | async-start | bytes 655360 | tf_op jit(solution)/shard_map/all_to_all | solution.py:549
  81.5 1.7 constant_dynamic-slice_fusion.flex_ref
  83.2 11.4 %all-to-all-done.2.incoming_ref = bf16[16,16,640]{2,1,0:T(8,128)(2,1)S(1)} async-done(((bf16[16,16,640]{2,1,0:T(8,128)(2,1)}), bf16[16,16,640]{2,1,0:T(8,128)(2,1)S(1)}, u32[]{:S(2)}, u32[]{:S(2)}) %all-to-all-start.2) | async-done | bytes 327712 | tf_op jit(solution)/shard_map/all_to_all | solution.py:549
  94.7 0.9 copy-done.5
  95.7 2.0 build.1
  97.7 1.0 collective-permute-start.2
  98.7 0.8 collective-permute-start.1
  99.5 5.0 %collective-permute-done.2 = f32[16,256]{1,0:T(8,128)S(1)} collective-permute-done((f32[16,256]{1,0:T(8,128)S(1)}, f32[16,256]{1,0:T(8,128)S(1)}, u32[]{:S(2)}, u32[]{:S(2)}) %collective-permute-start.2) | collective-permute-done | bytes 16416 | tf_op jit(solution)/shard_map/ppermute | solution.py:561
  104.5 0.7 collective-permute-start.5
  105.2 2.9 %collective-permute-start.3 = (f32[2,16,256]{2,1,0:T(8,128)S(1)}, f32[2,16,256]{2,1,0:T(8,128)S(1)}, u32[]{:S(2)}, u32[]{:S(2)}) collective-permute-start(f32[2,16,256]{2,1,0:T(8,128)S(1)} %pad_maximum_fusion.own_ref), channel_id=1, source_target_pairs={{0,32},{16,48},{32,0},{48,16},{64,96},{80,112},{96,64},{112,80},{1... | collective-permute-start | bytes 98312 | tf_op jit(solution)/shard_map/ppermute | solution.py:561
  108.1 1.1 collective-permute-done.5.three_ref
  110.4 2.3 spread.2
  112.8 30.2 %all_to_all.25 = f32[16,128,256]{2,1,0:T(8,128)S(1)} all-to-all(f32[16,128,256]{2,1,0:T(8,128)} %spread.2), channel_id=1, replica_groups=mesh['sub'=16,'sep'=16] {'sep'}, dimensions={0} | all-to-all | bytes 4194304 | tf_op jit(solution)/shard_map/all_to_all | solution.py:569
  143.0 1.1 fusion.8
  144.1 1.3 copy-done.1
  145.4 3.0 %collective-permute-start.6 = (f32[16,256]{1,0:T(8,128)S(1)}, f32[16,256]{1,0:T(8,128)S(1)}, u32[]{:S(2)}, u32[]{:S(2)}) collective-permute-start(f32[16,256]{1,0:T(8,128)S(1)} %slice.34), channel_id=1, source_target_pairs={{0,16},{16,0},{32,48},{48,32},{64,80},{80,64},{96,112},{112,96},{1... | collective-permute-start | bytes 49160 | tf_op jit(solution)/shard_map/ppermute | solution.py:521
  148.4 0.8 collective-permute-done.6
  149.3 0.9 collective-permute-start.7
  150.1 5.6 %collective-permute-done.7 = f32[16,256]{1,0:T(8,128)S(1)} collective-permute-done((f32[16,256]{1,0:T(8,128)S(1)}, f32[16,256]{1,0:T(8,128)S(1)}, u32[]{:S(2)}, u32[]{:S(2)}) %collective-permute-start.7) | collective-permute-done | bytes 16416 | tf_op jit(solution)/shard_map/ppermute | solution.py:561
  155.8 2.3 collective-permute-start.10
  158.5 0.9 collective-permute-start.8
  159.4 1.0 collective-permute-done.10.three_ref
  160.5 1.9 collective-permute-done.9.two_ref
  163.6 2.3 spread.3.after_ref
  165.9 4.4 %all-to-all-start.4 = ((f32[16,128,256]{2,1,0:T(8,128)}), f32[16,128,256]{2,1,0:T(8,128)}, u32[]{:S(2)}, u32[]{:S(2)}) async-start(f32[16,128,256]{2,1,0:T(8,128)} %spread.3.after_ref), calls=%async_computation.4 | async-start | bytes 4194304 | tf_op jit(solution)/shard_map/all_to_all | solution.py:569
  170.4 1.6 copy-done.2
  172.0 1.6 copy-done.4
  173.6 1.3 gram.1.refs_0_
  174.9 2.4 %collective-permute-start.11 = (f32[256,256]{1,0:T(8,128)S(1)}, f32[256,256]{1,0:T(8,128)S(1)}, u32[]{:S(2)}, u32[]{:S(2)}) collective-permute-start(f32[256,256]{1,0:T(8,128)S(1)} %gram.1.refs_0_), channel_id=1, source_target_pairs={{0,16},{16,0},{32,48},{48,32},{64,80},{80,64},{96,112},{112,96},{1... | collective-permute-start | bytes 786440 | tf_op jit(solution)/shard_map/ppermute | solution.py:521
  177.5 1.0 collective-permute-done.11.refs_1_
  178.5 14.2 %factor.1.factor_ref = f32[256,256]{1,0:T(8,128)S(1)} custom-call(f32[256,256]{1,0:T(8,128)S(1)} %gram.1.refs_0_, f32[256,256]{1,0:T(8,128)S(1)} %collective-permute-done.11.refs_1_), custom_call_target="tpu_custom_call" | custom-call | flops 12000000000 | bytes 800000 | tf_op jit(solution)/shard_map/factor/pallas_call | solution.py:132
  192.7 2.0 iterate.1.iterate_ref
  194.7 1.3 copy-done.9
  196.0 1.6 copy-done.10
  197.6 7.1 %image.1 = (f32[2048,256]{1,0:T(8,128)S(1)}, f32[640,256]{1,0:T(8,128)S(1)}, f32[264,256]{1,0:T(8,128)S(1)}) custom-call(s32[5]{0:T(128)S(1)} %pad_add_fusion.1.place_ref, f32[2048,256]{1,0:T(8,128)} %bitcast.16.raw_ref, f32[2048,256]{1,0:T(8,128)S(1)} %copy-done.10, f32[256,256]{1,0:T(8,128)S(1)} %factor.1.factor_ref), custom_call_target="tpu_custom_call" | custom-call | flops 3000000000 | bytes 7000000 | tf_op jit(solution)/shard_map/image/pallas_call | solution.py:233
  204.7 5.2 %collective-permute-start.13 = (f32[640,256]{1,0:T(8,128)S(1)}, f32[640,256]{1,0:T(8,128)S(1)}, u32[]{:S(2)}, u32[]{:S(2)}) collective-permute-start(f32[640,256]{1,0:T(8,128)S(1)} %get-tuple-element.21), channel_id=1, source_target_pairs={{0,16},{16,0},{32,48},{48,32},{64,80},{80,64},{96,112},{112,96},{1... | collective-permute-start | bytes 1966088 | tf_op jit(solution)/shard_map/ppermute | solution.py:521
  210.1 1.9 collective-permute-done.12.refs_3_
  212.0 21.3 %last.1 = (f32[256,256]{1,0:T(8,128)}, f32[1,256]{1,0:T(1,128)}, bf16[2048,256]{1,0:T(8,128)(2,1)}) custom-call(s32[6]{0:T(128)S(1)} %broadcast_shift-right-arithmetic_fusion.refs_0_, s32[6]{0:T(128)S(1)} %compare_convert_fusion.refs_1_, f32[264,256]{1,0:T(8,128)S(1)} %get-tuple-element.19.refs_2_, f32[264,256]{1,0:T(8,128)S(1)} %collective-permute-done.12.refs_3_, ...), custom_call_target="tpu_custom_call" | custom-call | flops 16000000000 | bytes 8000000 | tf_op jit(solution)/shard_map/last/pallas_call | solution.py:468
  (73 shorter events, 5.7 us)
Async XLA Ops:
  0.6 1.6 copy-start
  7.7 7.8 %copy-start.23 = (s32[1,4]{1,0:T(1,128)S(1)}, s32[1,4]{1,0:T(1,128)}, u32[]{:S(2)}) copy-start(s32[1,4]{1,0:T(1,128)} %param.13) | copy-start | bytes 52
  7.7 23.2 %all-to-all-start = ((bf16[16,32,1024]{2,1,0:T(8,128)(2,1)}), bf16[16,32,1024]{2,1,0:T(8,128)(2,1)S(1)}, u32[]{:S(2)}, u32[]{:S(2)}) async-start(bf16[16,32,1024]{2,1,0:T(8,128)(2,1)} %bitcast.41), calls=%async_computation | async-start | bytes 2097152 | tf_op jit(solution)/shard_map/all_to_all | solution.py:528
  32.8 5.2 %copy-start.22 = (f32[1,1024]{1,0:T(1,128)S(1)}, f32[1,1024]{1,0:T(1,128)}, u32[]{:S(2)}) copy-start(f32[1,1024]{1,0:T(1,128)} %param.10) | copy-start | bytes 12292
  32.8 29.8 %copy-start.7 = (s32[1,4]{1,0:T(1,128)S(1)}, s32[1,4]{1,0:T(1,128)}, u32[]{:S(2)}) copy-start(s32[1,4]{1,0:T(1,128)} %param.12) | copy-start | bytes 52
  32.8 29.8 %all-to-all-start.1 = ((bf16[16,64,1024]{2,1,0:T(8,128)(2,1)}), bf16[16,64,1024]{2,1,0:T(8,128)(2,1)}, u32[]{:S(2)}, u32[]{:S(2)}) async-start(bf16[16,64,1024]{2,1,0:T(8,128)(2,1)} %broadcast_in_dim.45), calls=%async_computation.1 | async-start | bytes 4194304 | tf_op jit(solution)/shard_map/all_to_all | solution.py:501
  66.5 0.7 copy-start.6
  67.2 27.5 %collective-permute-start = (bf16[2048,256]{1,0:T(8,128)(2,1)S(1)}, bf16[2048,256]{1,0:T(8,128)(2,1)}, u32[]{:S(2)}, u32[]{:S(2)}) collective-permute-start(bf16[2048,256]{1,0:T(8,128)(2,1)S(1)} %bitcast.35), channel_id=1, source_target_pairs={{0,16},{16,0},{32,48},{48,32},{64,80},{80,64},{96,112},{112,96},{1... | collective-permute-start | bytes 3145736 | tf_op jit(solution)/shard_map/ppermute | solution.py:521
  72.9 21.7 %all-to-all-start.2 = ((bf16[16,16,640]{2,1,0:T(8,128)(2,1)}), bf16[16,16,640]{2,1,0:T(8,128)(2,1)S(1)}, u32[]{:S(2)}, u32[]{:S(2)}) async-start(bf16[16,16,640]{2,1,0:T(8,128)(2,1)} %copy-done.6), calls=%async_computation.2 | async-start | bytes 655360 | tf_op jit(solution)/shard_map/all_to_all | solution.py:549
  94.7 1.0 copy-start.5
  97.7 6.8 %collective-permute-start.2 = (f32[16,256]{1,0:T(8,128)S(1)}, f32[16,256]{1,0:T(8,128)S(1)}, u32[]{:S(2)}, u32[]{:S(2)}) collective-permute-start(f32[16,256]{1,0:T(8,128)S(1)} %get-tuple-element.18), channel_id=1, source_target_pairs={{0,128},{16,144},{32,160},{48,176},{64,192},{80,208},{96,224},{112... | collective-permute-start | bytes 49160 | tf_op jit(solution)/shard_map/ppermute | solution.py:561
  98.7 9.4 %collective-permute-start.1 = (f32[16,2048]{1,0:T(8,128)S(1)}, f32[16,2048]{1,0:T(8,128)S(1)}, u32[]{:S(2)}, u32[]{:S(2)}) collective-permute-start(f32[16,2048]{1,0:T(8,128)S(1)} %get-tuple-element.17), channel_id=1, source_target_pairs={{0,16},{16,0},{32,48},{48,32},{64,80},{80,64},{96,112},{112,96},{1... | collective-permute-start | bytes 393224 | tf_op jit(solution)/shard_map/ppermute | solution.py:521
  104.5 5.4 %copy-start.14 = (f32[2,16,256]{2,1,0:T(8,128)}, f32[2,16,256]{2,1,0:T(8,128)S(1)}, u32[]{:S(2)}) copy-start(f32[2,16,256]{2,1,0:T(8,128)S(1)} %pad_maximum_fusion.own_ref) | copy-start | bytes 98308
  104.5 4.7 %collective-permute-start.5 = (f32[2,16,256]{2,1,0:T(8,128)S(1)}, f32[2,16,256]{2,1,0:T(8,128)S(1)}, u32[]{:S(2)}, u32[]{:S(2)}) collective-permute-start(f32[2,16,256]{2,1,0:T(8,128)S(1)} %pad_maximum_fusion.own_ref), channel_id=1, source_target_pairs={{0,96},{16,112},{32,64},{48,80},{64,32},{80,48},{96,0},{112,16},{1... | collective-permute-start | bytes 98312 | tf_op jit(solution)/shard_map/ppermute | solution.py:561
  105.2 4.0 %collective-permute-start.4 = (f32[2,16,256]{2,1,0:T(8,128)S(1)}, f32[2,16,256]{2,1,0:T(8,128)S(1)}, u32[]{:S(2)}, u32[]{:S(2)}) collective-permute-start(f32[2,16,256]{2,1,0:T(8,128)S(1)} %pad_maximum_fusion.own_ref), channel_id=1, source_target_pairs={{0,64},{16,80},{32,96},{48,112},{64,0},{80,16},{96,32},{112,48},{1... | collective-permute-start | bytes 98312 | tf_op jit(solution)/shard_map/ppermute | solution.py:561
  105.2 4.7 %collective-permute-start.3 = (f32[2,16,256]{2,1,0:T(8,128)S(1)}, f32[2,16,256]{2,1,0:T(8,128)S(1)}, u32[]{:S(2)}, u32[]{:S(2)}) collective-permute-start(f32[2,16,256]{2,1,0:T(8,128)S(1)} %pad_maximum_fusion.own_ref), channel_id=1, source_target_pairs={{0,32},{16,48},{32,0},{48,16},{64,96},{80,112},{96,64},{112,80},{1... | collective-permute-start | bytes 98312 | tf_op jit(solution)/shard_map/ppermute | solution.py:561
  108.1 1.7 copy-start.11
  109.2 0.6 copy-start.16
  109.2 0.6 copy-start.17
  109.8 0.6 copy-start.19
  112.8 30.2 %copy-start.12 = (f32[32,2048]{1,0:T(8,128)S(1)}, f32[32,2048]{1,0:T(8,128)}, u32[]{:S(2)}) copy-start(f32[32,2048]{1,0:T(8,128)} %copy-done.11) | copy-start | bytes 786436
  144.1 1.3 copy-start.1
  145.4 3.9 %collective-permute-start.6 = (f32[16,256]{1,0:T(8,128)S(1)}, f32[16,256]{1,0:T(8,128)S(1)}, u32[]{:S(2)}, u32[]{:S(2)}) collective-permute-start(f32[16,256]{1,0:T(8,128)S(1)} %slice.34), channel_id=1, source_target_pairs={{0,16},{16,0},{32,48},{48,32},{64,80},{80,64},{96,112},{112,96},{1... | collective-permute-start | bytes 49160 | tf_op jit(solution)/shard_map/ppermute | solution.py:521
  149.3 13.1 %copy-start.13 = (f32[16,256]{1,0:T(8,128)}, f32[16,256]{1,0:T(8,128)S(1)}, u32[]{:S(2)}) copy-start(f32[16,256]{1,0:T(8,128)S(1)} %slice_add_fusion.after_ref) | copy-start | bytes 49156
  149.3 6.5 %collective-permute-start.7 = (f32[16,256]{1,0:T(8,128)S(1)}, f32[16,256]{1,0:T(8,128)S(1)}, u32[]{:S(2)}, u32[]{:S(2)}) collective-permute-start(f32[16,256]{1,0:T(8,128)S(1)} %slice_add_fusion.after_ref), channel_id=1, source_target_pairs={{0,128},{16,144},{32,160},{48,176},{64,192},{80,208},{96,224},{112... | collective-permute-start | bytes 49160 | tf_op jit(solution)/shard_map/ppermute | solution.py:561
  155.8 6.6 %copy-start.15 = (f32[2,16,256]{2,1,0:T(8,128)}, f32[2,16,256]{2,1,0:T(8,128)S(1)}, u32[]{:S(2)}) copy-start(f32[2,16,256]{2,1,0:T(8,128)S(1)} %pad_maximum_fusion.1.own_ref) | copy-start | bytes 98308
  155.8 4.7 %collective-permute-start.10 = (f32[2,16,256]{2,1,0:T(8,128)S(1)}, f32[2,16,256]{2,1,0:T(8,128)S(1)}, u32[]{:S(2)}, u32[]{:S(2)}) collective-permute-start(f32[2,16,256]{2,1,0:T(8,128)S(1)} %pad_maximum_fusion.1.own_ref), channel_id=1, source_target_pairs={{0,96},{16,112},{32,64},{48,80},{64,32},{80,48},{96,0},{112,16},{1... | collective-permute-start | bytes 98312 | tf_op jit(solution)/shard_map/ppermute | solution.py:561
  158.1 4.3 %collective-permute-start.9 = (f32[2,16,256]{2,1,0:T(8,128)S(1)}, f32[2,16,256]{2,1,0:T(8,128)S(1)}, u32[]{:S(2)}, u32[]{:S(2)}) collective-permute-start(f32[2,16,256]{2,1,0:T(8,128)S(1)} %pad_maximum_fusion.1.own_ref), channel_id=1, source_target_pairs={{0,64},{16,80},{32,96},{48,112},{64,0},{80,16},{96,32},{112,48},{1... | collective-permute-start | bytes 98312 | tf_op jit(solution)/shard_map/ppermute | solution.py:561
  158.5 3.9 %collective-permute-start.8 = (f32[2,16,256]{2,1,0:T(8,128)S(1)}, f32[2,16,256]{2,1,0:T(8,128)S(1)}, u32[]{:S(2)}, u32[]{:S(2)}) collective-permute-start(f32[2,16,256]{2,1,0:T(8,128)S(1)} %pad_maximum_fusion.1.own_ref), channel_id=1, source_target_pairs={{0,32},{16,48},{32,0},{48,16},{64,96},{80,112},{96,64},{112,80},{1... | collective-permute-start | bytes 98312 | tf_op jit(solution)/shard_map/ppermute | solution.py:561
  160.5 2.0 copy-start.18
  162.4 0.6 copy-start.20
  163.0 0.6 copy-start.21
  165.9 30.1 %all-to-all-start.4 = ((f32[16,128,256]{2,1,0:T(8,128)}), f32[16,128,256]{2,1,0:T(8,128)}, u32[]{:S(2)}, u32[]{:S(2)}) async-start(f32[16,128,256]{2,1,0:T(8,128)} %spread.3.after_ref), calls=%async_computation.4 | async-start | bytes 4194304 | tf_op jit(solution)/shard_map/all_to_all | solution.py:569
  170.4 1.6 copy-start.2
  172.0 1.6 copy-start.4
  174.9 3.6 %collective-permute-start.11 = (f32[256,256]{1,0:T(8,128)S(1)}, f32[256,256]{1,0:T(8,128)S(1)}, u32[]{:S(2)}, u32[]{:S(2)}) collective-permute-start(f32[256,256]{1,0:T(8,128)S(1)} %gram.1.refs_0_), channel_id=1, source_target_pairs={{0,16},{16,0},{32,48},{48,32},{64,80},{80,64},{96,112},{112,96},{1... | collective-permute-start | bytes 786440 | tf_op jit(solution)/shard_map/ppermute | solution.py:521
  177.5 15.2 %copy-start.3 = (f32[16,128,256]{2,1,0:T(8,128)S(1)}, f32[16,128,256]{2,1,0:T(8,128)}, u32[]{:S(2)}) copy-start(f32[16,128,256]{2,1,0:T(8,128)} %copy-done.1) | copy-start | bytes 6291460
  194.6 1.3 copy-start.9
  196.0 1.6 copy-start.10
  197.6 14.4 %copy-start.8 = (bf16[1,2048,1024]{2,1,0:T(8,128)(2,1)S(1)}, bf16[1,2048,1024]{2,1,0:T(8,128)(2,1)}, u32[]{:S(2)}) copy-start(bf16[1,2048,1024]{2,1,0:T(8,128)(2,1)} %param.8) | copy-start | bytes 12582916
  204.7 7.3 %collective-permute-start.13 = (f32[640,256]{1,0:T(8,128)S(1)}, f32[640,256]{1,0:T(8,128)S(1)}, u32[]{:S(2)}, u32[]{:S(2)}) collective-permute-start(f32[640,256]{1,0:T(8,128)S(1)} %get-tuple-element.21), channel_id=1, source_target_pairs={{0,16},{16,0},{32,48},{48,32},{64,80},{80,64},{96,112},{112,96},{1... | collective-permute-start | bytes 1966088 | tf_op jit(solution)/shard_map/ppermute | solution.py:521
  209.9 2.1 collective-permute-start.12
